TPU v7x, 32 devices: a whole 2x2x4 slice. The times are simulated.
32 devices in a mesh: batch: 4 (over y, x), tensor: 8 (over z, core).
Axes of the slice: x: 2, y: 2, z: 4, core: 2. Of those that a mesh axis runs over, the one named last changes fastest.
Arguments:
- hidden: bfloat16 [4096, 2048], P('batch', 'tensor'), may hold values from -6 to 6
- w_query: bfloat16 [2048, 2048], P(None, 'tensor'), may hold values from -0.125 to 0.125
- w_key: bfloat16 [2048, 2048], P(None, 'tensor'), may hold values from -0.125 to 0.125
- w_value: bfloat16 [2048, 4096], P(None, 'tensor'), may hold values from -0.125 to 0.125
- conv_query: float32 [4, 2048], P(None, 'tensor'), may hold values from -0.6 to 0.6
- conv_key: float32 [4, 2048], P(None, 'tensor'), may hold values from -0.6 to 0.6
- conv_value: float32 [4, 4096], P(None, 'tensor'), may hold values from -0.6 to 0.6
- decay_log: float32 [4096, 32], P('batch', 'tensor'), may hold values from -1 to 0, as said below
- beta_gate: float32 [4096, 32], P('batch', 'tensor'), may hold values from 0.1 to 0.95
- init_state: float32 [32, 32, 128, 128], P('batch', 'tensor'), may hold values from -4 to 4
- grad_out: bfloat16 [4096, 4096], P('batch', 'tensor'), may hold values from -6 to 6
- state_grad_in: float32 [32, 32, 128, 128], P('batch', 'tensor'), may hold values from -4 to 4
- rollout_lengths: int32 [32], P('batch'), may hold values from 1 to 128, 2560 in all
- slot_map: int32 [32], P('batch'), may hold values from 0 to 31, as said below
Outputs:
- grad_hidden: bfloat16 [4096, 2048], P('batch', 'tensor')
- grad_w_query: float32 [2048, 2048], P('batch', 'tensor')
- grad_w_key: float32 [2048, 2048], P('batch', 'tensor')
- grad_w_value: float32 [2048, 4096], P('batch', 'tensor')
- grad_conv_query: float32 [4, 2048], P(None, 'tensor')
- grad_conv_key: float32 [4, 2048], P(None, 'tensor')
- grad_conv_value: float32 [4, 4096], P(None, 'tensor')
- grad_decay: float32 [4096, 32], P('batch', 'tensor')
- grad_beta: float32 [4096, 32], P('batch', 'tensor')
- slot_state_grad: float32 [32, 32, 128, 128], P('batch', 'tensor')
Inputs may be any that keep to these rules, and one draw needn't show every extreme that they name: `decay_log`: Non-positive. `slot_map`: each slot is named once; slot s is held by batch index s // 8; the 8 requests of one batch index go to 4 different slot holders, exactly 2 to each.
All inputs are finite; a program needn't handle non-finite values. No bound on the sum of `rollout_lengths` on one device may be relied on, other than what follows from the above.
Results may differ from a plain program's by a relative error of at most 0.014.
Values may be sent and summed in bfloat16 or wider, within the bound.
No kernel may reach another device: no remote copies, remote signals or barrier semaphores. Data moves between devices by JAX's collectives and lax.ppermute only.
A program may use at most 128 MiB of HBM per device.

v0:
```python
import jax
import jax.numpy as jnp
from jax import lax
from jax.sharding import PartitionSpec as P

R_DEV = 8


EPSILON = 1e-06


def short_conv(projected, weights):
    kernel_taps = weights.shape[0]
    length = projected.shape[1]
    padded = jnp.pad(projected, ((0, 0), (kernel_taps - 1, 0), (0, 0)))
    mixed_sum = jnp.zeros_like(projected)
    for offset in range(kernel_taps):
        mixed_sum = mixed_sum + padded[:, offset : offset + length, :] * weights[offset]
    return mixed_sum


def unit_rows(heads_in, factor):
    return heads_in * (
        factor * lax.rsqrt(jnp.sum(heads_in * heads_in, axis=-1, keepdims=True) + EPSILON)
    )


def block_step(carry_state, blocks_in):
    queries, key_rows, values, gate_logs, write_rates = blocks_in
    precise = lax.Precision.HIGHEST
    block_len = gate_logs.shape[-1]
    cumulative = jnp.cumsum(gate_logs, axis=-1)
    row_index = lax.broadcasted_iota(jnp.int32, (block_len, block_len), 0)
    col_index = lax.broadcasted_iota(jnp.int32, (block_len, block_len), 1)
    strict = row_index > col_index
    causal = row_index >= col_index
    spread = cumulative[..., :, None] - cumulative[..., None, :]
    within = jnp.where(causal, jnp.exp(jnp.where(causal, spread, 0.0)), 0.0)
    intersections = jnp.einsum("rhik,rhjk->rhij", key_rows, key_rows, precision=precise)
    coupling = jnp.where(strict, write_rates[..., :, None] * intersections * within, 0.0)
    system = coupling + jnp.eye(block_len, dtype=jnp.float32)
    growth = jnp.exp(cumulative)
    weighted = (write_rates * growth)[..., None] * key_rows
    scaled = write_rates[..., None] * values
    solved_w = jax.scipy.linalg.solve_triangular(system, weighted, lower=True, unit_diagonal=True)
    solved_u = jax.scipy.linalg.solve_triangular(system, scaled, lower=True, unit_diagonal=True)
    new_values = solved_u - jnp.einsum("rhck,rhkv->rhcv", solved_w, carry_state, precision=precise)
    scores = jnp.einsum("rhik,rhjk->rhij", queries, key_rows, precision=precise) * within
    outputs = growth[..., None] * jnp.einsum(
        "rhck,rhkv->rhcv", queries, carry_state, precision=precise
    )
    outputs = outputs + jnp.einsum("rhij,rhjv->rhiv", scores, new_values, precision=precise)
    final_gate = cumulative[..., -1:]
    carried = jnp.exp(final_gate - cumulative)[..., None] * key_rows
    new_state = jnp.exp(final_gate)[..., None] * carry_state
    new_state = new_state + jnp.einsum("rhck,rhcv->rhkv", carried, new_values, precision=precise)
    return (new_state, outputs)


def core(
    proj_query,
    proj_key,
    proj_value,
    conv_query,
    conv_key,
    conv_value,
    decay_log,
    beta_gate,
    init_state,
    live_rows,
):
    requests = init_state.shape[0]
    length = proj_query.shape[0] // requests
    head_count = init_state.shape[1]
    key_size = init_state.shape[2]
    value_size = init_state.shape[3]
    key_heads = proj_query.shape[1] // key_size
    group_size = head_count // key_heads
    block_len = min(length, 128)
    block_count = length // block_len

    def prepare(projected, weights):
        return jax.nn.silu(
            short_conv(projected.astype(jnp.float32).reshape(requests, length, -1), weights)
        )

    queries = unit_rows(
        prepare(proj_query, conv_query).reshape(requests, length, key_heads, key_size),
        key_size ** (-0.5),
    )
    key_rows = unit_rows(
        prepare(proj_key, conv_key).reshape(requests, length, key_heads, key_size), 1.0
    )
    values = prepare(proj_value, conv_value).reshape(requests, length, head_count, value_size)
    queries = jnp.repeat(queries, group_size, axis=2)
    key_rows = jnp.repeat(key_rows, group_size, axis=2)
    live_mask = live_rows.reshape(requests, length, 1)
    gate_logs = decay_log.reshape(requests, length, head_count) * live_mask
    write_rates = beta_gate.reshape(requests, length, head_count) * live_mask

    def to_blocks(array_in):
        dims_in = array_in.shape
        reshaped = array_in.reshape((requests, block_count, block_len) + dims_in[2:])
        return jnp.moveaxis(jnp.moveaxis(reshaped, 1, 0), 3, 2)

    final_state, outputs = lax.scan(
        block_step,
        init_state,
        (
            to_blocks(queries),
            to_blocks(key_rows),
            to_blocks(values),
            to_blocks(gate_logs),
            to_blocks(write_rates),
        ),
    )
    outputs = jnp.moveaxis(jnp.moveaxis(outputs, 0, 1), 2, 3)
    outputs = outputs.reshape(requests * length, head_count * value_size) * live_rows[:, None]
    return (outputs, final_state)


def core_grads(
    proj_query,
    proj_key,
    proj_value,
    conv_query,
    conv_key,
    conv_value,
    decay_log,
    beta_gate,
    init_state,
    live_rows,
    grad_out,
    state_grad_in,
):

    def forward(p_query, p_key, p_value, c_query, c_key, c_value, d_log, b_gate, s_init):
        return core(
            p_query, p_key, p_value, c_query, c_key, c_value, d_log, b_gate, s_init, live_rows
        )

    primal, pullback = jax.vjp(
        forward,
        proj_query,
        proj_key,
        proj_value,
        conv_query,
        conv_key,
        conv_value,
        decay_log,
        beta_gate,
        init_state,
    )
    return pullback((grad_out.astype(jnp.float32), state_grad_in))


def body(
    hidden,
    w_query,
    w_key,
    w_value,
    conv_query,
    conv_key,
    conv_value,
    decay_log,
    beta_gate,
    init_state,
    grad_out,
    state_grad_in,
    rollout_lengths,
    slot_map,
):
    features_all = lax.all_gather(hidden, "tensor", axis=1, tiled=True)
    all_slots = lax.all_gather(slot_map, "batch", axis=0, tiled=True)
    proj_query = jnp.dot(features_all, w_query, preferred_element_type=jnp.float32).astype(
        jnp.bfloat16
    )
    proj_key = jnp.dot(features_all, w_key, preferred_element_type=jnp.float32).astype(jnp.bfloat16)
    proj_value = jnp.dot(features_all, w_value, preferred_element_type=jnp.float32).astype(
        jnp.bfloat16
    )
    requests = rollout_lengths.shape[0]
    length = hidden.shape[0] // requests
    position = jnp.arange(length, dtype=jnp.int32)
    live_rows = (position[None, :] < rollout_lengths[:, None]).astype(jnp.float32).reshape(-1)
    local_grads = core_grads(
        proj_query,
        proj_key,
        proj_value,
        conv_query,
        conv_key,
        conv_value,
        decay_log,
        beta_gate,
        init_state,
        live_rows,
        grad_out,
        state_grad_in,
    )
    d_query, d_key, d_value = (local_grads[0], local_grads[1], local_grads[2])
    grad_decay, grad_beta, grad_init = (local_grads[6], local_grads[7], local_grads[8])
    grad_conv_query, grad_conv_key, grad_conv_value = lax.psum(
        (local_grads[3], local_grads[4], local_grads[5]), "batch"
    )
    combined = jnp.concatenate([d_query, d_key, d_value], axis=1)
    width_all = features_all.shape[1]
    weight_grads = lax.psum_scatter(
        lax.dot_general(
            features_all, combined, (((0,), (0,)), ((), ())), preferred_element_type=jnp.float32
        ).astype(jnp.bfloat16),
        "batch",
        scatter_dimension=0,
        tiled=True,
    ).astype(jnp.float32)
    query_cols = w_query.shape[1]
    key_cols = w_key.shape[1]
    grad_w_query = weight_grads[:, :query_cols]
    grad_w_key = weight_grads[:, query_cols : query_cols + key_cols]
    grad_w_value = weight_grads[:, query_cols + key_cols :]
    contract = (((1,), (1,)), ((), ()))
    term_sum = jnp.zeros(
        (lax.axis_size("tensor") * (width_all // lax.axis_size("tensor")), features_all.shape[0]),
        jnp.float32,
    )
    for matrix, grad_rows in ((w_query, d_query), (w_key, d_key), (w_value, d_value)):
        term_sum = term_sum + lax.dot_general(
            matrix, grad_rows, contract, preferred_element_type=jnp.float32
        )
    feature_part = lax.psum_scatter(
        term_sum.astype(jnp.bfloat16), "tensor", scatter_dimension=0, tiled=True
    ).astype(jnp.float32)
    grad_hidden = feature_part.T.astype(jnp.bfloat16)
    my_index = lax.axis_index("batch")
    positions = jnp.arange(R_DEV, dtype=jnp.int32)
    own_slots = my_index * R_DEV + positions
    request_ids = jnp.arange(all_slots.shape[0], dtype=jnp.int32)
    matches = all_slots[None, :] == own_slots[:, None]
    source = jnp.sum(jnp.where(matches, request_ids[None, :], 0), axis=1)
    everything = lax.all_gather(grad_init.astype(jnp.bfloat16), "batch", axis=0, tiled=True).astype(
        grad_init.dtype
    )
    slot_state_grad = everything[source]
    return (
        grad_hidden,
        grad_w_query,
        grad_w_key,
        grad_w_value,
        grad_conv_query,
        grad_conv_key,
        grad_conv_value,
        grad_decay,
        grad_beta,
        slot_state_grad,
    )


def solution(mesh):
    placed = (
        P("batch", "tensor"),
        P(None, "tensor"),
        P(None, "tensor"),
        P(None, "tensor"),
        P(None, "tensor"),
        P(None, "tensor"),
        P(None, "tensor"),
        P("batch", "tensor"),
        P("batch", "tensor"),
        P("batch", "tensor", None, None),
        P("batch", "tensor"),
        P("batch", "tensor", None, None),
        P("batch"),
        P("batch"),
    )
    return jax.shard_map(
        body,
        mesh=mesh,
        in_specs=placed,
        out_specs=(
            P("batch", "tensor"),
            P("batch", "tensor"),
            P("batch", "tensor"),
            P("batch", "tensor"),
            P(None, "tensor"),
            P(None, "tensor"),
            P(None, "tensor"),
            P("batch", "tensor"),
            P("batch", "tensor"),
            P("batch", "tensor", None, None),
        ),
        check_vma=False,
    )
```

profile of v0, /device:TPU:0, one launch (start us, length us, event | category | flops | bytes accessed | tf_op | source)
XLA Modules:
  0.0 710.6 jit_solution(9368347106355070869)
XLA Ops:
  19.9 40.2 %all-gather.3.cloned.1.call-done = bf16[1024,2048]{1,0:T(8,128)(2,1)} async-done(((bf16[1024,256]{1,0:T(8,128)(2,1)}), bf16[1024,2048]{1,0:T(8,128)(2,1)}) %all-gather.3.cloned.1.call-update) | async-done | bytes 4194320 | tf_op jit(solution)/shard_map/all_gather | solution.py:173
  60.2 4.2 convolution_convert_fusion.1
  66.6 3.7 convolution_convert_fusion.2
  71.5 4.5 convolution_convert_fusion
  78.2 3.7 multiply_reduce_fusion.19
  97.5 5.0 fusion.120
  104.7 316.0 %custom-call.10 = f32[8,4,1,128,128]{3,4,2,1,0:T(8,128)} custom-call(f32[8,4,1,128,128]{4,3,2,1,0:T(8,128)} %add_bitcast_fusion), custom_call_target="InvertDiagBlocksLowerTriangular" | custom-call | tf_op jit(solution)/shard_map/jvp()/while/body/eval_jaxpr/jit(_solve_triangular)/vmap(vmap())/triangular_solve | solution.py:46
  420.7 6.5 fusion.28
  427.2 4.1 fusion.24
  435.1 6.1 fusion.45
  449.7 11.0 %multiply_reduce_fusion.7 = (f32[512]{0:T(512)S(1)}, f32[512]{0:T(512)S(1)}, f32[512]{0:T(512)S(1)}, f32[512]{0:T(512)}, f32[8,128,512]{1,2,0:T(8,128)}, /*index=5*/f32[8,128,512]{1,2,0:T(8,128)S(1)}) fusion(f32[8,128,512]{1,2,0:T(8,128)} %copy.474, f32[8,128,512]{1,2,0:T(8,128)} %bitcast.273, f32[512]{0:T(512)S(1)} %bitcast.290, f32[512]{0:T(512)S(1)} %bitcast.292, ...), kind=kLoop, calls=%fused_computation.59 | loop fusion | flops 12580864 | bytes 8404992 | tf_op jit(solution)/shard_map/transpose(jvp())/reduce_sum | solution.py:18
  469.4 4.0 fusion.9
  476.9 5.8 fusion.121
  485.1 4.8 fusion.26
  489.9 4.5 fusion.119
  494.5 4.5 fusion.122
  499.0 6.2 fusion.15
  505.2 4.9 multiply_reduce_fusion.1
  510.5 11.6 %multiply_reduce_fusion = (f32[8,4,128]{2,1,0:T(4,128)S(1)}, f32[8,4,128,128]{3,2,1,0:T(8,128)S(1)}, f32[8,4,128,128]{3,2,1,0:T(8,128)}) fusion(f32[8,4,128,128]{3,2,1,0:T(8,128)} %copy-done.29, f32[8,4,128]{2,1,0:T(4,128)S(1)} %copy.471, pred[128,128]{1,0:T(8,128)(4,1)S(1)} %get-tuple-element.697, f32[8,4,128]{2,1,0:T(4,128)S(1)} %copy.465, ...), kind=kOutput, calls=%fused_computation.51 | convolution fusion | flops 815263744 | bytes 16875520 | tf_op jit(solution)/shard_map/transpose(jvp())/while/body/eval_jaxpr/jit(_solve_triangular)/vmap(vmap())/triangular_solve/dot.0 | solution.py:46
  523.7 4.6 fusion.37
  528.3 4.8 add_convert_fusion.1
  533.2 7.0 fusion.56
  540.2 4.9 fusion.47
  553.4 7.8 %fusion.39 = f32[8,4,128,128]{2,3,1,0:T(8,128)S(1)} fusion(f32[8,4,128,128]{2,3,1,0:T(8,128)} %bitcast.262, f32[8,4,128]{2,1,0:T(4,128)S(1)} %copy.465, f32[8,4,128,128]{3,2,1,0:T(8,128)} %get-tuple-element.694, f32[8,4,128]{2,1,0:T(4,128)S(1)} %copy.471, pred[128,128]{1,0:T(8,128)(4,1)S(1)} %get-tuple-element.697), kind=kOutput, calls=%fused_computation.76 | convolution fusion | flops 807927808 | bytes 6340608 | tf_op jit(solution)/shard_map/transpose(jvp())/while/body/eval_jaxpr/rhik,rhjk->rhij/dot_general | solution.py:39
  564.2 4.6 add_add_fusion
  589.8 9.3 %convert_bitcast_fusion = bf16[2048,1024]{0,1:T(8,128)(2,1)} fusion(bf16[1024,2048]{1,0:T(8,128)(2,1)} %all-gather.3.cloned.1.call-done, bf16[1024,512]{1,0:T(8,128)(2,1)} %bitcast.281, bf16[1024,256]{1,0:T(8,128)(2,1)} %bitcast.278, bf16[1024,256]{1,0:T(8,128)(2,1)} %bitcast.276), kind=kOutput, calls=%fused_computation.5 | convolution fusion | flops 4303355904 | bytes 10485760 | tf_op jit(solution)/shard_map/dot_general | solution.py:208
  610.6 7.5 %all-reduce.28 = s32[32]{0:T(128)S(1)} all-reduce(s32[32]{0:T(128)S(1)} %dynamic-update-slice), channel_id=1, replica_groups=mesh['batch'=4,'tensor'=8] {'batch'}, use_global_device_ids=true, to_apply=%add.28 | all-reduce | flops 32 | bytes 256
  618.3 5.2 reduce_window_sum.32
  623.6 15.8 %all-reduce.29 = (f32[4,256]{1,0:T(4,128)}, f32[4,256]{1,0:T(4,128)}, f32[4,512]{1,0:T(4,128)}) all-reduce(f32[4,256]{1,0:T(4,128)S(1)} %pad_add_fusion.11, f32[4,256]{1,0:T(4,128)S(1)} %pad_add_fusion.10, f32[4,512]{1,0:T(4,128)S(1)} %pad_add_fusion.9), channel_id=1, replica_groups=mesh['batch'=4,'tensor'=8] {'batch'}, use_global_device_ids=true, to_apply=%region_13.16 | all-reduce | flops 4096 | bytes 32768 | tf_op jit(solution)/shard_map/psum | solution.py:202
  640.0 6.5 convert_element_type.102
  646.5 5.5 gather_fusion
  661.9 42.0 %reduce-scatter.3.cloned.1.call-done = bf16[256,1024]{0,1:T(8,128)(2,1)} async-done(((bf16[2048,1024]{0,1:T(8,128)(2,1)}), bf16[256,1024]{0,1:T(8,128)(2,1)}) %reduce-scatter.3.cloned.1.call-update) | async-done | bytes 524304 | tf_op jit(solution)/shard_map/reduce_scatter | solution.py:229
  (212 shorter events, 118.3 us)
Async XLA Ops:
  7.2 64.4 %copy-start = (bf16[2048,512]{1,0:T(8,128)(2,1)S(1)}, bf16[2048,512]{1,0:T(8,128)(2,1)}, u32[]{:S(2)}) copy-start(bf16[2048,512]{1,0:T(8,128)(2,1)} %param.21) | copy-start | bytes 6291460
  7.2 53.0 %all-gather.3.cloned.1.call-start = ((), (), s32[]{:S(2)}) async-start(), calls=%async_computation.2 | async-start | bytes 4718592 | tf_op jit(solution)/shard_map/all_gather | solution.py:173
  7.9 4.2 copy-start.48
  8.0 4.3 copy-start.45
  8.0 632.0 %all-gather.5.cloned.1.call-start = ((), (), s32[]{:S(2)}) async-start(), calls=%async_computation.5 | async-start | bytes 5242880 | tf_op jit(solution)/shard_map/all_gather | solution.py:239
  16.7 43.5 %copy-start.43 = (bf16[2048,256]{1,0:T(8,128)(2,1)S(1)}, bf16[2048,256]{1,0:T(8,128)(2,1)}, u32[]{:S(2)}) copy-start(bf16[2048,256]{1,0:T(8,128)(2,1)} %param.19) | copy-start | bytes 3145732
  97.2 5.3 copy-start.29
  97.5 5.0 copy-start.14
  420.7 6.5 copy-start.7
  420.7 6.5 copy-start.26
  427.2 4.2 copy-start.2
  427.2 4.2 copy-start.21
  435.0 6.1 copy-start.17
  435.1 6.1 copy-start.5
  476.9 17.5 %copy-start.24 = (f32[8,4,128,128]{3,2,1,0:T(8,128)}, f32[8,4,128,128]{3,2,1,0:T(8,128)S(1)}, u32[]{:S(2)}) copy-start(f32[8,4,128,128]{3,2,1,0:T(8,128)S(1)} %fusion.21) | copy-start | bytes 6291460
  476.9 5.8 copy-start.12
  485.1 4.8 copy-start.22
  489.9 4.5 copy-start.28
  494.5 10.7 %copy-start.30 = (f32[8,4,128,128]{2,3,1,0:T(8,128)}, f32[8,4,128,128]{2,3,1,0:T(8,128)S(1)}, u32[]{:S(2)}) copy-start(f32[8,4,128,128]{2,3,1,0:T(8,128)S(1)} %fusion.119) | copy-start | bytes 6291460
  510.5 12.4 %copy-start.15 = (f32[8,128,2,2,128]{1,4,3,2,0:T(8,128)S(1)}, f32[8,128,2,2,128]{1,4,3,2,0:T(8,128)}, u32[]{:S(2)}) copy-start(f32[8,128,2,2,128]{1,4,3,2,0:T(8,128)} %copy-done.14) | copy-start | bytes 6291460
  523.7 4.6 copy-start.19
  523.7 4.6 copy-start.23
  523.7 4.7 copy-start.25
  533.1 118.8 %reduce-scatter.5.cloned.1.call-start = ((), (), s32[]{:S(2)}) async-start(), calls=%async_computation.4 | async-start | bytes 5242880 | tf_op jit(solution)/shard_map/reduce_scatter | solution.py:207
  533.2 7.0 copy-start.10
  533.2 7.0 copy-start.13
  553.4 7.8 %copy-start.4 = (f32[8,128,2,2,128]{1,4,3,2,0:T(8,128)S(1)}, f32[8,128,2,2,128]{1,4,3,2,0:T(8,128)}, u32[]{:S(2)}) copy-start(f32[8,128,2,2,128]{1,4,3,2,0:T(8,128)} %copy-done.1) | copy-start | bytes 6291460
  553.4 7.8 %copy-start.27 = (f32[8,4,128,128]{3,2,1,0:T(8,128)S(1)}, f32[8,4,128,128]{3,2,1,0:T(8,128)}, u32[]{:S(2)}) copy-start(f32[8,4,128,128]{3,2,1,0:T(8,128)} %get-tuple-element.694) | copy-start | bytes 6291460
  553.4 10.8 %copy-start.38 = (f32[8,4,128,128]{2,3,1,0:T(8,128)S(1)}, f32[8,4,128,128]{2,3,1,0:T(8,128)}, u32[]{:S(2)}) copy-start(f32[8,4,128,128]{2,3,1,0:T(8,128)} %get-tuple-element.695) | copy-start | bytes 6291460
  599.2 104.7 %reduce-scatter.3.cloned.1.call-start = ((), (), s32[]{:S(2)}) async-start(), calls=%async_computation.3 | async-start | bytes 4718592 | tf_op jit(solution)/shard_map/reduce_scatter | solution.py:229
  608.5 15.1 %copy-start.50 = (f32[512]{0:T(512)S(1)}, f32[512]{0:T(512)}, u32[]{:S(2)}) copy-start(f32[512]{0:T(512)} %get-tuple-element.626) | copy-start | bytes 6148
  651.9 4.8 copy-start.40
  (28 other events, 75.6 us)
Sparse Core Ops, SparseCore 0:
  9.6 50.4 all-gather.2
  533.3 50.9 all-gather.4
  599.3 51.7 reduce-scatter.4
  653.9 49.9 reduce-scatter.2
where the time goes:
time: 716 us; the launch traced here: 711 us
  other arithmetic  386 us (54%)
  matrix products  150 us (21%)
  waiting for transfers between devices  82.9 us (12%)
  local copies, waits for them, and re-layouts  52.5 us (7%)
  blocking collectives  23.3 us (3%)
  between operations  15.6 us (2%)
    another operation x5, other arithmetic, block_step(): jax.scipy.linalg.solve_triangular(system, scaled, lower=True, unit_diagon...  318 us
    reduce_scatter x1, waiting for transfers between devices, body(): lax.psum_scatter(term_sum.astype(jnp.bfloat16), 'tensor', scatter_dimensi...  42 us
    all_gather x1, waiting for transfers between devices, body(): features_all = lax.all_gather(hidden, 'tensor', axis=1, tiled=True)  40.2 us
    another operation x3, matrix products, block_step(): jax.scipy.linalg.solve_triangular(system, scaled, lower=True, unit_diagon...  18 us
    dot_general x3, matrix products, block_step(): jnp.einsum('rhik,rhjk->rhij', queries, key_rows, precision=precise) * within  16.6 us
    dot_general x3, matrix products, block_step(): jnp.einsum('rhck,rhkv->rhcv', queries, carry_state, precision=precise)  16 us
    psum x1, blocking collectives, body(): lax.psum((local_grads[3], local_grads[4], local_grads[5]), 'batch')  15.8 us
    reduce_sum x3, other arithmetic, short_conv(): padded[:, offset:offset + length, :] * weights[offset]  14.9 us
  transfers between devices with their start and end apart: 4, of which 2 were waited for; matrix products, arithmetic and copies ran while one was open for 16% of the time, Pallas kernels for 0%

commit v1 on v0

v1 whole, which is shorter than its diff:
```python
import functools
import jax
import jax.numpy as jnp
from jax import lax
from jax.experimental import pallas as pl
from jax.experimental.pallas import tpu as pltpu
from jax.sharding import PartitionSpec as P

EPSILON = 1e-06
F32 = jnp.float32
BF16 = jnp.bfloat16
NN = (((1,), (0,)), ((), ()))
NT = (((1,), (1,)), ((), ()))
TN = (((0,), (0,)), ((), ()))


def dot(a, b, dims=NN):
    return lax.dot_general(a.astype(BF16), b.astype(BF16), dims, preferred_element_type=F32)


def exact_dot(a, b, dims=NN):
    return lax.dot_general(
        a, b, dims, preferred_element_type=F32, precision=lax.Precision.HIGHEST
    )


def shift_down(x, count, rows):
    if count == 0:
        return x
    return jnp.where(rows >= count, pltpu.roll(x, count, 0), 0.0)


def shift_up(x, count, rows):
    if count == 0:
        return x
    size = x.shape[0]
    return jnp.where(rows < size - count, pltpu.roll(x, size - count, 0), 0.0)


def unit_lower_inverse(couplings, rows, cols):
    size = rows.shape[0]
    one = (rows == cols).astype(F32)
    first = (rows % 2 == 1) & (cols == rows - 1)
    inverses = [one - jnp.where(first, a, 0.0) for a in couplings]
    block = 2
    while block < min(8, size):
        mask = ((rows // block) % 2 == 1) & (cols // block == rows // block - 1)
        inner = [dot(t, jnp.where(mask, a, 0.0)) for t, a in zip(inverses, couplings)]
        inverses = [t - dot(x, t) for t, x in zip(inverses, inner)]
        block *= 2
    while block < size:
        count = size // (2 * block)
        half_rows = lax.broadcasted_iota(jnp.int32, (size // 2, size), 0)
        half_cols = lax.broadcasted_iota(jnp.int32, (size // 2, size), 1)
        mask = half_cols // block == 2 * (half_rows // block)
        odd = [
            jnp.concatenate(
                [t[(2 * i + 1) * block : (2 * i + 2) * block] for i in range(count)], axis=0
            )
            for t in inverses
        ]
        inner = [jnp.where(mask, dot(o, a), 0.0) for o, a in zip(odd, couplings)]
        odd = [o - dot(x, t) for o, x, t in zip(odd, inner, inverses)]
        inverses = [
            jnp.concatenate(
                [
                    piece
                    for i in range(count)
                    for piece in (
                        t[2 * i * block : (2 * i + 1) * block],
                        o[i * block : (i + 1) * block],
                    )
                ],
                axis=0,
            )
            for t, o in zip(inverses, odd)
        ]
        block *= 2
    return inverses


def core_kernel(
    key_heads,
    group,
    lengths,
    places,
    proj_q,
    proj_k,
    proj_v,
    taps_q,
    taps_k,
    taps_v,
    decay,
    beta,
    init_state,
    grad_out,
    state_grad,
    grads,
    grad_taps,
    grad_decay,
    grad_beta,
    grad_init,
):
    step = pl.program_id(0)
    size = proj_q.shape[0]
    width = init_state.shape[-1]
    heads = key_heads * group
    rows = lax.broadcasted_iota(jnp.int32, (size, size), 0)
    cols = lax.broadcasted_iota(jnp.int32, (size, size), 1)
    wide_rows = lax.broadcasted_iota(jnp.int32, (size, width), 0)
    length = lengths[step]
    causal = rows >= cols
    strict = rows > cols
    lower = causal.astype(F32)
    upper = (rows <= cols).astype(F32)
    one = (rows == cols).astype(F32)
    live_row = (lax.broadcasted_iota(jnp.int32, (heads, size), 1) < length).astype(F32)
    live_col = (lax.broadcasted_iota(jnp.int32, (size, heads), 0) < length).astype(F32)
    live_wide = (wide_rows < length).astype(F32)

    gate_row = decay[0] * live_row
    rate_row = beta[0] * live_row
    cum_row = exact_dot(gate_row, lower, NT)
    cum_col = exact_dot(lower, gate_row, NT)
    rate_col = exact_dot(one, rate_row, NT)
    last_row = cum_row[:, size - 1 :]
    growth_col = jnp.exp(cum_col)

    def prepare(ref, taps, index):
        cut = slice(index * width, (index + 1) * width)
        x = ref[:, cut].astype(F32)
        mixed = x * taps[3:4, cut]
        for i in range(3):
            mixed = mixed + shift_down(x, 3 - i, wide_rows) * taps[i : i + 1, cut]
        gate = 1.0 / (1.0 + jnp.exp(-mixed))
        active = mixed * gate
        return active, gate + active * (1.0 - gate)

    def unit(active, factor):
        total = jnp.sum(active * active, axis=-1, keepdims=True) + EPSILON
        scale = factor * lax.rsqrt(total)
        return active * scale, scale, 1.0 / total

    q_in = [prepare(proj_q, taps_q, i) for i in range(key_heads)]
    k_in = [prepare(proj_k, taps_k, i) for i in range(key_heads)]
    v_in = [prepare(proj_v, taps_v, i) for i in range(heads)]
    q_unit = [unit(x[0], width ** (-0.5)) for x in q_in]
    k_unit = [unit(x[0], 1.0) for x in k_in]
    q_f = [x[0] for x in q_unit]
    k_f = [x[0] for x in k_unit]
    q_b = [x.astype(BF16) for x in q_f]
    k_b = [x.astype(BF16) for x in k_f]
    kk = [dot(k, k, NT) for k in k_b]
    qk = [dot(q, k, NT) for q, k in zip(q_b, k_b)]
    kq = [dot(k, q, NT) for q, k in zip(q_b, k_b)]

    cum_c = [cum_col[:, h : h + 1] for h in range(heads)]
    cum_r = [cum_row[h : h + 1, :] for h in range(heads)]
    rate = [rate_col[:, h : h + 1] for h in range(heads)]
    growth = [growth_col[:, h : h + 1] for h in range(heads)]
    final = [jnp.exp(last_row[h : h + 1, :]) for h in range(heads)]
    rest = [jnp.exp(last_row[h : h + 1, :] - cum_c[h]) for h in range(heads)]
    within = [
        jnp.where(causal, jnp.exp(jnp.where(causal, cum_c[h] - cum_r[h], 0.0)), 0.0)
        for h in range(heads)
    ]
    within_t = [
        jnp.where(rows <= cols, jnp.exp(jnp.where(rows <= cols, cum_r[h] - cum_c[h], 0.0)), 0.0)
        for h in range(heads)
    ]
    couplings = [
        jnp.where(strict, rate[h] * kk[h // group] * within[h], 0.0) for h in range(heads)
    ]
    inverses = [t.astype(BF16) for t in unit_lower_inverse(couplings, rows, cols)]

    s_f = [init_state[0, h] for h in range(heads)]
    ds_f = [state_grad[0, h] for h in range(heads)]
    s_b = [x.astype(BF16) for x in s_f]
    ds_b = [x.astype(BF16) for x in ds_f]
    k_s = [dot(k_b[h // group], s_b[h]) for h in range(heads)]
    left = [v_in[h][0] - growth[h] * k_s[h] for h in range(heads)]
    new_b = [dot(inverses[h], rate[h] * left[h]).astype(BF16) for h in range(heads)]
    out_b = [
        (grad_out[:, h * width : (h + 1) * width].astype(F32) * live_wide).astype(BF16)
        for h in range(heads)
    ]
    d_new = [
        dot(kq[h // group] * within_t[h], out_b[h]) + rest[h] * dot(k_b[h // group], ds_b[h])
        for h in range(heads)
    ]
    d_right = [dot(inverses[h], d_new[h], TN) for h in range(heads)]
    d_scores = [dot(out_b[h], new_b[h], NT) * within[h] for h in range(heads)]
    d_coup = [
        jnp.where(strict, -dot(d_right[h], new_b[h], NT) * within[h], 0.0) for h in range(heads)
    ]
    back_b = [(-(rate[h] * growth[h]) * d_right[h]).astype(BF16) for h in range(heads)]
    u_q = [growth[h] * dot(out_b[h], s_b[h], NT) for h in range(heads)]
    u_k = [dot(back_b[h], s_b[h], NT) for h in range(heads)]
    u_e = [rest[h] * dot(new_b[h], ds_b[h], NT) for h in range(heads)]
    cum_from_rows = []
    cum_from_cols = []
    rate_grads = []
    last_grads = []
    for h in range(heads):
        g = h // group
        y = d_coup[h] * kk[g]
        y_row = jnp.sum(y, axis=-1, keepdims=True)
        scored = d_scores[h] * qk[g]
        ended = jnp.sum(k_f[g] * u_e[h], axis=-1, keepdims=True)
        rate_grads.append(jnp.sum(d_right[h] * left[h], axis=-1, keepdims=True) + y_row)
        direct = q_f[g] * u_q[h] + k_f[g] * u_k[h] + scored
        cum_from_rows.append(
            jnp.sum(direct, axis=-1, keepdims=True) + rate[h] * y_row - ended
        )
        cum_from_cols.append(jnp.sum(scored + rate[h] * y, axis=0, keepdims=True))
        last_grads.append(
            jnp.sum(ended, axis=0, keepdims=True)
            + final[h] * jnp.sum(jnp.sum(ds_f[h] * s_f[h], axis=-1, keepdims=True), axis=0, keepdims=True)
        )
        grad_init[0, h] = (
            final[h] * ds_f[h]
            + dot(q_b[g], growth[h] * out_b[h].astype(F32), TN)
            + dot(k_b[g], back_b[h], TN)
        ).astype(BF16)
    gate_grad = exact_dot(upper, jnp.concatenate(cum_from_rows, axis=1))
    gate_grad = gate_grad - exact_dot(upper, jnp.concatenate(cum_from_cols, axis=0), NT)
    gate_grad = gate_grad + jnp.concatenate(last_grads, axis=1)
    grad_decay[...] = gate_grad * live_col
    grad_beta[...] = jnp.concatenate(rate_grads, axis=1) * live_col

    @pl.when(step == 0)
    def _():
        grad_taps[...] = jnp.zeros_like(grad_taps)

    def conv_back(d_active, slope, ref, taps, index, offset):
        cut = slice(index * width, (index + 1) * width)
        place = slice(offset + index * width, offset + (index + 1) * width)
        x = ref[:, cut].astype(F32)
        d_mixed = d_active * slope
        d_x = d_mixed * taps[3:4, cut]
        sums = []
        for i in range(3):
            d_x = d_x + shift_up(d_mixed, 3 - i, wide_rows) * taps[i : i + 1, cut]
            sums.append(jnp.sum(d_mixed * shift_down(x, 3 - i, wide_rows), axis=0, keepdims=True))
        sums.append(jnp.sum(d_mixed * x, axis=0, keepdims=True))
        grads[:, place] = d_x.astype(BF16)
        grad_taps[:, place] += jnp.concatenate(sums, axis=0)

    def unit_back(d_unit, unit_in):
        unit_rows, scale, inverse_total, active = unit_in
        inner = jnp.sum(d_unit * active, axis=-1, keepdims=True)
        return scale * (d_unit - active * (inner * inverse_total))

    for g in range(key_heads):
        members = range(g * group, (g + 1) * group)
        scores_sum = sum(d_scores[h] for h in members).astype(BF16)
        kk_sum = sum(rate[h] * d_coup[h] for h in members).astype(BF16)
        d_q = sum(u_q[h] for h in members) + dot(scores_sum, k_b[g])
        d_k = sum(u_k[h] + u_e[h] for h in members)
        d_k = d_k + dot(scores_sum, q_b[g], TN) + dot(kk_sum, k_b[g]) + dot(kk_sum, k_b[g], TN)
        d_q = unit_back(d_q, q_unit[g] + (q_in[g][0],))
        d_k = unit_back(d_k, k_unit[g] + (k_in[g][0],))
        conv_back(d_q, q_in[g][1], proj_q, taps_q, g, 0)
        conv_back(d_k, k_in[g][1], proj_k, taps_k, g, key_heads * width)
    for h in range(heads):
        conv_back(rate[h] * d_right[h], v_in[h][1], proj_v, taps_v, h, 2 * key_heads * width)


def core_call(proj_q, proj_k, proj_v, taps_q, taps_k, taps_v, decay, beta, init_state, grad_out, state_grad, lengths, places, out_places):
    requests, heads, width, _ = init_state.shape
    size = proj_q.shape[0] // requests
    key_heads = proj_q.shape[1] // width
    columns = proj_q.shape[1] * 2 + proj_v.shape[1]

    def rows_of(array):
        return pl.BlockSpec((size, array.shape[1]), lambda r, *_: (r, 0))

    def fixed(array):
        return pl.BlockSpec(array.shape, lambda r, *_: (0,) * array.ndim)

    by_request = pl.BlockSpec((1, heads, size), lambda r, *_: (r, 0, 0))
    state = pl.BlockSpec((1, heads, width, width), lambda r, *_: (r, 0, 0, 0))
    return pl.pallas_call(
        functools.partial(core_kernel, key_heads, heads // key_heads),
        grid_spec=pltpu.PrefetchScalarGridSpec(
            num_scalar_prefetch=2,
            grid=(requests,),
            in_specs=[
                rows_of(proj_q), rows_of(proj_k), rows_of(proj_v),
                fixed(taps_q), fixed(taps_k), fixed(taps_v),
                by_request, by_request, state, rows_of(grad_out), state,
            ],
            out_specs=[
                pl.BlockSpec((size, columns), lambda r, *_: (r, 0)),
                pl.BlockSpec((taps_q.shape[0], columns), lambda r, *_: (0, 0)),
                pl.BlockSpec((size, heads), lambda r, *_: (r, 0)),
                pl.BlockSpec((size, heads), lambda r, *_: (r, 0)),
                pl.BlockSpec((1, heads, width, width), lambda r, lengths, places: (places[r], 0, 0, 0)),
            ],
        ),
        out_shape=[
            jax.ShapeDtypeStruct((requests * size, columns), BF16),
            jax.ShapeDtypeStruct((taps_q.shape[0], columns), F32),
            jax.ShapeDtypeStruct((requests * size, heads), F32),
            jax.ShapeDtypeStruct((requests * size, heads), F32),
            jax.ShapeDtypeStruct((out_places, heads, width, width), BF16),
        ],
        compiler_params=pltpu.CompilerParams(vmem_limit_bytes=48 << 20),
        name="core_grads",
    )(lengths, places, proj_q, proj_k, proj_v, taps_q, taps_k, taps_v, decay, beta, init_state, grad_out, state_grad)


def place_kernel(sources, ranks, *refs):
    received, out = refs[:-1], refs[-1]
    step = pl.program_id(0)
    for index, block in enumerate(received):

        @pl.when(sources[step] == index)
        def _():
            out[...] = block[...].astype(out.dtype)


def place_states(sources, ranks, received):
    requests = sources.shape[0]
    block = (1,) + received[0].shape[1:]

    def pick(index):
        def index_map(r, sources, ranks):
            return (jnp.where(sources[r] == index, ranks[r], 0), 0, 0, 0)

        return index_map

    return pl.pallas_call(
        place_kernel,
        grid_spec=pltpu.PrefetchScalarGridSpec(
            num_scalar_prefetch=2,
            grid=(requests,),
            in_specs=[pl.BlockSpec(block, pick(i)) for i in range(len(received))],
            out_specs=pl.BlockSpec(block, lambda r, *_: (r, 0, 0, 0)),
        ),
        out_shape=jax.ShapeDtypeStruct((requests,) + block[1:], F32),
        compiler_params=pltpu.CompilerParams(vmem_limit_bytes=32 << 20),
        name="place_states",
    )(sources, ranks, *received)


def slot_plan(slot_map, all_slots, me, parts):
    requests = slot_map.shape[0]
    capacity = max(1, requests // parts)
    owners = all_slots // requests
    request_ids = jnp.arange(all_slots.shape[0], dtype=jnp.int32)
    earlier = (
        (request_ids[:, None] > request_ids[None, :])
        & (request_ids[:, None] // requests == request_ids[None, :] // requests)
        & (owners[:, None] == owners[None, :])
    )
    ranks = jnp.sum(earlier.astype(jnp.int32), axis=1)
    hops = jnp.bitwise_xor(owners, request_ids // requests)
    places = lax.dynamic_slice_in_dim(hops * capacity + ranks, me * requests, requests)
    own_slots = me * requests + jnp.arange(requests, dtype=jnp.int32)
    matches = (all_slots[None, :] == own_slots[:, None]).astype(jnp.int32)
    sources = jnp.sum(matches * hops[None, :], axis=1)
    source_ranks = jnp.sum(matches * ranks[None, :], axis=1)
    return places, sources, source_ranks, capacity


def swap(array, axis, parts, hop):
    return lax.ppermute(array, axis, [(i, i ^ hop) for i in range(parts)])


def body(
    hidden, w_query, w_key, w_value, conv_query, conv_key, conv_value, decay_log, beta_gate,
    init_state, grad_out, state_grad_in, rollout_lengths, slot_map,
):
    parts = lax.axis_size("batch")
    me = lax.axis_index("batch")
    requests = rollout_lengths.shape[0]
    size = hidden.shape[0] // requests
    heads = init_state.shape[1]
    all_slots = lax.all_gather(slot_map, "batch", axis=0, tiled=True)
    features = lax.all_gather(hidden, "tensor", axis=1, tiled=True)
    places, sources, ranks, capacity = slot_plan(slot_map, all_slots, me, parts)
    proj = [
        jnp.dot(features, w, preferred_element_type=F32).astype(BF16)
        for w in (w_query, w_key, w_value)
    ]

    def by_head(array):
        return array.reshape(requests, size, heads).transpose(0, 2, 1)

    grads, grad_taps, grad_decay, grad_beta, sent = core_call(
        *proj, conv_query, conv_key, conv_value, by_head(decay_log), by_head(beta_gate),
        init_state, grad_out, state_grad_in, rollout_lengths, places, parts * capacity,
    )
    partial = lax.dot_general(features, grads, TN, preferred_element_type=F32).astype(BF16)
    blocks = partial.reshape(parts, -1, partial.shape[1])
    received = [
        swap(lax.dynamic_index_in_dim(blocks, me ^ hop, 0, False), "batch", parts, hop)
        for hop in range(1, parts)
    ]
    weight_grads = lax.dynamic_index_in_dim(blocks, me, 0, False).astype(F32)
    for block in received:
        weight_grads = weight_grads + block.astype(F32)
    q_cols, k_cols = w_query.shape[1], w_key.shape[1]
    grad_w = (
        weight_grads[:, :q_cols],
        weight_grads[:, q_cols : q_cols + k_cols],
        weight_grads[:, q_cols + k_cols :],
    )
    weights = jnp.concatenate([w_query, w_key, w_value], axis=1)
    term = lax.dot_general(weights, grads, NT, preferred_element_type=F32).astype(BF16)
    grad_hidden = lax.psum_scatter(term, "tensor", scatter_dimension=0, tiled=True).T
    hop = 1
    while hop < parts:
        grad_taps = grad_taps + swap(grad_taps, "batch", parts, hop)
        hop *= 2
    states = [sent[i * capacity : (i + 1) * capacity] for i in range(parts)]
    states = [states[0]] + [swap(states[i], "batch", parts, i) for i in range(1, parts)]
    slot_state_grad = place_states(sources, ranks, states)
    return (
        grad_hidden, *grad_w, grad_taps[:, :q_cols], grad_taps[:, q_cols : q_cols + k_cols],
        grad_taps[:, q_cols + k_cols :], grad_decay, grad_beta, slot_state_grad,
    )


def solution(mesh):
    placed = (
        P("batch", "tensor"),
        P(None, "tensor"),
        P(None, "tensor"),
        P(None, "tensor"),
        P(None, "tensor"),
        P(None, "tensor"),
        P(None, "tensor"),
        P("batch", "tensor"),
        P("batch", "tensor"),
        P("batch", "tensor", None, None),
        P("batch", "tensor"),
        P("batch", "tensor", None, None),
        P("batch"),
        P("batch"),
    )
    return jax.shard_map(
        body,
        mesh=mesh,
        in_specs=placed,
        out_specs=(
            P("batch", "tensor"),
            P("batch", "tensor"),
            P("batch", "tensor"),
            P("batch", "tensor"),
            P(None, "tensor"),
            P(None, "tensor"),
            P(None, "tensor"),
            P("batch", "tensor"),
            P("batch", "tensor"),
            P("batch", "tensor", None, None),
        ),
        check_vma=False,
    )
```

time: 716 us -> 241 us (0.34)
  other arithmetic: 386 us -> 3.09 us
  matrix products: 150 us -> 24.5 us
  Pallas kernels: 0 us -> 40.5 us
  blocking collectives: 23.3 us -> 8.82 us
  starting transfers between devices: 0.16 us -> 9.02 us
    another operation x10 -> x0, other arithmetic: 329 us -> none  [the longest x5 318 us: block_step(): jax.scipy.linalg.solve_triangular(system, scaled, lower=True, unit_diagon...]
    dot_general x25 -> x5, matrix products: 118 us -> 24.5 us  [the longest x1 9.37 us: body(): lax.dot_general(features, grads, TN, preferred_element_type=F32)]
    ppermute x0 -> x8, waiting for transfers between devices: none -> 42 us  [swap(): return lax.ppermute(array, axis, [(i, i ^ hop) for i in range(parts)])]
    reduce_scatter x2 -> x1, waiting for transfers between devices: 42 us -> 0.01 us  [body(): lax.psum_scatter(term, 'tensor', scatter_dimension=0, tiled=True)]
    pallas_call x0 -> x2, Pallas kernels: none -> 40.5 us  [the longest x1 36.9 us: core_call(): pl.pallas_call(functools.partial(core_kernel, key_heads, heads // key_hea...]
    dynamic_slice x0 -> x5, local copies, waits for them, and re-layouts: none -> 33.1 us  [the longest x3 17.5 us: body(): lax.dynamic_index_in_dim(blocks, me ^ hop, 0, False)]
    another operation x6 -> x0, matrix products: 32.5 us -> none  [the longest x3 18 us: block_step(): jax.scipy.linalg.solve_triangular(system, scaled, lower=True, unit_diagon...]
    reduce_sum x12 -> x2, other arithmetic: 31.8 us -> 0.36 us  [the longest x1 0.18 us: slot_plan(): ranks = jnp.sum(earlier.astype(jnp.int32), axis=1)]
  transfers between devices with their start and end apart: 4 -> 10, of which waited for: 2 -> 4; matrix products, arithmetic and copies ran while one was open for 16% -> 27% of each run, Pallas kernels for 0% -> 2%
where the time goes in v1:
time: 241 us; the launch traced here: 240 us
  waiting for transfers between devices  83 us (34%)
  local copies, waits for them, and re-layouts  55.9 us (23%)
  Pallas kernels  40.5 us (17%)
  matrix products  24.5 us (10%)
  between operations  14.9 us (6%)
  starting transfers between devices  9.02 us (4%)
  blocking collectives  8.82 us (4%)
  other arithmetic  3.09 us (1%)
    ppermute x8, waiting for transfers between devices, swap(): return lax.ppermute(array, axis, [(i, i ^ hop) for i in range(parts)])  42 us
    all_gather x1, waiting for transfers between devices, body(): features = lax.all_gather(hidden, 'tensor', axis=1, tiled=True)  40.3 us
    pallas_call x1, Pallas kernels, core_call(): pl.pallas_call(functools.partial(core_kernel, key_heads, heads // key_hea...  36.9 us
    dynamic_slice x3, local copies, waits for them, and re-layouts, body(): lax.dynamic_index_in_dim(blocks, me ^ hop, 0, False)  17.5 us
    dynamic_slice x1, local copies, waits for them, and re-layouts, body(): weight_grads = lax.dynamic_index_in_dim(blocks, me, 0, False).astype(F32)  15.5 us
    unnamed x29, local copies, waits for them, and re-layouts  10.7 us
    dot_general x1, matrix products, body(): lax.dot_general(features, grads, TN, preferred_element_type=F32)  9.37 us
    ppermute x8, starting transfers between devices, swap(): return lax.ppermute(array, axis, [(i, i ^ hop) for i in range(parts)])  8.94 us
  transfers between devices with their start and end apart: 10, of which 4 were waited for; matrix products, arithmetic and copies ran while one was open for 27% of the time, Pallas kernels for 2%

profile of v1, /device:TPU:0, one launch (start us, length us, event | category | flops | bytes accessed | tf_op | source)
XLA Modules:
  0.0 239.8 jit_solution(5983798930249935028)
XLA Ops:
  7.2 0.7 all-gather.2.cloned.1.call-update
  8.0 1.2 dynamic-slice
  9.9 0.9 dynamic-update-slice
  10.7 8.8 %all-reduce = s32[32]{0:T(128)S(1)} all-reduce(s32[32]{0:T(128)S(1)} %dynamic-update-slice), channel_id=1, replica_groups=mesh['batch'=4,'tensor'=8] {'batch'}, use_global_device_ids=true, to_apply=%add | all-reduce | flops 32 | bytes 256
  19.8 40.3 %all-gather.2.cloned.1.call-done = bf16[1024,2048]{1,0:T(8,128)(2,1)} async-done(((bf16[1024,256]{1,0:T(8,128)(2,1)}), bf16[1024,2048]{1,0:T(8,128)(2,1)}) %all-gather.2.cloned.1.call-update) | async-done | bytes 4194320 | tf_op jit(solution)/shard_map/all_gather | solution.py:381
  60.1 3.9 %convolution_convert_fusion.2.proj_q = bf16[1024,256]{1,0:T(8,128)(2,1)S(1)} fusion(bf16[1024,2048]{1,0:T(8,128)(2,1)} %all-gather.2.cloned.1.call-done, bf16[2048,256]{1,0:T(8,128)(2,1)} %param.15), kind=kOutput, calls=%fused_computation.13 | convolution fusion | flops 1074003968 | bytes 5767168 | tf_op jit(solution)/shard_map/dot_general | solution.py:384
  64.1 1.3 convolution_convert_fusion.1.proj_k
  65.7 2.3 convolution_convert_fusion.proj_v
  68.1 36.9 %core_grads.1 = (bf16[1024,1024]{1,0:T(8,128)(2,1)}, f32[4,1024]{1,0:T(4,128)S(1)}, f32[1024,4]{1,0:T(8,128)S(1)}, f32[1024,4]{1,0:T(8,128)S(1)}, bf16[8,4,128,128]{3,2,1,0:T(8,128)(2,1)S(1)}) custom-call(s32[8]{0:T(128)S(1)} %copy-done.6, s32[8]{0:T(128)S(1)} %dynamic_slice.16.places, bf16[1024,256]{1,0:T(8,128)(2,1)S(1)} %convolution_convert_fusion.2.proj_q, ...), custom_call_target="tpu_custom_call" | custom-call | tf_op jit(solution)/shard_map/core_grads/pallas_call | solution.py:283
  105.0 7.7 %fusion.6 = bf16[2048,1024]{1,0:T(8,128)(2,1)} fusion(bf16[1024,1024]{1,0:T(8,128)(2,1)} %get-tuple-element.15, bf16[2048,512]{1,0:T(8,128)(2,1)S(1)} %copy-done.8, bf16[2048,256]{1,0:T(8,128)(2,1)S(1)} %copy-done.10, bf16[2048,256]{1,0:T(8,128)(2,1)S(1)} %copy-done.9), kind=kOutput, calls=%fused_computation.7 | convolution fusion | flops 4309647360 | bytes 10485760 | tf_op jit(solution)/shard_map/dot_general | solution.py:411
  112.8 9.4 %convert_bitcast_fusion = bf16[2048,1024]{0,1:T(8,128)(2,1)} fusion(bf16[1024,1024]{1,0:T(8,128)(2,1)} %get-tuple-element.15, bf16[1024,2048]{1,0:T(8,128)(2,1)} %all-gather.2.cloned.1.call-done), kind=kOutput, calls=%fused_computation.6 | convolution fusion | flops 4297064448 | bytes 10485760 | tf_op jit(solution)/shard_map/dot_general | solution.py:395
  122.1 7.9 %reshape.116 = bf16[4,512,1024]{1,0,2:T(4,128)(2,1)} reshape(bf16[2048,1024]{0,1:T(8,128)(2,1)} %convert_bitcast_fusion) | data formatting | bytes 8388608 | tf_op jit(solution)/shard_map/reshape | solution.py:396
  130.0 15.5 %constant_dynamic-slice_fusion.3 = (bf16[1,512,1024]{1,0,2:T(2,128)(2,1)}, bf16[1,512,1024]{1,0,2:T(2,128)(2,1)}, bf16[1,512,1024]{1,0,2:T(2,128)(2,1)}, bf16[1,512,1024]{1,0,2:T(2,128)(2,1)}) fusion(bf16[4,512,1024]{1,0,2:T(4,128)(2,1)} %reshape.116, s32[]{:T(128)S(6)} %select_n.45, s32[]{:T(128)S(6)} %select_n.48, s32[]{:T(128)S(6)} %select_n.47, ...), kind=kLoop, calls=%fused_computation.33 | loop fusion | bytes 8388624 | tf_op jit(solution)/shard_map/jit(dynamic_index_in_dim)/dynamic_slice | solution.py:401
  145.6 5.8 %copy.34 = bf16[1,512,1024]{2,1,0:T(8,128)(2,1)} copy(bf16[1,512,1024]{1,0,2:T(2,128)(2,1)} %get-tuple-element.45) | data formatting | bytes 2097152 | tf_op jit(solution)/shard_map/jit(dynamic_index_in_dim)/dynamic_slice | solution.py:398
  151.4 2.4 %collective-permute-start.2 = (bf16[512,1024]{1,0:T(8,128)(2,1)}, bf16[512,1024]{1,0:T(8,128)(2,1)}, u32[]{:S(2)}, u32[]{:S(2)}) collective-permute-start(bf16[512,1024]{1,0:T(8,128)(2,1)} %bitcast.10), channel_id=1, source_target_pairs={{0,24},{8,16},{16,8},{24,0},{1,25},{9,17},{17,9},{25,1},{2,26},{10... | collective-permute-start | bytes 3145736 | tf_op jit(solution)/shard_map/ppermute | solution.py:368
  153.8 5.9 %copy.33 = bf16[1,512,1024]{2,1,0:T(8,128)(2,1)} copy(bf16[1,512,1024]{1,0,2:T(2,128)(2,1)} %get-tuple-element.46) | data formatting | bytes 2097152 | tf_op jit(solution)/shard_map/jit(dynamic_index_in_dim)/dynamic_slice | solution.py:398
  160.2 5.8 %copy.32 = bf16[1,512,1024]{2,1,0:T(8,128)(2,1)} copy(bf16[1,512,1024]{1,0,2:T(2,128)(2,1)} %get-tuple-element.47) | data formatting | bytes 2097152 | tf_op jit(solution)/shard_map/jit(dynamic_index_in_dim)/dynamic_slice | solution.py:398
  166.6 0.9 fusion.18
  167.5 1.5 collective-permute-start.5
  169.5 36.9 %collective-permute-done.3 = f32[4,1024]{1,0:T(4,128)S(1)} collective-permute-done((f32[4,1024]{1,0:T(4,128)S(1)}, f32[4,1024]{1,0:T(4,128)S(1)}, u32[]{:S(2)}, u32[]{:S(2)}) %collective-permute-start.3) | collective-permute-done | bytes 16416 | tf_op jit(solution)/shard_map/ppermute | solution.py:368
  206.9 3.2 %collective-permute-done.4 = f32[4,1024]{1,0:T(4,128)S(1)} collective-permute-done((f32[4,1024]{1,0:T(4,128)S(1)}, f32[4,1024]{1,0:T(4,128)S(1)}, u32[]{:S(2)}, u32[]{:S(2)}) %collective-permute-start.4) | collective-permute-done | bytes 16416 | tf_op jit(solution)/shard_map/ppermute | solution.py:368
  210.6 2.4 %collective-permute-start.7 = (bf16[2,4,128,128]{3,2,1,0:T(8,128)(2,1)}, bf16[2,4,128,128]{3,2,1,0:T(8,128)(2,1)S(1)}, u32[]{:S(2)}, u32[]{:S(2)}) collective-permute-start(bf16[2,4,128,128]{3,2,1,0:T(8,128)(2,1)} %get-tuple-element.50), channel_id=1, source_target_pairs={{0,24},{8,16},{16,8},{24,0},{1,25},{9,17},{17,9},{25,1},{2,26},{10... | collective-permute-start | bytes 786440 | tf_op jit(solution)/shard_map/ppermute | solution.py:368
  213.2 4.6 %copy.38 = bf16[1,512,1024]{2,1,0:T(8,128)(2,1)S(1)} copy(bf16[1,512,1024]{1,0,2:T(2,128)(2,1)} %get-tuple-element.44) | data formatting | bytes 2097152
  217.8 0.8 copy.36
  218.6 0.8 copy.37
  219.4 0.6 slice.45
  220.6 1.9 collective-permute-done.6.refs_2_
  222.5 3.6 %place_states.1 = f32[8,4,128,128]{3,2,1,0:T(8,128)} custom-call(s32[8]{0:T(128)S(1)} %get-tuple-element.41.sources, s32[8]{0:T(128)S(1)} %get-tuple-element.40.ranks, bf16[2,4,128,128]{3,2,1,0:T(8,128)(2,1)S(1)} %get-tuple-element.53.refs_0_, bf16[2,4,128,128]{3,2,1,0:T(8,128)(2,1)S(1)} %collective-permute-done.5.refs_1_, ...), custom_call_target="tpu_custom_call" | custom-call | tf_op jit(solution)/shard_map/place_states/pallas_call | solution.py:333
  226.1 2.7 %fusion.10 = f32[512,1024]{1,0:T(8,128)S(1)} fusion(bf16[512,1024]{1,0:T(8,128)(2,1)} %collective-permute-done.2, bf16[512,1024]{1,0:T(8,128)(2,1)} %collective-permute-done.1, bf16[512,1024]{1,0:T(8,128)(2,1)} %collective-permute-done, bf16[1,512,1024]{2,1,0:T(8,128)(2,1)S(1)} %copy.38), kind=kLoop, calls=%fused_computation.10 | loop fusion | flops 3670016 | bytes 6291456 | tf_op jit(solution)/shard_map/add | solution.py:403
  228.8 1.0 slice.42
  229.9 1.1 fusion.17
  230.9 2.0 copy.35
  (47 shorter events, 4.2 us)
Async XLA Ops:
  7.2 53.0 %all-gather.2.cloned.1.call-start = ((), (), s32[]{:S(2)}) async-start(), calls=%async_computation.1 | async-start | bytes 4718592 | tf_op jit(solution)/shard_map/all_gather | solution.py:381
  7.9 223.0 %reduce-scatter.2.cloned.1.call-start = ((), (), s32[]{:S(2)}) async-start(), calls=%async_computation.2 | async-start | bytes 4718592 | tf_op jit(solution)/shard_map/reduce_scatter | solution.py:412
  19.8 44.2 %copy-start.10 = (bf16[2048,256]{1,0:T(8,128)(2,1)S(1)}, bf16[2048,256]{1,0:T(8,128)(2,1)}, u32[]{:S(2)}) copy-start(bf16[2048,256]{1,0:T(8,128)(2,1)} %param.16) | copy-start | bytes 3145732
  60.1 3.9 %copy-start.7 = (bf16[1024,2048]{1,0:T(8,128)(2,1)S(1)}, bf16[1024,2048]{1,0:T(8,128)(2,1)}, u32[]{:S(2)}) copy-start(bf16[1024,2048]{1,0:T(8,128)(2,1)} %all-gather.2.cloned.1.call-done) | copy-start | bytes 12582916
  64.0 1.6 copy-start.8
  65.6 2.4 copy-start
  65.6 2.4 copy-start.1
  65.6 2.4 copy-start.2
  65.7 2.4 copy-start.3
  65.7 2.4 %copy-start.4 = (f32[4,256]{1,0:T(4,128)S(1)}, f32[4,256]{1,0:T(4,128)}, u32[]{:S(2)}) copy-start(f32[4,256]{1,0:T(4,128)} %taps_q.1) | copy-start | bytes 12292
  65.7 2.4 %copy-start.5 = (f32[4,256]{1,0:T(4,128)S(1)}, f32[4,256]{1,0:T(4,128)}, u32[]{:S(2)}) copy-start(f32[4,256]{1,0:T(4,128)} %taps_k.1) | copy-start | bytes 12292
  65.7 2.4 %copy-start.6 = (s32[8]{0:T(128)S(1)}, s32[8]{0:T(128)}, u32[]{:S(2)}) copy-start(s32[8]{0:T(128)} %lengths.1) | copy-start | bytes 100
  68.1 37.0 %copy-start.9 = (bf16[2048,256]{1,0:T(8,128)(2,1)S(1)}, bf16[2048,256]{1,0:T(8,128)(2,1)}, u32[]{:S(2)}) copy-start(bf16[2048,256]{1,0:T(8,128)(2,1)} %param.15) | copy-start | bytes 3145732
  151.4 74.7 %collective-permute-start.2 = (bf16[512,1024]{1,0:T(8,128)(2,1)}, bf16[512,1024]{1,0:T(8,128)(2,1)}, u32[]{:S(2)}, u32[]{:S(2)}) collective-permute-start(bf16[512,1024]{1,0:T(8,128)(2,1)} %bitcast.10), channel_id=1, source_target_pairs={{0,24},{8,16},{16,8},{24,0},{1,25},{9,17},{17,9},{25,1},{2,26},{10... | collective-permute-start | bytes 3145736 | tf_op jit(solution)/shard_map/ppermute | solution.py:368
  159.7 66.5 %collective-permute-start.1 = (bf16[512,1024]{1,0:T(8,128)(2,1)}, bf16[512,1024]{1,0:T(8,128)(2,1)}, u32[]{:S(2)}, u32[]{:S(2)}) collective-permute-start(bf16[512,1024]{1,0:T(8,128)(2,1)} %bitcast.9), channel_id=1, source_target_pairs={{0,16},{8,24},{16,0},{24,8},{1,17},{9,25},{17,1},{25,9},{2,18},{10... | collective-permute-start | bytes 3145736 | tf_op jit(solution)/shard_map/ppermute | solution.py:368
  166.0 60.1 %collective-permute-start = (bf16[512,1024]{1,0:T(8,128)(2,1)}, bf16[512,1024]{1,0:T(8,128)(2,1)}, u32[]{:S(2)}, u32[]{:S(2)}) collective-permute-start(bf16[512,1024]{1,0:T(8,128)(2,1)} %bitcast.8), channel_id=1, source_target_pairs={{0,8},{8,0},{16,24},{24,16},{1,9},{9,1},{17,25},{25,17},{2,10},{10... | collective-permute-start | bytes 3145736 | tf_op jit(solution)/shard_map/ppermute | solution.py:368
  167.5 43.2 %collective-permute-start.5 = (bf16[2,4,128,128]{3,2,1,0:T(8,128)(2,1)S(1)}, bf16[2,4,128,128]{3,2,1,0:T(8,128)(2,1)S(1)}, u32[]{:S(2)}, u32[]{:S(2)}) collective-permute-start(bf16[2,4,128,128]{3,2,1,0:T(8,128)(2,1)S(1)} %get-tuple-element.52), channel_id=1, source_target_pairs={{0,8},{8,0},{16,24},{24,16},{1,9},{9,1},{17,25},{25,17},{2,10},{10... | collective-permute-start | bytes 786440 | tf_op jit(solution)/shard_map/ppermute | solution.py:368
  169.0 37.4 %collective-permute-start.3 = (f32[4,1024]{1,0:T(4,128)S(1)}, f32[4,1024]{1,0:T(4,128)S(1)}, u32[]{:S(2)}, u32[]{:S(2)}) collective-permute-start(f32[4,1024]{1,0:T(4,128)S(1)} %get-tuple-element.16), channel_id=1, source_target_pairs={{0,8},{8,0},{16,24},{24,16},{1,9},{9,1},{17,25},{25,17},{2,10},{10... | collective-permute-start | bytes 49160 | tf_op jit(solution)/shard_map/ppermute | solution.py:368
  206.4 3.7 %collective-permute-start.4 = (f32[4,1024]{1,0:T(4,128)S(1)}, f32[4,1024]{1,0:T(4,128)S(1)}, u32[]{:S(2)}, u32[]{:S(2)}) collective-permute-start(f32[4,1024]{1,0:T(4,128)S(1)} %add.69), channel_id=1, source_target_pairs={{0,16},{8,24},{16,0},{24,8},{1,17},{9,25},{17,1},{25,9},{2,18},{10... | collective-permute-start | bytes 49160 | tf_op jit(solution)/shard_map/ppermute | solution.py:368
  210.1 12.4 %collective-permute-start.6 = (bf16[2,4,128,128]{3,2,1,0:T(8,128)(2,1)}, bf16[2,4,128,128]{3,2,1,0:T(8,128)(2,1)S(1)}, u32[]{:S(2)}, u32[]{:S(2)}) collective-permute-start(bf16[2,4,128,128]{3,2,1,0:T(8,128)(2,1)} %get-tuple-element.51), channel_id=1, source_target_pairs={{0,16},{8,24},{16,0},{24,8},{1,17},{9,25},{17,1},{25,9},{2,18},{10... | collective-permute-start | bytes 786440 | tf_op jit(solution)/shard_map/ppermute | solution.py:368
  210.6 11.9 %collective-permute-start.7 = (bf16[2,4,128,128]{3,2,1,0:T(8,128)(2,1)}, bf16[2,4,128,128]{3,2,1,0:T(8,128)(2,1)S(1)}, u32[]{:S(2)}, u32[]{:S(2)}) collective-permute-start(bf16[2,4,128,128]{3,2,1,0:T(8,128)(2,1)} %get-tuple-element.50), channel_id=1, source_target_pairs={{0,24},{8,16},{16,8},{24,0},{1,25},{9,17},{17,9},{25,1},{2,26},{10... | collective-permute-start | bytes 786440 | tf_op jit(solution)/shard_map/ppermute | solution.py:368
Sparse Core Ops, SparseCore 0:
  9.6 50.4 all-gather.1
  112.9 48.2 reduce-scatter.1

commit v2 on v1

v2 whole, which is shorter than its diff:
```python
import functools
import jax
import jax.numpy as jnp
from jax import lax
from jax.experimental import pallas as pl
from jax.experimental.pallas import tpu as pltpu
from jax.sharding import PartitionSpec as P

EPSILON = 1e-06
F32 = jnp.float32
BF16 = jnp.bfloat16
NN = (((1,), (0,)), ((), ()))
NT = (((1,), (1,)), ((), ()))
TN = (((0,), (0,)), ((), ()))


def dot(a, b, dims=NN):
    return lax.dot_general(a.astype(BF16), b.astype(BF16), dims, preferred_element_type=F32)


def exact_dot(a, b, dims=NN):
    return lax.dot_general(
        a, b, dims, preferred_element_type=F32, precision=lax.Precision.HIGHEST
    )


def shift_down(x, count, rows):
    return jnp.where(rows >= count, pltpu.roll(x, count, 0), 0.0)


def shift_up(x, count, rows):
    size = x.shape[0]
    return jnp.where(rows < size - count, pltpu.roll(x, size - count, 0), 0.0)


def unit_lower_inverse(couplings, rows, cols):
    size = rows.shape[0]
    one = (rows == cols).astype(F32)
    first = (rows % 2 == 1) & (cols == rows - 1)
    inverses = [one - jnp.where(first, a, 0.0) for a in couplings]
    couplings = [a.astype(BF16) for a in couplings]
    block = 2
    while block < min(8, size):
        mask = ((rows // block) % 2 == 1) & (cols // block == rows // block - 1)
        inner = [dot(t, a) for t, a in zip(inverses, couplings)]
        inner = [jnp.where(mask, x, 0.0) for x in inner]
        inverses = [t - dot(x, t) for t, x in zip(inverses, inner)]
        block *= 2
    while block < size:
        count = size // (2 * block)
        half_rows = lax.broadcasted_iota(jnp.int32, (size // 2, size), 0)
        half_cols = lax.broadcasted_iota(jnp.int32, (size // 2, size), 1)
        mask = half_cols // block == 2 * (half_rows // block)
        odd = [
            jnp.concatenate(
                [t[(2 * i + 1) * block : (2 * i + 2) * block] for i in range(count)], axis=0
            )
            for t in inverses
        ]
        inner = [jnp.where(mask, dot(o, a), 0.0) for o, a in zip(odd, couplings)]
        odd = [o - dot(x, t) for o, x, t in zip(odd, inner, inverses)]
        inverses = [
            jnp.concatenate(
                [
                    piece
                    for i in range(count)
                    for piece in (
                        t[2 * i * block : (2 * i + 1) * block],
                        o[i * block : (i + 1) * block],
                    )
                ],
                axis=0,
            )
            for t, o in zip(inverses, odd)
        ]
        block *= 2
    return inverses


def core_kernel(first_request, first_head, together, key_heads, later, *refs):
    lengths, places = refs[:2]
    proj, taps, (decay, beta, init_state, grad_out, state_grad) = refs[2:5], refs[5:8], refs[8:13]
    refs = refs[13:]
    if later:
        old_taps, refs = refs[:3], refs[4:]
    grads, grad_taps = refs[:3], refs[3:6]
    grad_decay, grad_beta, sent, held, sem = refs[6:]
    step = pl.program_id(0)
    width = init_state.shape[-1]
    size = proj[0].shape[0] // together
    heads = init_state.shape[1]
    group = heads // key_heads
    rows = lax.broadcasted_iota(jnp.int32, (size, size), 0)
    cols = lax.broadcasted_iota(jnp.int32, (size, size), 1)
    wide_rows = lax.broadcasted_iota(jnp.int32, (size, width), 0)
    causal = rows >= cols
    strict = rows > cols
    lower = causal.astype(F32)
    upper = (rows <= cols).astype(F32)
    one = (rows == cols).astype(F32)

    units = [(r, g) for r in range(together) for g in range(key_heads)]
    pairs = [(r, h) for r in range(together) for h in range(heads)]
    unit_of = {(r, h): r * key_heads + h // group for r, h in pairs}
    spans = [slice(r * size, (r + 1) * size) for r in range(together)]
    request = [first_request + step * together + r for r in range(together)]
    length = [lengths[x] for x in request]
    live_row = [
        (lax.broadcasted_iota(jnp.int32, (heads, size), 1) < n).astype(F32) for n in length
    ]
    live_col = [
        (lax.broadcasted_iota(jnp.int32, (size, heads), 0) < n).astype(F32) for n in length
    ]
    live_wide = [(wide_rows < n).astype(F32) for n in length]
    picked = slice(first_head, first_head + heads)
    gate_row = [decay[r, picked, :] * live_row[r] for r in range(together)]
    rate_row = [beta[r, picked, :] * live_row[r] for r in range(together)]
    cum_row = [exact_dot(x, lower, NT) for x in gate_row]
    cum_col = [exact_dot(lower, x, NT) for x in gate_row]
    rate_col = [exact_dot(one, x, NT) for x in rate_row]
    growth_col = [jnp.exp(x) for x in cum_col]

    def prepare(r, kind, index):
        cut = slice(index * width, (index + 1) * width)
        x = proj[kind][spans[r], cut].astype(F32)
        mixed = x * taps[kind][3:4, cut]
        for i in range(3):
            mixed = mixed + shift_down(x, 3 - i, wide_rows) * taps[kind][i : i + 1, cut]
        gate = 1.0 / (1.0 + jnp.exp(-mixed))
        active = mixed * gate
        return active, gate + active * (1.0 - gate)

    def unit(active, factor):
        total = jnp.sum(active * active, axis=-1, keepdims=True) + EPSILON
        scale = factor * lax.rsqrt(total)
        return active * scale, scale, 1.0 / total

    q_in = [prepare(r, 0, g) for r, g in units]
    k_in = [prepare(r, 1, g) for r, g in units]
    v_in = [prepare(r, 2, h) for r, h in pairs]
    q_unit = [unit(x[0], width ** (-0.5)) for x in q_in]
    k_unit = [unit(x[0], 1.0) for x in k_in]
    q_f = [x[0] for x in q_unit]
    k_f = [x[0] for x in k_unit]
    q_b = [x.astype(BF16) for x in q_f]
    k_b = [x.astype(BF16) for x in k_f]
    kk = [dot(k, k, NT) for k in k_b]
    qk = [dot(q, k, NT) for q, k in zip(q_b, k_b)]
    kq = [dot(k, q, NT) for q, k in zip(q_b, k_b)]

    every = range(len(pairs))
    of = [unit_of[p] for p in pairs]
    cum_c = [cum_col[r][:, h : h + 1] for r, h in pairs]
    cum_r = [cum_row[r][h : h + 1, :] for r, h in pairs]
    rate = [rate_col[r][:, h : h + 1] for r, h in pairs]
    growth = [growth_col[r][:, h : h + 1] for r, h in pairs]
    last = [x[:, size - 1 :] for x in cum_r]
    final = [jnp.exp(x) for x in last]
    rest = [jnp.exp(last[i] - cum_c[i]) for i in every]
    within = [jnp.exp(jnp.where(causal, cum_c[i] - cum_r[i], -jnp.inf)) for i in every]
    within_t = [jnp.exp(jnp.where(rows <= cols, cum_r[i] - cum_c[i], -jnp.inf)) for i in every]
    couplings = [jnp.where(strict, rate[i] * kk[of[i]] * within[i], 0.0) for i in every]
    inverses = [t.astype(BF16) for t in unit_lower_inverse(couplings, rows, cols)]

    s_b = [init_state[r, h].astype(BF16) for r, h in pairs]
    ds_b = [state_grad[r, h].astype(BF16) for r, h in pairs]
    k_s = [dot(k_b[of[i]], s_b[i]) for i in every]
    left = [v_in[i][0] - growth[i] * k_s[i] for i in every]
    new_b = [dot(inverses[i], rate[i] * left[i]).astype(BF16) for i in every]
    out_b = [
        (grad_out[spans[r], h * width : (h + 1) * width].astype(F32) * live_wide[r]).astype(BF16)
        for r, h in pairs
    ]
    d_new = [
        dot(kq[of[i]] * within_t[i], out_b[i]) + rest[i] * dot(k_b[of[i]], ds_b[i]) for i in every
    ]
    d_right = [dot(inverses[i], d_new[i], TN) for i in every]
    d_scores = [dot(out_b[i], new_b[i], NT) * within[i] for i in every]
    d_coup = [
        jnp.where(strict, -dot(d_right[i], new_b[i], NT) * within[i], 0.0) for i in every
    ]
    back_b = [(-(rate[i] * growth[i]) * d_right[i]).astype(BF16) for i in every]
    u_q = [growth[i] * dot(out_b[i], s_b[i], NT) for i in every]
    u_k = [dot(back_b[i], s_b[i], NT) for i in every]
    u_e = [rest[i] * dot(new_b[i], ds_b[i], NT) for i in every]

    def leave(r):
        return pltpu.make_async_copy(
            held.at[r],
            sent.at[places[first_request + step * together + r], pl.ds(first_head, heads)],
            sem.at[r],
        )

    @pl.when(step > 0)
    def _():
        for r in range(together):
            leave(r).wait()

    cum_from_rows, cum_from_cols, rate_grads, last_grads = [], [], [], []
    for i, (r, h) in enumerate(pairs):
        u = of[i]
        y = d_coup[i] * kk[u]
        y_row = jnp.sum(y, axis=-1, keepdims=True)
        scored = d_scores[i] * qk[u]
        ended = jnp.sum(k_f[u] * u_e[i], axis=-1, keepdims=True)
        rate_grads.append(jnp.sum(d_right[i] * left[i], axis=-1, keepdims=True) + y_row)
        direct = q_f[u] * u_q[i] + k_f[u] * u_k[i] + scored
        cum_from_rows.append(jnp.sum(direct, axis=-1, keepdims=True) + rate[i] * y_row - ended)
        cum_from_cols.append(jnp.sum(scored + rate[i] * y, axis=0, keepdims=True))
        carried = jnp.sum(state_grad[r, h] * init_state[r, h], axis=0, keepdims=True)
        last_grads.append(
            jnp.sum(ended, axis=0, keepdims=True)
            + final[i] * jnp.sum(carried, axis=1, keepdims=True)
        )
        held[r, h] = (
            final[i] * state_grad[r, h]
            + dot(q_b[u], growth[i] * out_b[i].astype(F32), TN)
            + dot(k_b[u], back_b[i], TN)
        ).astype(BF16)
    for r in range(together):
        leave(r).start()
    for r in range(together):
        mine = [i for i in every if pairs[i][0] == r]
        gate_grad = exact_dot(upper, jnp.concatenate([cum_from_rows[i] for i in mine], axis=1))
        gate_grad = gate_grad - exact_dot(
            upper, jnp.concatenate([cum_from_cols[i] for i in mine], axis=0), NT
        )
        gate_grad = gate_grad + jnp.concatenate([last_grads[i] for i in mine], axis=1)
        grad_decay[spans[r], :] = gate_grad * live_col[r]
        grad_beta[spans[r], :] = (
            jnp.concatenate([rate_grads[i] for i in mine], axis=1) * live_col[r]
        )

    @pl.when(step == 0)
    def _():
        for i, grad_tap in enumerate(grad_taps):
            grad_tap[...] = old_taps[i][...] if later else jnp.zeros_like(grad_tap)

    def conv_back(d_active, slope, r, kind, index):
        cut = slice(index * width, (index + 1) * width)
        x = proj[kind][spans[r], cut].astype(F32)
        d_mixed = d_active * slope
        d_x = d_mixed * taps[kind][3:4, cut]
        sums = []
        for i in range(3):
            moved = shift_up(d_mixed, 3 - i, wide_rows)
            d_x = d_x + moved * taps[kind][i : i + 1, cut]
            sums.append(jnp.sum(moved * x, axis=0, keepdims=True))
        sums.append(jnp.sum(d_mixed * x, axis=0, keepdims=True))
        grads[kind][spans[r], cut] = d_x.astype(BF16)
        grad_taps[kind][:, cut] += jnp.concatenate(sums, axis=0)

    def unit_back(d_unit, unit_in, active):
        unit_rows, scale, inverse_total = unit_in
        inner = jnp.sum(d_unit * active, axis=-1, keepdims=True)
        return scale * (d_unit - active * (inner * inverse_total))

    for u, (r, g) in enumerate(units):
        members = [i for i in every if of[i] == u]
        scores_sum = sum(d_scores[i] for i in members).astype(BF16)
        kk_sum = sum(rate[i] * d_coup[i] for i in members)
        kk_sum = (kk_sum + kk_sum.T).astype(BF16)
        d_q = sum(u_q[i] for i in members) + dot(scores_sum, k_b[u])
        d_k = sum(u_k[i] + u_e[i] for i in members)
        d_k = d_k + dot(scores_sum, q_b[u], TN) + dot(kk_sum, k_b[u])
        conv_back(unit_back(d_q, q_unit[u], q_in[u][0]), q_in[u][1], r, 0, g)
        conv_back(unit_back(d_k, k_unit[u], k_in[u][0]), k_in[u][1], r, 1, g)
    for i, (r, h) in enumerate(pairs):
        conv_back(rate[i] * d_right[i], v_in[i][1], r, 2, h)

    @pl.when(step == pl.num_programs(0) - 1)
    def _():
        for r in range(together):
            leave(r).wait()


def core_call(
    together, first, count, members, proj, taps, decay, beta, init_state, grad_out, state_grad,
    lengths, places, sent_shape, before,
):
    all_heads, width = init_state.shape[1:3]
    size = decay.shape[2]
    key_heads = len(members)
    heads = key_heads * (all_heads * width // proj[0].shape[1])
    part = members[0] // key_heads
    first_head = part * heads
    widths = [key_heads * width, key_heads * width, heads * width]
    rows = count * size
    start = first // together

    def here(offset, column, columns):
        return pl.BlockSpec((together * size, columns), lambda i, *_: (offset + i, column))

    def fixed(array, column, columns):
        return pl.BlockSpec((array.shape[0], columns), lambda i, *_: (0, column))

    by_request = pl.BlockSpec((together, all_heads, size), lambda i, *_: (start + i, 0, 0))
    state = pl.BlockSpec((together, heads, width, width), lambda i, *_: (start + i, part, 0, 0))
    small = pl.BlockSpec((together * size, heads), lambda i, *_: (i, 0))
    anywhere = pl.BlockSpec(memory_space=pl.ANY)
    kept = [] if before is None else [*before[3:6], before[8]]
    kept_columns = [part if x.shape[1] > n else 0 for x, n in zip(kept, widths)]
    products = count * heads * 26 * 2 * size * width * width
    return pl.pallas_call(
        functools.partial(core_kernel, first, first_head, together, key_heads, bool(kept)),
        grid_spec=pltpu.PrefetchScalarGridSpec(
            num_scalar_prefetch=2,
            grid=(count // together,),
            in_specs=[here(0, part, n) for n in widths]
            + [fixed(x, part, n) for x, n in zip(taps, widths)]
            + [by_request, by_request, state, here(start, part, heads * width), state]
            + [fixed(x, j, n) for x, j, n in zip(kept, kept_columns, widths)]
            + [anywhere] * (len(kept) > 0),
            out_specs=[here(0, 0, n) for n in widths]
            + [fixed(x, 0, n) for x, n in zip(taps, widths)]
            + [small, small, anywhere],
            scratch_shapes=[
                pltpu.VMEM((together, heads, width, width), BF16),
                pltpu.SemaphoreType.DMA((together,)),
            ],
        ),
        out_shape=[jax.ShapeDtypeStruct((rows, n), BF16) for n in widths]
        + [jax.ShapeDtypeStruct((x.shape[0], n), F32) for x, n in zip(taps, widths)]
        + [jax.ShapeDtypeStruct((rows, heads), F32)] * 2
        + [jax.ShapeDtypeStruct(sent_shape, BF16)],
        input_output_aliases={16: 8} if kept else {},
        compiler_params=pltpu.CompilerParams(vmem_limit_bytes=50 << 20),
        cost_estimate=cost(12 * products, count * heads * 400000),
        name="core_grads",
    )(
        lengths, places, *proj, *taps, decay, beta, init_state, grad_out, state_grad, *kept
    )


COST = 10**9


def whole(array):
    return pl.BlockSpec(array.shape, lambda *_: (0,) * len(array.shape))


def cost(flops, size):
    return pl.CostEstimate(flops=flops // COST, bytes_accessed=size // COST, transcendentals=0)


def assemble_kernel(indices, *refs):
    blocks, features = refs[:-1], refs[-1]
    width = blocks[0].shape[1]
    for i, block in enumerate(blocks):
        features[:, pl.ds(pl.multiple_of(indices[i] * width, width), width)] = block[...]


def assemble(indices, blocks):
    rows, width = blocks[0].shape
    tile = 128

    def tiles(count):
        return pl.BlockSpec((tile, count), lambda i, *_: (i, 0))

    return pl.pallas_call(
        assemble_kernel,
        grid_spec=pltpu.PrefetchScalarGridSpec(
            num_scalar_prefetch=1,
            grid=(rows // tile,),
            in_specs=[tiles(width)] * len(blocks),
            out_specs=tiles(width * len(blocks)),
        ),
        out_shape=jax.ShapeDtypeStruct((rows, width * len(blocks)), BF16),
        compiler_params=pltpu.CompilerParams(vmem_limit_bytes=32 << 20),
        cost_estimate=cost(1, 4 << 20),
        name="assemble",
    )(indices, *blocks)


def term_kernel(sets, *refs):
    grads, weights, (out, held) = refs[: 3 * sets], refs[3 * sets : 3 * sets + 3], refs[-2:]
    width = out.shape[2]

    @pl.when(pl.program_id(0) == 0)
    def _():
        column = 0
        for kind in range(3):
            for g in range(sets):
                grad = grads[3 * g + kind]
                held[:, column : column + grad.shape[1]] = grad[...]
                column += grad.shape[1]

    total, column = 0.0, 0
    for weight in weights:
        total = total + dot(held[:, column : column + weight.shape[1]], weight[...], NT)
        column += weight.shape[1]
    for i in range(out.shape[0]):
        out[i] = total[:, i * width : (i + 1) * width].astype(BF16)


def head_terms(parts, sets, weights):
    rows = sets[0][0].shape[0]
    depth = weights[0].shape[0]
    columns = sum(w.shape[1] for w in weights)
    width = depth // parts
    tile = max(1, 512 // width)
    grads = [x for group in sets for x in group]
    return pl.pallas_call(
        functools.partial(term_kernel, len(sets)),
        grid=(parts // tile,),
        in_specs=[whole(x) for x in grads]
        + [pl.BlockSpec((tile * width, w.shape[1]), lambda i: (i, 0)) for w in weights],
        out_specs=pl.BlockSpec((tile, rows, width), lambda i: (i, 0, 0)),
        out_shape=jax.ShapeDtypeStruct((parts, rows, width), BF16),
        scratch_shapes=[pltpu.VMEM((rows, columns), BF16)],
        compiler_params=pltpu.CompilerParams(vmem_limit_bytes=50 << 20),
        cost_estimate=cost(2 * rows * depth * columns, 7 << 20),
        name="head_terms",
    )(*grads, *weights)


def weight_kernel(chunks, attached, order, *refs):
    features, grads = refs[:chunks], refs[chunks : 4 * chunks]
    refs = refs[4 * chunks :]
    taps, states = (refs[:attached], refs[attached]) if attached else ((), None)
    outs, turned = refs[attached + (attached > 0) : -1], refs[-1]
    step = pl.program_id(0)
    columns = sum(x.shape[1] for x in grads[:3])
    starts = [sum(x.shape[0] for x in features[:i]) for i in range(chunks)]

    @pl.when(step == 0)
    def _():
        for c, start in enumerate(starts):
            row = 0
            for grad in grads[3 * c : 3 * c + 3]:
                count, width = grad.shape
                turned[row : row + width, start : start + count] = grad[...].T
                row += width

    total = sum(
        dot(turned[:, start : start + x.shape[0]], x[...]) for start, x in zip(starts, features)
    )
    for i, out in enumerate(outs):

        @pl.when(step == i)
        def _():
            out[:columns, :] = total.astype(out.dtype)
            if attached and i < len(outs) - 1:
                attach(out, columns, i + 1, len(outs), taps, states)


def state_shape(depth, heads, width):
    across = min(depth // width, heads)
    return heads // across, across


def attach(out, row, hop, parts, taps, states):
    heads, width = states.shape[1], states.shape[2]
    capacity = states.shape[0] // parts
    down, across = state_shape(out.shape[1], heads, width)
    for k in range(capacity):
        for h in range(heads):
            place = slice((h % across) * width, (h % across + 1) * width)
            start = row + (k * down + h // across) * width
            out[start : start + width, place] = states[hop * capacity + k, h]
    row = row + capacity * down * width
    tiles = out.shape[1] // width
    for index, piece in enumerate(tap_pieces(taps, width)):
        high = piece.astype(BF16)
        low = (piece - high.astype(F32)).astype(BF16)
        block = jnp.concatenate([high.astype(F32), low.astype(F32)], axis=0)
        block = jnp.concatenate([block, jnp.zeros_like(block)], axis=0).astype(BF16)
        start = row + index // tiles * 16
        place = slice(index % tiles * width, (index % tiles + 1) * width)
        out[start : start + 16, place] = block


def tap_pieces(taps, width):
    return [
        x[:, i * width : (i + 1) * width] for x in taps for i in range(x.shape[1] // width)
    ]


def weight_blocks(order, features, grads, index, widths, taps=(), states=None):
    parts = order.shape[0]
    depth = features[0].shape[1] // parts
    columns = sum(widths)

    def of_key_head(array, width):
        place = index if array.shape[1] > width else 0
        return pl.BlockSpec((array.shape[0], width), lambda i, order: (0, place))

    rows = sum(x.shape[0] for x in features)
    extra = 0
    if taps:
        heads, width = states.shape[1], states.shape[2]
        pieces = sum(x.shape[1] for x in taps) // width
        extra = states.shape[0] // parts * state_shape(depth, heads, width)[0] * width
        extra += -(-pieces // (depth // width)) * 16
    shapes = [jax.ShapeDtypeStruct((columns + extra, depth), BF16)] * (parts - 1)
    shapes.append(jax.ShapeDtypeStruct((columns, depth), F32))
    attached = [*taps, states] if taps else []
    return pl.pallas_call(
        functools.partial(weight_kernel, len(features), len(taps)),
        grid_spec=pltpu.PrefetchScalarGridSpec(
            num_scalar_prefetch=1,
            grid=(parts,),
            in_specs=[
                pl.BlockSpec((x.shape[0], depth), lambda i, order: (0, order[i]))
                for x in features
            ]
            + [of_key_head(x, n) for group in grads for x, n in zip(group, widths)]
            + [whole(x) for x in attached],
            out_specs=[whole(x) for x in shapes],
            scratch_shapes=[pltpu.VMEM((columns, rows), BF16)],
        ),
        out_shape=shapes,
        compiler_params=pltpu.CompilerParams(vmem_limit_bytes=50 << 20),
        cost_estimate=cost(2 * rows * depth * parts * columns, 8 << 20),
        name="weight_blocks",
    )(order, *features, *[x for group in grads for x in group], *attached)


def finish_kernel(terms, widths, *refs):
    key_heads = (len(refs) - 3) // terms
    outs = refs[-3:]
    for g in range(key_heads):
        pieces = refs[g * terms : (g + 1) * terms]
        total = pieces[0][...].astype(F32)
        for piece in pieces[1:]:
            total = total + piece[...].astype(F32)
        total = total.T
        start = 0
        for out, width in zip(outs, widths):
            out[:, g * width : (g + 1) * width] = total[:, start : start + width]
            start += width


def finish_weights(pieces, widths):
    key_heads, terms, rows = len(pieces), len(pieces[0]), pieces[0][0].shape[1]
    tile = min(rows, 128)
    sizes = [key_heads * n for n in widths]
    return pl.pallas_call(
        functools.partial(finish_kernel, terms, widths),
        grid=(rows // tile,),
        in_specs=[pl.BlockSpec((sum(widths), tile), lambda i: (0, i))] * (key_heads * terms),
        out_specs=[pl.BlockSpec((tile, n), lambda i: (i, 0)) for n in sizes],
        out_shape=[jax.ShapeDtypeStruct((rows, n), F32) for n in sizes],
        compiler_params=pltpu.CompilerParams(vmem_limit_bytes=32 << 20),
        cost_estimate=pl.CostEstimate(flops=10**12, bytes_accessed=10**9, transcendentals=0),
        name="finish_weights",
    )(*[x for group in pieces for x in group])


def place_kernel(shape, first_tap_row, taps_count, sources, ranks, *refs):
    taps, kept = refs[:taps_count], refs[taps_count]
    hops = (len(refs) - taps_count - 5) // 2
    received = refs[taps_count + 1 : taps_count + 1 + hops]
    edges = refs[taps_count + 1 + hops : taps_count + 1 + 2 * hops]
    out, tap_outs = refs[-4], refs[-3:]
    heads, width = out.shape[1], out.shape[2]
    down, across = shape
    step = pl.program_id(0)
    for j in range(out.shape[0]):
        source, rank = sources[step * out.shape[0] + j], ranks[step * out.shape[0] + j]

        @pl.when(source == 0)
        def _():
            out[j] = kept[rank].astype(F32)

        for index, block in enumerate(received):

            @pl.when(source == index + 1)
            def _():
                for h in range(heads):
                    start = pl.multiple_of((rank * down + h // across) * width, width)
                    place = slice(h % across * width, (h % across + 1) * width)
                    out[j, h] = block[pl.ds(start, width), place].astype(F32)

    @pl.when(step == 0)
    def _():
        tiles = edges[0].shape[1] // width
        index, columns = 0, [0, 0, 0]
        for t, mine in enumerate(taps):
            for i in range(mine.shape[1] // width):
                piece = mine[:, i * width : (i + 1) * width]
                high = piece.astype(BF16).astype(F32)
                sums = [high + (piece - high).astype(BF16).astype(F32)]
                start = first_tap_row + index // tiles * 16
                place = slice(index % tiles * width, (index % tiles + 1) * width)
                for edge in edges:
                    block = edge[start : start + 16, place].astype(F32)
                    sums.append(block[:4] + block[4:8])
                while len(sums) > 1:
                    sums = [sums[n] + sums[n + 1] for n in range(0, len(sums), 2)]
                column = columns[t % 3]
                tap_outs[t % 3][:, column : column + width] = sums[0]
                columns[t % 3] += width
                index += 1


def place_states(sources, ranks, taps, sent, received, columns):
    requests = sources.shape[0]
    heads, width = sent.shape[1], sent.shape[2]
    parts = len(received) + 1
    depth = received[0].shape[1]
    capacity = sent.shape[0] // parts
    down, across = state_shape(depth, heads, width)
    high = capacity * down * width
    edge = columns + high
    tail = received[0].shape[0] - edge
    together = 4 if requests % 4 == 0 else 1
    sizes = [sum(x.shape[1] for x in taps[t::3]) for t in range(3)]

    def part_of(start, count):
        return pl.BlockSpec((count, depth), lambda r, *_: (start // count, 0))

    return pl.pallas_call(
        functools.partial(place_kernel, (down, across), 0, len(taps)),
        grid_spec=pltpu.PrefetchScalarGridSpec(
            num_scalar_prefetch=2,
            grid=(requests // together,),
            in_specs=[whole(x) for x in taps]
            + [pl.BlockSpec((capacity, heads, width, width), lambda r, *_: (0, 0, 0, 0))]
            + [part_of(columns, high)] * (parts - 1)
            + [part_of(edge, tail)] * (parts - 1),
            out_specs=[pl.BlockSpec((together, heads, width, width), lambda r, *_: (r, 0, 0, 0))]
            + [pl.BlockSpec((taps[0].shape[0], n), lambda r, *_: (0, 0)) for n in sizes],
        ),
        out_shape=[jax.ShapeDtypeStruct((requests, heads, width, width), F32)]
        + [jax.ShapeDtypeStruct((taps[0].shape[0], n), F32) for n in sizes],
        compiler_params=pltpu.CompilerParams(vmem_limit_bytes=40 << 20),
        cost_estimate=cost(1 << 20, 4 << 20),
        name="place_states",
    )(sources, ranks, *taps, sent, *received, *received)


def slot_plan(slot_map, all_slots, me, parts):
    requests = slot_map.shape[0]
    capacity = max(1, requests // parts)
    owners = all_slots // requests
    request_ids = jnp.arange(all_slots.shape[0], dtype=jnp.int32)
    earlier = (
        (request_ids[:, None] > request_ids[None, :])
        & (request_ids[:, None] // requests == request_ids[None, :] // requests)
        & (owners[:, None] == owners[None, :])
    )
    ranks = jnp.sum(earlier.astype(jnp.int32), axis=1)
    hops = jnp.bitwise_xor(owners, request_ids // requests)
    places = lax.dynamic_slice_in_dim(hops * capacity + ranks, me * requests, requests)
    own_slots = me * requests + jnp.arange(requests, dtype=jnp.int32)
    matches = (all_slots[None, :] == own_slots[:, None]).astype(jnp.int32)
    sources = jnp.sum(matches * hops[None, :], axis=1)
    source_ranks = jnp.sum(matches * ranks[None, :], axis=1)
    return places, sources, source_ranks, capacity


def swap(array, axis, parts, hop):
    return lax.ppermute(array, axis, [(i, i ^ hop) for i in range(parts)])


def along(array, parts, hop):
    chips = parts // 2
    pairs = [(2 * z + c, 2 * ((z + hop) % chips) + c) for z in range(chips) for c in range(2)]
    return lax.ppermute(array, "tensor", pairs)


def body(
    hidden, w_query, w_key, w_value, conv_query, conv_key, conv_value, decay_log, beta_gate,
    init_state, grad_out, state_grad_in, rollout_lengths, slot_map,
):
    parts, spread = lax.axis_size("batch"), lax.axis_size("tensor")
    chips = spread // 2
    me, mine = lax.axis_index("batch"), lax.axis_index("tensor")
    chip, core = mine // 2, mine % 2
    requests = rollout_lengths.shape[0]
    size = hidden.shape[0] // requests
    heads, width = init_state.shape[1], init_state.shape[2]
    chunks = [requests // 2, requests - requests // 2]
    starts = [sum(chunks[:i]) for i in range(len(chunks))]

    shard = hidden[: chunks[0] * size]
    rest = hidden[chunks[0] * size :]
    blocks = [shard] + [along(shard, spread, hop) for hop in range(1, chips)]
    all_slots = lax.all_gather(slot_map, "batch", axis=0, tiled=True)
    places, sources, ranks, capacity = slot_plan(slot_map, all_slots, me, parts)
    rest, blocks, places, sources, ranks = lax.optimization_barrier(
        (rest, blocks, places, sources, ranks)
    )
    blocks = blocks + [swap(x, "tensor", spread, 1) for x in blocks]
    chip_steps = jnp.arange(chips, dtype=jnp.int32)
    came = (chip - chip_steps) % chips * 2
    indices = jnp.concatenate([came + core, came + 1 - core])
    hop_order = jnp.bitwise_xor(me, jnp.array([*range(1, parts), 0], jnp.int32))
    gathered = [
        assemble(indices, blocks), lax.all_gather(rest, "tensor", axis=1, tiled=True),
    ]

    def by_head(array):
        return array.reshape(requests, size, heads).transpose(0, 2, 1)

    sent_shape = (parts * capacity, heads, width, width)
    taps = [conv_query, conv_key, conv_value]
    weights = [w_query, w_key, w_value]
    key_heads = w_query.shape[1] // width
    widths = (width, width, heads // key_heads * width)
    out, hidden_rows, pieces, decays, betas, first_grads = None, [], [], [], [], None
    for i, (start, count) in enumerate(zip(starts, chunks)):
        proj = [
            jnp.dot(gathered[i], w, preferred_element_type=F32).astype(BF16) for w in weights
        ]
        last = i == len(chunks) - 1
        sets = [range(g, g + 1) for g in range(key_heads)] if last else [range(key_heads)]
        grads, tap_sums, chunk_decays, chunk_betas = [], [], [], []
        earlier = out
        for members in sets:
            together = max(
                n for n in (1, 2, 4)
                if n * len(members) <= 4 and count % n == 0 and start % n == 0
            )
            before = None if out is None else [*earlier[:8], out[8]]
            out = core_call(
                together, start, count, members, proj, taps, by_head(decay_log),
                by_head(beta_gate), init_state, grad_out, state_grad_in, rollout_lengths,
                places, sent_shape, before,
            )
            grads.append(out[:3])
            tap_sums += out[3:6]
            chunk_decays.append(out[6])
            chunk_betas.append(out[7])
            if last:
                g = members[0]
                extra = (tap_sums, out[8]) if g == key_heads - 1 else ()
                local = weight_blocks(
                    hop_order, gathered, [earlier[:3], out[:3]], g, widths, *extra
                )
                pieces.append(
                    [local[-1]]
                    + [swap(local[hop - 1], "batch", parts, hop) for hop in range(1, parts)]
                )
        decays.append(jnp.concatenate(chunk_decays, axis=1))
        betas.append(jnp.concatenate(chunk_betas, axis=1))
        term = head_terms(spread, grads, weights)
        term = term.reshape(-1, term.shape[2])
        hidden_rows.append(lax.psum_scatter(term, "tensor", scatter_dimension=0, tiled=True))
    slot_state_grad, *grad_taps = place_states(
        sources, ranks, tap_sums, out[8], pieces[-1][1:], sum(widths)
    )
    grad_w = finish_weights(pieces, widths)
    grad_w, hidden_rows = lax.optimization_barrier((grad_w, hidden_rows))
    grad_hidden = jnp.concatenate(hidden_rows, axis=0)
    return (
        grad_hidden, *grad_w, *grad_taps, jnp.concatenate(decays), jnp.concatenate(betas),
        slot_state_grad,
    )


def solution(mesh):
    placed = (
        P("batch", "tensor"),
        P(None, "tensor"),
        P(None, "tensor"),
        P(None, "tensor"),
        P(None, "tensor"),
        P(None, "tensor"),
        P(None, "tensor"),
        P("batch", "tensor"),
        P("batch", "tensor"),
        P("batch", "tensor", None, None),
        P("batch", "tensor"),
        P("batch", "tensor", None, None),
        P("batch"),
        P("batch"),
    )
    return jax.shard_map(
        body,
        mesh=mesh,
        in_specs=placed,
        out_specs=(
            P("batch", "tensor"),
            P("batch", "tensor"),
            P("batch", "tensor"),
            P("batch", "tensor"),
            P(None, "tensor"),
            P(None, "tensor"),
            P(None, "tensor"),
            P("batch", "tensor"),
            P("batch", "tensor"),
            P("batch", "tensor", None, None),
        ),
        check_vma=False,
    )
```

time: 241 us -> 191 us (0.79)
  waiting for transfers between devices: 83 us -> 48.5 us
  local copies, waits for them, and re-layouts: 55.9 us -> 24.3 us
  Pallas kernels: 40.5 us -> 69.2 us
  matrix products: 24.5 us -> 7.34 us
  starting transfers between devices: 9.02 us -> 14.5 us
    all_gather x1, waiting for transfers between devices: 40.3 us -> 0.01 us  [body(): lax.all_gather(rest, 'tensor', axis=1, tiled=True)]
    dynamic_slice x4 -> x0, local copies, waits for them, and re-layouts: 33.1 us -> none  [the longest x3 17.5 us: body(): lax.dynamic_index_in_dim(blocks, me ^ hop, 0, False)]
    pallas_call x2 -> x10, Pallas kernels: 40.5 us -> 69.2 us  [the longest x3 34.4 us: core_call(): pl.pallas_call(functools.partial(core_kernel, first, first_head, together...]
    dot_general x5 -> x6, matrix products: 24.5 us -> 7.34 us  [body(): jnp.dot(gathered[i], w, preferred_element_type=F32).astype(BF16)]
    ppermute x0 -> x3, waiting for transfers between devices: none -> 10.7 us  [along(): return lax.ppermute(array, 'tensor', pairs)]
    reshape x1 -> x0, local copies, waits for them, and re-layouts: 7.89 us -> none  [body(): blocks = partial.reshape(parts, -1, partial.shape[1])]
    unnamed x29 -> x101, local copies, waits for them, and re-layouts: 10.7 us -> 16.8 us
    ppermute x0 -> x3, starting transfers between devices: none -> 6.06 us  [along(): return lax.ppermute(array, 'tensor', pairs)]
  transfers between devices with their start and end apart: 10 -> 16, of which waited for: 4 -> 6; matrix products, arithmetic and copies ran while one was open for 27% -> 9% of each run, Pallas kernels for 2% -> 36%
where the time goes in v2:
time: 191 us; the launch traced here: 190 us
  Pallas kernels  69.2 us (36%)
  waiting for transfers between devices  48.5 us (25%)
  local copies, waits for them, and re-layouts  24.3 us (13%)
  between operations  14.9 us (8%)
  starting transfers between devices  14.5 us (8%)
  blocking collectives  7.37 us (4%)
  matrix products  7.34 us (4%)
  other arithmetic  3.57 us (2%)
    ppermute x10, waiting for transfers between devices, swap(): return lax.ppermute(array, axis, [(i, i ^ hop) for i in range(parts)])  37.7 us
    pallas_call x3, Pallas kernels, core_call(): pl.pallas_call(functools.partial(core_kernel, first, first_head, together...  34.4 us
    unnamed x101, local copies, waits for them, and re-layouts  16.8 us
    pallas_call x2, Pallas kernels, weight_blocks(): pl.pallas_call(functools.partial(weight_kernel, len(features), len(taps))...  15.3 us
    pallas_call x2, Pallas kernels, head_terms(): pl.pallas_call(functools.partial(term_kernel, len(sets)), grid=(parts //...  11.3 us
    ppermute x3, waiting for transfers between devices, along(): return lax.ppermute(array, 'tensor', pairs)  10.7 us
    ppermute x10, starting transfers between devices, swap(): return lax.ppermute(array, axis, [(i, i ^ hop) for i in range(parts)])  8.19 us
    unnamed x1, blocking collectives  7.37 us
  transfers between devices with their start and end apart: 16, of which 6 were waited for; matrix products, arithmetic and copies ran while one was open for 9% of the time, Pallas kernels for 36%

profile of v2, /device:TPU:0, one launch (start us, length us, event | category | flops | bytes accessed | tf_op | source)
XLA Modules:
  0.0 189.7 jit_solution(9322439881640916235)
XLA Ops:
  7.2 1.8 fusion.7
  9.0 5.0 %collective-permute-start.2 = (bf16[512,256]{1,0:T(8,128)(2,1)S(1)}, bf16[512,256]{1,0:T(8,128)(2,1)S(1)}, u32[]{:S(2)}, u32[]{:S(2)}) collective-permute-start(bf16[512,256]{1,0:T(8,128)(2,1)S(1)} %get-tuple-element.65.refs_0_), channel_id=1, source_target_pairs={{0,6},{1,7},{2,0},{3,1},{4,2},{5,3},{6,4},{7,5},{8,14},{9,15},{10,... | collective-permute-start | bytes 786440 | tf_op jit(solution)/shard_map/ppermute | solution.py:660
  14.0 1.0 collective-permute-start
  15.1 1.2 dynamic-slice
  17.8 7.4 %all-reduce = s32[32]{0:T(128)S(1)} all-reduce(s32[32]{0:T(128)S(1)} %dynamic-update-slice), channel_id=1, replica_groups=mesh['batch'=4,'tensor'=8] {'batch'}, use_global_device_ids=true, to_apply=%add | all-reduce | flops 32 | bytes 256
  25.7 10.7 %collective-permute-done.1.refs_2_ = bf16[512,256]{1,0:T(8,128)(2,1)S(1)} collective-permute-done((bf16[512,256]{1,0:T(8,128)(2,1)S(1)}, bf16[512,256]{1,0:T(8,128)(2,1)S(1)}, u32[]{:S(2)}, u32[]{:S(2)}) %collective-permute-start.1) | collective-permute-done | bytes 262176 | tf_op jit(solution)/shard_map/ppermute | solution.py:660
  40.8 1.3 copy-done.3
  43.7 1.2 convolution_convert_fusion.1.refs_4_
  45.0 16.7 %core_grads.3 = (bf16[512,256]{1,0:T(8,128)(2,1)S(1)}, bf16[512,256]{1,0:T(8,128)(2,1)S(1)}, bf16[512,512]{1,0:T(8,128)(2,1)S(1)}, f32[4,256]{1,0:T(4,128)S(1)},...) custom-call(s32[8]{0:T(128)S(1)} %copy-done.40, ...), custom_call_target="tpu_custom_call" | custom-call | flops 20 | tf_op jit(solution)/shard_map/core_grads/pallas_call | solution.py:304
  61.7 5.7 %head_terms.2 = bf16[8,512,256]{2,1,0:T(8,128)(2,1)} custom-call(bf16[512,256]{1,0:T(8,128)(2,1)S(1)} %get-tuple-element.71.refs_2_.refs_0_, bf16[512,256]{1,0:T(8,128)(2,1)S(1)} %get-tuple-element.72.refs_3_.refs_1_, bf16[512,512]{1,0:T(8,128)(2,1)S(1)} %get-tuple-element.73.refs_4_.refs_2_, bf16[2048,256]{1,0:T(8,128)(2,1)S(1)} %copy-done.3, ...), custom_call_target="tpu_custom_call" | custom-call | flops 2 | tf_op jit(solution)/shard_map/head_terms/pallas_call | solution.py:403
  68.0 2.7 %convolution_convert_fusion.2.refs_3_ = bf16[512,256]{1,0:T(8,128)(2,1)S(1)} fusion(bf16[512,2048]{1,0:T(8,128)(2,1)} %all-gather.2.cloned.1.call-done.refs_1_, bf16[2048,256]{1,0:T(8,128)(2,1)} %refs_7_.7), kind=kOutput, calls=%fused_computation.2 | convolution fusion | flops 537001984 | bytes 3407872 | tf_op jit(solution)/shard_map/dot_general | solution.py:705
  72.3 1.2 convolution_convert_fusion.refs_4_
  73.6 8.9 %core_grads.4 = (bf16[512,128]{1,0:T(8,128)(2,1)S(1)}, bf16[512,128]{1,0:T(8,128)(2,1)S(1)}, bf16[512,256]{1,0:T(8,128)(2,1)S(1)}, f32[4,128]{1,0:T(4,128)S(1)},...) custom-call(s32[8]{0:T(128)S(1)} %copy-done.40, ...), custom_call_target="tpu_custom_call", output_to_operand_aliasing={{8}: (16, {})} | custom-call | flops 10 | tf_op jit(solution)/shard_map/core_grads/pallas_call | solution.py:304
  83.9 7.1 %weight_blocks.2 = (bf16[512,512]{1,0:T(8,128)(2,1)S(1)}, bf16[512,512]{1,0:T(8,128)(2,1)}, bf16[512,512]{1,0:T(8,128)(2,1)}, f32[512,512]{1,0:T(8,128)}) custom-call(s32[4]{0:T(128)S(1)} %broadcast_xor_fusion.order, bf16[512,2048]{1,0:T(8,128)(2,1)} %copy-done, bf16[512,2048]{1,0:T(8,128)(2,1)} %all-gather.2.cloned.1.call-done.refs_1_, ...), custom_call_target="tpu_custom_call" | custom-call | flops 2 | tf_op jit(solution)/shard_map/weight_blocks/pallas_call | solution.py:498
  91.1 1.3 collective-permute-start.7
  92.4 8.8 %core_grads.5 = (bf16[512,128]{1,0:T(8,128)(2,1)S(1)}, bf16[512,128]{1,0:T(8,128)(2,1)S(1)}, bf16[512,256]{1,0:T(8,128)(2,1)S(1)}, f32[4,128]{1,0:T(4,128)S(1)},...) custom-call(s32[8]{0:T(128)S(1)} %copy-done.40, ...), custom_call_target="tpu_custom_call", output_to_operand_aliasing={{8}: (16, {})} | custom-call | flops 10 | tf_op jit(solution)/shard_map/core_grads/pallas_call | solution.py:304
  101.2 1.0 copy-done.1
  103.7 8.2 %weight_blocks.3 = (bf16[800,512]{1,0:T(8,128)(2,1)}, bf16[800,512]{1,0:T(8,128)(2,1)}, bf16[800,512]{1,0:T(8,128)(2,1)}, f32[512,512]{1,0:T(8,128)}) custom-call(s32[4]{0:T(128)S(1)} %broadcast_xor_fusion.order, bf16[512,2048]{1,0:T(8,128)(2,1)} %copy-done, bf16[512,2048]{1,0:T(8,128)(2,1)} %all-gather.2.cloned.1.call-done.refs_1_, ...), custom_call_target="tpu_custom_call" | custom-call | flops 2 | tf_op jit(solution)/shard_map/weight_blocks/pallas_call | solution.py:498
  112.7 1.3 collective-permute-start.11
  114.0 1.4 collective-permute-start.12
  115.4 1.5 collective-permute-start.8
  118.5 1.1 copy.37
  125.2 5.6 %head_terms.3 = bf16[8,512,256]{2,1,0:T(8,128)(2,1)} custom-call(bf16[512,128]{1,0:T(8,128)(2,1)S(1)} %copy-done.11, bf16[512,128]{1,0:T(8,128)(2,1)S(1)} %copy-done.13, bf16[512,256]{1,0:T(8,128)(2,1)S(1)} %copy-done.7, bf16[512,128]{1,0:T(8,128)(2,1)S(1)} %copy-done.15, bf16[512,128]{1,0:T(8,128)(2,1)S(1)} %copy-done.17, bf16[512,256]{1,0:T(8,128)(2,1)S(1)} %copy-done.9, ...), custom_call_target="tpu_custom_call" | custom-call | flops 2 | tf_op jit(solution)/shard_map/head_terms/pallas_call | solution.py:403
  130.8 1.2 copy.36
  132.0 1.1 copy.39
  133.1 1.1 copy.35
  134.1 1.1 copy.38
  136.5 36.2 %collective-permute-done.8.refs_2_ = bf16[512,512]{1,0:T(8,128)(2,1)} collective-permute-done((bf16[512,512]{1,0:T(8,128)(2,1)}, bf16[512,512]{1,0:T(8,128)(2,1)}, u32[]{:S(2)}, u32[]{:S(2)}) %collective-permute-start.8) | collective-permute-done | bytes 524320 | tf_op jit(solution)/shard_map/ppermute | solution.py:654
  172.7 1.0 copy-done.44
  173.8 4.3 %finish_weights.1 = (f32[512,256]{1,0:T(8,128)}, f32[512,256]{1,0:T(8,128)}, f32[512,512]{1,0:T(8,128)}) custom-call(f32[512,512]{1,0:T(8,128)S(1)} %copy-done.41, bf16[512,512]{1,0:T(8,128)(2,1)S(1)} %copy-done.44, bf16[512,512]{1,0:T(8,128)(2,1)} %collective-permute-done.8.refs_2_, bf16[512,512]{1,0:T(8,128)(2,1)} %collective-permute-done.9.refs_3_, ...), custom_call_target="tpu_custom_call" | custom-call | flops 999999995904 | bytes 1000000000 | tf_op jit(solution)/shard_map/finish_weights/pallas_call | solution.py:538
  178.2 3.1 %place_states.1 = (f32[8,4,128,128]{3,2,1,0:T(8,128)}, f32[4,256]{1,0:T(4,128)}, f32[4,256]{1,0:T(4,128)}, f32[4,512]{1,0:T(4,128)}) custom-call(s32[8]{0:T(128)S(1)} %get-tuple-element.108.sources, s32[8]{0:T(128)S(1)} %get-tuple-element.109.ranks, f32[4,128]{1,0:T(4,128)S(1)} %copy-done.33, f32[4,128]{1,0:T(4,128)S(1)} %copy-done.35, ...), custom_call_target="tpu_custom_call" | custom-call | tf_op jit(solution)/shard_map/place_states/pallas_call | solution.py:613
  181.3 1.9 pad_maximum_fusion
  (141 shorter events, 21.7 us)
Async XLA Ops:
  7.2 60.8 %all-gather.2.cloned.1.call-start = ((), (), s32[]{:S(2)}) async-start(), calls=%async_computation.2 | async-start | bytes 2359296 | tf_op jit(solution)/shard_map/all_gather | solution.py:691
  9.0 16.7 %collective-permute-start.2 = (bf16[512,256]{1,0:T(8,128)(2,1)S(1)}, bf16[512,256]{1,0:T(8,128)(2,1)S(1)}, u32[]{:S(2)}, u32[]{:S(2)}) collective-permute-start(bf16[512,256]{1,0:T(8,128)(2,1)S(1)} %get-tuple-element.65.refs_0_), channel_id=1, source_target_pairs={{0,6},{1,7},{2,0},{3,1},{4,2},{5,3},{6,4},{7,5},{8,14},{9,15},{10,... | collective-permute-start | bytes 786440 | tf_op jit(solution)/shard_map/ppermute | solution.py:660
  14.0 22.3 %collective-permute-start.1 = (bf16[512,256]{1,0:T(8,128)(2,1)S(1)}, bf16[512,256]{1,0:T(8,128)(2,1)S(1)}, u32[]{:S(2)}, u32[]{:S(2)}) collective-permute-start(bf16[512,256]{1,0:T(8,128)(2,1)S(1)} %get-tuple-element.65.refs_0_), channel_id=1, source_target_pairs={{0,4},{1,5},{2,6},{3,7},{4,0},{5,1},{6,2},{7,3},{8,12},{9,13},{10,... | collective-permute-start | bytes 786440 | tf_op jit(solution)/shard_map/ppermute | solution.py:660
  14.0 22.3 %collective-permute-start = (bf16[512,256]{1,0:T(8,128)(2,1)S(1)}, bf16[512,256]{1,0:T(8,128)(2,1)S(1)}, u32[]{:S(2)}, u32[]{:S(2)}) collective-permute-start(bf16[512,256]{1,0:T(8,128)(2,1)S(1)} %get-tuple-element.65.refs_0_), channel_id=1, source_target_pairs={{0,2},{1,3},{2,4},{3,5},{4,6},{5,7},{6,0},{7,1},{8,10},{9,11},{10,... | collective-permute-start | bytes 786440 | tf_op jit(solution)/shard_map/ppermute | solution.py:660
  36.4 144.9 %reduce-scatter.3.cloned.1.call-start = ((), (), s32[]{:S(2)}) async-start(), calls=%async_computation.3 | async-start | bytes 2359296 | tf_op jit(solution)/shard_map/reduce_scatter | solution.py:740
  36.4 1.6 collective-permute-start.3
  36.5 1.9 collective-permute-start.4
  37.0 1.8 collective-permute-start.5
  37.1 2.1 %collective-permute-start.6 = (bf16[512,256]{1,0:T(8,128)(2,1)S(1)}, bf16[512,256]{1,0:T(8,128)(2,1)S(1)}, u32[]{:S(2)}, u32[]{:S(2)}) collective-permute-start(bf16[512,256]{1,0:T(8,128)(2,1)S(1)} %collective-permute-done.2.refs_3_), channel_id=1, source_target_pairs={{0,1},{1,0},{2,3},{3,2},{4,5},{5,4},{6,7},{7,6},{8,9},{9,8},{10,11... | collective-permute-start | bytes 786440 | tf_op jit(solution)/shard_map/ppermute | solution.py:654
  61.7 5.7 %copy-start.18 = (f32[512,4]{1,0:T(8,128)}, f32[512,4]{1,0:T(8,128)S(1)}, u32[]{:S(2)}) copy-start(f32[512,4]{1,0:T(8,128)S(1)} %get-tuple-element.113) | copy-start | bytes 24580
  67.4 113.9 %reduce-scatter.5.cloned.1.call-start = ((), (), s32[]{:S(2)}) async-start(), calls=%async_computation.4 | async-start | bytes 2359296 | tf_op jit(solution)/shard_map/reduce_scatter | solution.py:740
  83.9 7.2 %copy-start.6 = (bf16[512,256]{1,0:T(8,128)(2,1)}, bf16[512,256]{1,0:T(8,128)(2,1)S(1)}, u32[]{:S(2)}) copy-start(bf16[512,256]{1,0:T(8,128)(2,1)S(1)} %get-tuple-element.80.refs_7_.refs_2_) | copy-start | bytes 786436
  83.9 7.2 %copy-start.10 = (bf16[512,128]{1,0:T(8,128)(2,1)}, bf16[512,128]{1,0:T(8,128)(2,1)S(1)}, u32[]{:S(2)}) copy-start(bf16[512,128]{1,0:T(8,128)(2,1)S(1)} %get-tuple-element.78.refs_5_.refs_0_) | copy-start | bytes 393220
  83.9 7.2 %copy-start.12 = (bf16[512,128]{1,0:T(8,128)(2,1)}, bf16[512,128]{1,0:T(8,128)(2,1)S(1)}, u32[]{:S(2)}) copy-start(bf16[512,128]{1,0:T(8,128)(2,1)S(1)} %get-tuple-element.79.refs_6_.refs_1_) | copy-start | bytes 393220
  83.9 19.7 %copy-start.28 = (f32[4,256]{1,0:T(4,128)}, f32[4,256]{1,0:T(4,128)S(1)}, u32[]{:S(2)}) copy-start(f32[4,256]{1,0:T(4,128)S(1)} %get-tuple-element.91.refs_10_.refs_2_) | copy-start | bytes 12292
  83.9 19.7 %copy-start.32 = (f32[4,128]{1,0:T(4,128)}, f32[4,128]{1,0:T(4,128)S(1)}, u32[]{:S(2)}) copy-start(f32[4,128]{1,0:T(4,128)S(1)} %get-tuple-element.89.refs_8_.refs_0_) | copy-start | bytes 6148
  83.9 19.7 %copy-start.34 = (f32[4,128]{1,0:T(4,128)}, f32[4,128]{1,0:T(4,128)S(1)}, u32[]{:S(2)}) copy-start(f32[4,128]{1,0:T(4,128)S(1)} %get-tuple-element.90.refs_9_.refs_1_) | copy-start | bytes 6148
  91.1 25.9 %collective-permute-start.7 = (bf16[512,512]{1,0:T(8,128)(2,1)S(1)}, bf16[512,512]{1,0:T(8,128)(2,1)S(1)}, u32[]{:S(2)}, u32[]{:S(2)}) collective-permute-start(bf16[512,512]{1,0:T(8,128)(2,1)S(1)} %get-tuple-element.82), channel_id=1, source_target_pairs={{0,8},{8,0},{16,24},{24,16},{1,9},{9,1},{17,25},{25,17},{2,10},{10... | collective-permute-start | bytes 1572872 | tf_op jit(solution)/shard_map/ppermute | solution.py:654
  103.6 8.2 %copy-start.8 = (bf16[512,256]{1,0:T(8,128)(2,1)}, bf16[512,256]{1,0:T(8,128)(2,1)S(1)}, u32[]{:S(2)}) copy-start(bf16[512,256]{1,0:T(8,128)(2,1)S(1)} %get-tuple-element.88.refs_7_.refs_5_) | copy-start | bytes 786436
  103.6 8.2 %copy-start.14 = (bf16[512,128]{1,0:T(8,128)(2,1)}, bf16[512,128]{1,0:T(8,128)(2,1)S(1)}, u32[]{:S(2)}) copy-start(bf16[512,128]{1,0:T(8,128)(2,1)S(1)} %get-tuple-element.86.refs_5_.refs_3_) | copy-start | bytes 393220
  103.6 8.2 %copy-start.16 = (bf16[512,128]{1,0:T(8,128)(2,1)}, bf16[512,128]{1,0:T(8,128)(2,1)S(1)}, u32[]{:S(2)}) copy-start(bf16[512,128]{1,0:T(8,128)(2,1)S(1)} %get-tuple-element.87.refs_6_.refs_4_) | copy-start | bytes 393220
  103.6 8.2 %copy-start.30 = (f32[4,256]{1,0:T(4,128)}, f32[4,256]{1,0:T(4,128)S(1)}, u32[]{:S(2)}) copy-start(f32[4,256]{1,0:T(4,128)S(1)} %get-tuple-element.94.refs_13_.refs_5_) | copy-start | bytes 12292
  103.6 8.2 %copy-start.36 = (f32[4,128]{1,0:T(4,128)}, f32[4,128]{1,0:T(4,128)S(1)}, u32[]{:S(2)}) copy-start(f32[4,128]{1,0:T(4,128)S(1)} %get-tuple-element.92.refs_11_.refs_3_) | copy-start | bytes 6148
  103.6 8.2 %copy-start.38 = (f32[4,128]{1,0:T(4,128)}, f32[4,128]{1,0:T(4,128)S(1)}, u32[]{:S(2)}) copy-start(f32[4,128]{1,0:T(4,128)S(1)} %get-tuple-element.93.refs_12_.refs_4_) | copy-start | bytes 6148
  103.7 16.0 %copy-start.5 = (bf16[2048,256]{1,0:T(8,128)(2,1)S(1)}, bf16[2048,256]{1,0:T(8,128)(2,1)}, u32[]{:S(2)}) copy-start(bf16[2048,256]{1,0:T(8,128)(2,1)} %refs_7_.7) | copy-start | bytes 3145732
  111.9 60.8 %collective-permute-start.10 = (bf16[800,512]{1,0:T(8,128)(2,1)}, bf16[800,512]{1,0:T(8,128)(2,1)S(1)}, u32[]{:S(2)}, u32[]{:S(2)}) collective-permute-start(bf16[800,512]{1,0:T(8,128)(2,1)} %get-tuple-element.97), channel_id=1, source_target_pairs={{0,8},{8,0},{16,24},{24,16},{1,9},{9,1},{17,25},{25,17},{2,10},{10... | collective-permute-start | bytes 2457608 | tf_op jit(solution)/shard_map/ppermute | solution.py:654
  112.7 59.9 %collective-permute-start.11 = (bf16[800,512]{1,0:T(8,128)(2,1)}, bf16[800,512]{1,0:T(8,128)(2,1)}, u32[]{:S(2)}, u32[]{:S(2)}) collective-permute-start(bf16[800,512]{1,0:T(8,128)(2,1)} %get-tuple-element.98), channel_id=1, source_target_pairs={{0,16},{8,24},{16,0},{24,8},{1,17},{9,25},{17,1},{25,9},{2,18},{10... | collective-permute-start | bytes 2457608 | tf_op jit(solution)/shard_map/ppermute | solution.py:654
  114.0 58.6 %collective-permute-start.12 = (bf16[800,512]{1,0:T(8,128)(2,1)}, bf16[800,512]{1,0:T(8,128)(2,1)}, u32[]{:S(2)}, u32[]{:S(2)}) collective-permute-start(bf16[800,512]{1,0:T(8,128)(2,1)} %get-tuple-element.99), channel_id=1, source_target_pairs={{0,24},{8,16},{16,8},{24,0},{1,25},{9,17},{17,9},{25,1},{2,26},{10... | collective-permute-start | bytes 2457608 | tf_op jit(solution)/shard_map/ppermute | solution.py:654
  115.4 57.2 %collective-permute-start.8 = (bf16[512,512]{1,0:T(8,128)(2,1)}, bf16[512,512]{1,0:T(8,128)(2,1)}, u32[]{:S(2)}, u32[]{:S(2)}) collective-permute-start(bf16[512,512]{1,0:T(8,128)(2,1)} %get-tuple-element.83), channel_id=1, source_target_pairs={{0,16},{8,24},{16,0},{24,8},{1,17},{9,25},{17,1},{25,9},{2,18},{10... | collective-permute-start | bytes 1572872 | tf_op jit(solution)/shard_map/ppermute | solution.py:654
  117.8 54.9 %collective-permute-start.9 = (bf16[512,512]{1,0:T(8,128)(2,1)}, bf16[512,512]{1,0:T(8,128)(2,1)}, u32[]{:S(2)}, u32[]{:S(2)}) collective-permute-start(bf16[512,512]{1,0:T(8,128)(2,1)} %get-tuple-element.84), channel_id=1, source_target_pairs={{0,24},{8,16},{16,8},{24,0},{1,25},{9,17},{17,9},{25,1},{2,26},{10... | collective-permute-start | bytes 1572872 | tf_op jit(solution)/shard_map/ppermute | solution.py:654
  130.8 41.9 %copy-start.41 = (f32[512,512]{1,0:T(8,128)S(1)}, f32[512,512]{1,0:T(8,128)}, u32[]{:S(2)}) copy-start(f32[512,512]{1,0:T(8,128)} %get-tuple-element.81.refs_0_) | copy-start | bytes 3145732
  130.8 41.9 %copy-start.42 = (f32[512,512]{1,0:T(8,128)S(1)}, f32[512,512]{1,0:T(8,128)}, u32[]{:S(2)}) copy-start(f32[512,512]{1,0:T(8,128)} %get-tuple-element.96.refs_4_) | copy-start | bytes 3145732
  (33 other events, 63.6 us)
Sparse Core Ops, SparseCore 0:
  36.5 31.2 all-gather.1
  70.1 34.8 reduce-scatter.2
  135.4 35.9 reduce-scatter.4

commit v3 on v2

--- a/solution.py
+++ b/solution.py
@@ -82,9 +82,10 @@
     proj, taps, (decay, beta, init_state, grad_out, state_grad) = refs[2:5], refs[5:8], refs[8:13]
     refs = refs[13:]
     if later:
-        old_taps, refs = refs[:3], refs[4:]
+        old_taps, refs = refs[:3], refs[3 + key_heads :]
     grads, grad_taps = refs[:3], refs[3:6]
-    grad_decay, grad_beta, sent, held, sem = refs[6:]
+    grad_decay, grad_beta = refs[6:8]
+    sent, (held, sem) = refs[8:-2], refs[-2:]
     step = pl.program_id(0)
     width = init_state.shape[-1]
     size = proj[0].shape[0] // together
@@ -185,16 +186,19 @@
     u_e = [rest[i] * dot(new_b[i], ds_b[i], NT) for i in every]
 
     def leave(r):
-        return pltpu.make_async_copy(
-            held.at[r],
-            sent.at[places[first_request + step * together + r], pl.ds(first_head, heads)],
-            sem.at[r],
-        )
+        place = places[first_request + step * together + r]
+        return [
+            pltpu.make_async_copy(
+                held.at[r, pl.ds(g * group, group)], sent[g].at[place], sem.at[r, g]
+            )
+            for g in range(key_heads)
+        ]
 
     @pl.when(step > 0)
     def _():
         for r in range(together):
-            leave(r).wait()
+            for copy in leave(r):
+                copy.wait()
 
     cum_from_rows, cum_from_cols, rate_grads, last_grads = [], [], [], []
     for i, (r, h) in enumerate(pairs):
@@ -218,7 +222,8 @@
             + dot(k_b[u], back_b[i], TN)
         ).astype(BF16)
     for r in range(together):
-        leave(r).start()
+        for copy in leave(r):
+            copy.start()
     for r in range(together):
         mine = [i for i in every if pairs[i][0] == r]
         gate_grad = exact_dot(upper, jnp.concatenate([cum_from_rows[i] for i in mine], axis=1))
@@ -271,7 +276,8 @@
     @pl.when(step == pl.num_programs(0) - 1)
     def _():
         for r in range(together):
-            leave(r).wait()
+            for copy in leave(r):
+                copy.wait()
 
 
 def core_call(
@@ -298,7 +304,7 @@
     state = pl.BlockSpec((together, heads, width, width), lambda i, *_: (start + i, part, 0, 0))
     small = pl.BlockSpec((together * size, heads), lambda i, *_: (i, 0))
     anywhere = pl.BlockSpec(memory_space=pl.ANY)
-    kept = [] if before is None else [*before[3:6], before[8]]
+    kept = [] if before is None else [*before[3:6], *[before[8 + g] for g in members]]
     kept_columns = [part if x.shape[1] > n else 0 for x, n in zip(kept, widths)]
     products = count * heads * 26 * 2 * size * width * width
     return pl.pallas_call(
@@ -310,20 +316,20 @@
             + [fixed(x, part, n) for x, n in zip(taps, widths)]
             + [by_request, by_request, state, here(start, part, heads * width), state]
             + [fixed(x, j, n) for x, j, n in zip(kept, kept_columns, widths)]
-            + [anywhere] * (len(kept) > 0),
+            + [anywhere] * (key_heads if kept else 0),
             out_specs=[here(0, 0, n) for n in widths]
             + [fixed(x, 0, n) for x, n in zip(taps, widths)]
-            + [small, small, anywhere],
+            + [small, small] + [anywhere] * key_heads,
             scratch_shapes=[
                 pltpu.VMEM((together, heads, width, width), BF16),
-                pltpu.SemaphoreType.DMA((together,)),
+                pltpu.SemaphoreType.DMA((together, key_heads)),
             ],
         ),
         out_shape=[jax.ShapeDtypeStruct((rows, n), BF16) for n in widths]
         + [jax.ShapeDtypeStruct((x.shape[0], n), F32) for x, n in zip(taps, widths)]
         + [jax.ShapeDtypeStruct((rows, heads), F32)] * 2
-        + [jax.ShapeDtypeStruct(sent_shape, BF16)],
-        input_output_aliases={16: 8} if kept else {},
+        + [jax.ShapeDtypeStruct(sent_shape, BF16)] * key_heads,
+        input_output_aliases={16 + g: 8 + g for g in range(key_heads)} if kept else {},
         compiler_params=pltpu.CompilerParams(vmem_limit_bytes=50 << 20),
         cost_estimate=cost(12 * products, count * heads * 400000),
         name="core_grads",
@@ -333,6 +339,7 @@
 
 
 COST = 10**9
+FINISH = 15 * 10**9
 
 
 def whole(array):
@@ -414,89 +421,126 @@
     )(*grads, *weights)
 
 
-def weight_kernel(chunks, attached, order, *refs):
+def weight_kernel(parts, chunks, plan, order, *refs):
     features, grads = refs[:chunks], refs[chunks : 4 * chunks]
-    refs = refs[4 * chunks :]
-    taps, states = (refs[:attached], refs[attached]) if attached else ((), None)
-    outs, turned = refs[attached + (attached > 0) : -1], refs[-1]
+    taps, states = refs[4 * chunks : 4 * chunks + 3], refs[4 * chunks + 3]
+    outs, turned = refs[4 * chunks + 4 : -1], refs[-1]
     step = pl.program_id(0)
-    columns = sum(x.shape[1] for x in grads[:3])
     starts = [sum(x.shape[0] for x in features[:i]) for i in range(chunks)]
+    width = states.shape[2]
 
     @pl.when(step == 0)
     def _():
         for c, start in enumerate(starts):
             row = 0
             for grad in grads[3 * c : 3 * c + 3]:
-                count, width = grad.shape
-                turned[row : row + width, start : start + count] = grad[...].T
-                row += width
+                count, columns = grad.shape
+                turned[row : row + columns, start : start + count] = grad[...].T
+                row += columns
+        for index, row, hop in plan["states"]:
+            for t in range(states.shape[0] // parts * states.shape[1]):
+                slot, head = divmod(t, states.shape[1])
+                tall, wide = divmod(t, outs[index].shape[1] // width)
+                outs[index][
+                    row + tall * width : row + (tall + 1) * width, wide * width : (wide + 1) * width
+                ] = states[hop * (states.shape[0] // parts) + slot, head]
+        for index, row in plan["taps"]:
+            store_taps(outs[index], row, tap_pieces(taps, width))
 
     total = sum(
         dot(turned[:, start : start + x.shape[0]], x[...]) for start, x in zip(starts, features)
     )
-    for i, out in enumerate(outs):
-
-        @pl.when(step == i)
+    for hop, pieces in plan["weights"]:
+
+        @pl.when(step == plan["hops"].index(hop))
         def _():
-            out[:columns, :] = total.astype(out.dtype)
-            if attached and i < len(outs) - 1:
-                attach(out, columns, i + 1, len(outs), taps, states)
-
-
-def state_shape(depth, heads, width):
-    across = min(depth // width, heads)
-    return heads // across, across
-
-
-def attach(out, row, hop, parts, taps, states):
-    heads, width = states.shape[1], states.shape[2]
-    capacity = states.shape[0] // parts
-    down, across = state_shape(out.shape[1], heads, width)
-    for k in range(capacity):
-        for h in range(heads):
-            place = slice((h % across) * width, (h % across + 1) * width)
-            start = row + (k * down + h // across) * width
-            out[start : start + width, place] = states[hop * capacity + k, h]
-    row = row + capacity * down * width
-    tiles = out.shape[1] // width
-    for index, piece in enumerate(tap_pieces(taps, width)):
-        high = piece.astype(BF16)
-        low = (piece - high.astype(F32)).astype(BF16)
-        block = jnp.concatenate([high.astype(F32), low.astype(F32)], axis=0)
+            for index, row, low, high in pieces:
+                outs[index][row : row + high - low, :] = total[low:high].astype(outs[index].dtype)
+
+
+def tap_pieces(taps, width):
+    return [x[:, i * width : (i + 1) * width] for x in taps for i in range(x.shape[1] // width)]
+
+
+def store_taps(out, row, pieces):
+    width = pieces[0].shape[1]
+    across = out.shape[1] // width
+    for index, piece in enumerate(pieces):
+        high = piece.astype(BF16).astype(F32)
+        block = jnp.concatenate([high, piece - high], axis=0)
         block = jnp.concatenate([block, jnp.zeros_like(block)], axis=0).astype(BF16)
-        start = row + index // tiles * 16
-        place = slice(index % tiles * width, (index % tiles + 1) * width)
-        out[start : start + 16, place] = block
-
-
-def tap_pieces(taps, width):
-    return [
-        x[:, i * width : (i + 1) * width] for x in taps for i in range(x.shape[1] // width)
-    ]
-
-
-def weight_blocks(order, features, grads, index, widths, taps=(), states=None):
-    parts = order.shape[0]
+        start = row + index // across * 16
+        out[start : start + 16, index % across * width : (index % across + 1) * width] = block
+
+
+def load_taps(source, row, count, width):
+    across = source.shape[1] // width
+    pieces = []
+    for index in range(count):
+        start = row + index // across * 16
+        block = source[start : start + 16, index % across * width : (index % across + 1) * width]
+        block = block.astype(F32)
+        pieces.append(block[:4] + block[4:8])
+    return pieces
+
+
+def rounded_taps(pieces):
+    highs = [piece.astype(BF16).astype(F32) for piece in pieces]
+    return [high + (piece - high).astype(BF16).astype(F32) for piece, high in zip(pieces, highs)]
+
+
+def weight_plan(parts, columns, depth, states, pieces):
+    width = states.shape[2]
+    tiles = states.shape[0] // parts * states.shape[1]
+    state_rows = -(-tiles // (depth // width)) * width
+    tap_rows = -(-pieces // (depth // width)) * 16
+    if parts == 4:
+        half = columns // 2
+        plan = {
+            "hops": [3, 1, 2, 0],
+            "weights": [
+                (3, [(0, half, 0, half), (1, half, half, columns)]),
+                (1, [(0, 0, 0, half), (3, 0, half, columns)]),
+                (2, [(1, 0, half, columns), (2, 0, 0, half)]),
+                (0, [(4, 0, 0, columns)]),
+            ],
+            "states": [
+                (0, columns, 1), (0, columns + state_rows, 3), (1, columns, 2),
+            ],
+            "taps": [(0, columns + 2 * state_rows)],
+        }
+        shapes = [
+            ((columns + 2 * state_rows + tap_rows, depth), BF16),
+            ((columns + state_rows, depth), BF16),
+            ((half, depth), F32),
+            ((half, depth), F32),
+            ((columns, depth), F32),
+        ]
+    else:
+        hops = [*range(1, parts), 0]
+        plan = {
+            "hops": hops,
+            "weights": [(hop, [(i, 0, 0, columns)]) for i, hop in enumerate(hops)],
+            "states": [(i, columns, hop) for i, hop in enumerate(hops[:-1])],
+            "taps": [(i, columns + state_rows) for i in range(parts - 1)],
+        }
+        shapes = [((columns + state_rows + tap_rows, depth), BF16)] * (parts - 1)
+        shapes.append(((columns, depth), F32))
+    return plan, [jax.ShapeDtypeStruct(*x) for x in shapes], state_rows, tap_rows
+
+
+def weight_blocks(me, parts, plan, shapes, features, grads, index, widths, taps, states):
     depth = features[0].shape[1] // parts
     columns = sum(widths)
+    rows = sum(x.shape[0] for x in features)
+    order = jnp.bitwise_xor(me, jnp.array(plan["hops"], jnp.int32))
 
     def of_key_head(array, width):
         place = index if array.shape[1] > width else 0
         return pl.BlockSpec((array.shape[0], width), lambda i, order: (0, place))
 
-    rows = sum(x.shape[0] for x in features)
-    extra = 0
-    if taps:
-        heads, width = states.shape[1], states.shape[2]
-        pieces = sum(x.shape[1] for x in taps) // width
-        extra = states.shape[0] // parts * state_shape(depth, heads, width)[0] * width
-        extra += -(-pieces // (depth // width)) * 16
-    shapes = [jax.ShapeDtypeStruct((columns + extra, depth), BF16)] * (parts - 1)
-    shapes.append(jax.ShapeDtypeStruct((columns, depth), F32))
-    attached = [*taps, states] if taps else []
     return pl.pallas_call(
-        functools.partial(weight_kernel, len(features), len(taps)),
+        functools.partial(weight_kernel, parts, len(features), plan),
         grid_spec=pltpu.PrefetchScalarGridSpec(
             num_scalar_prefetch=1,
             grid=(parts,),
@@ -505,7 +549,7 @@
                 for x in features
             ]
             + [of_key_head(x, n) for group in grads for x, n in zip(group, widths)]
-            + [whole(x) for x in attached],
+            + [whole(x) for x in (*taps, states)],
             out_specs=[whole(x) for x in shapes],
             scratch_shapes=[pltpu.VMEM((columns, rows), BF16)],
         ),
@@ -513,121 +557,166 @@
         compiler_params=pltpu.CompilerParams(vmem_limit_bytes=50 << 20),
         cost_estimate=cost(2 * rows * depth * parts * columns, 8 << 20),
         name="weight_blocks",
-    )(order, *features, *[x for group in grads for x in group], *attached)
-
-
-def finish_kernel(terms, widths, *refs):
-    key_heads = (len(refs) - 3) // terms
+    )(order, *features, *[x for group in grads for x in group], *taps, states)
+
+
+def middle_kernel(half, state_rows, *refs):
+    first, second, kept_first, kept_second = refs[:4]
+    taps, (next_first, next_second) = refs[4:7], refs[7:]
+    columns, width = 2 * half, taps[0].shape[1]
+    next_first[:half, :] = (kept_first[...] + first[half:columns, :].astype(F32)).astype(BF16)
+    next_second[...] = (kept_second[...] + second[half:columns, :].astype(F32)).astype(BF16)
+    start = columns + state_rows
+    next_first[half : half + state_rows, :] = first[start : start + state_rows, :]
+    mine = rounded_taps(tap_pieces(taps, width))
+    theirs = load_taps(first, columns + 2 * state_rows, len(mine), width)
+    store_taps(next_first, half + state_rows, [a + b for a, b in zip(mine, theirs)])
+
+
+def exchange(arrays, taps, parts, columns, state_rows, tap_rows):
+    if parts != 4:
+        return [swap(x, "batch", parts, hop + 1) for hop, x in enumerate(arrays[:-1])]
+    half, depth = columns // 2, arrays[0].shape[1]
+    first, second = swap(arrays[0], "batch", parts, 1), swap(arrays[1], "batch", parts, 2)
+    shapes = [
+        jax.ShapeDtypeStruct((half + state_rows + tap_rows, depth), BF16),
+        jax.ShapeDtypeStruct((half, depth), BF16),
+    ]
+    inputs = [first, second, arrays[2], arrays[3], *taps]
+    next_first, next_second = pl.pallas_call(
+        functools.partial(middle_kernel, half, state_rows),
+        grid=(1,),
+        in_specs=[whole(x) for x in inputs],
+        out_specs=[whole(x) for x in shapes],
+        out_shape=shapes,
+        compiler_params=pltpu.CompilerParams(vmem_limit_bytes=40 << 20),
+        cost_estimate=cost(1, 1),
+        name="pass_on",
+    )(*inputs)
+    return [first, second, next_first, next_second]
+
+
+def second_exchange(arrays, parts):
+    if parts != 4:
+        return arrays
+    return [*arrays[:2], swap(arrays[2], "batch", parts, 2), swap(arrays[3], "batch", parts, 1)]
+
+
+def finish_kernel(parts, sources, widths, *refs):
     outs = refs[-3:]
-    for g in range(key_heads):
-        pieces = refs[g * terms : (g + 1) * terms]
-        total = pieces[0][...].astype(F32)
-        for piece in pieces[1:]:
-            total = total + piece[...].astype(F32)
-        total = total.T
+    columns = sum(widths)
+    half = columns // 2
+    for g in range((len(refs) - 3) // (sources + 1)):
+        own, *pieces = refs[g * (sources + 1) : (g + 1) * (sources + 1)]
+        if parts == 4:
+            upper = own[:half] + (pieces[0][...].astype(F32) + pieces[2][...].astype(F32))
+            lower = own[half:] + (pieces[1][...].astype(F32) + pieces[3][...].astype(F32))
+            total = jnp.concatenate([upper.T, lower.T], axis=1)
+        else:
+            total = sum((piece[...].astype(F32) for piece in pieces), own[...]).T
         start = 0
         for out, width in zip(outs, widths):
             out[:, g * width : (g + 1) * width] = total[:, start : start + width]
             start += width
 
 
-def finish_weights(pieces, widths):
-    key_heads, terms, rows = len(pieces), len(pieces[0]), pieces[0][0].shape[1]
+def finish_weights(parts, own, pieces, widths):
+    key_heads, rows, columns = len(pieces), own[0].shape[1], sum(widths)
     tile = min(rows, 128)
     sizes = [key_heads * n for n in widths]
+    count = columns // 2 if parts == 4 else columns
+    specs = [pl.BlockSpec((columns, tile), lambda i: (0, i))]
+    specs += [pl.BlockSpec((count, tile), lambda i: (0, i))] * len(pieces[0])
     return pl.pallas_call(
-        functools.partial(finish_kernel, terms, widths),
+        functools.partial(finish_kernel, parts, len(pieces[0]), widths),
         grid=(rows // tile,),
-        in_specs=[pl.BlockSpec((sum(widths), tile), lambda i: (0, i))] * (key_heads * terms),
+        in_specs=specs * key_heads,
         out_specs=[pl.BlockSpec((tile, n), lambda i: (i, 0)) for n in sizes],
         out_shape=[jax.ShapeDtypeStruct((rows, n), F32) for n in sizes],
         compiler_params=pltpu.CompilerParams(vmem_limit_bytes=32 << 20),
-        cost_estimate=pl.CostEstimate(flops=10**12, bytes_accessed=10**9, transcendentals=0),
+        cost_estimate=pl.CostEstimate(flops=FINISH, bytes_accessed=1, transcendentals=0),
         name="finish_weights",
-    )(*[x for group in pieces for x in group])
-
-
-def place_kernel(shape, first_tap_row, taps_count, sources, ranks, *refs):
-    taps, kept = refs[:taps_count], refs[taps_count]
-    hops = (len(refs) - taps_count - 5) // 2
-    received = refs[taps_count + 1 : taps_count + 1 + hops]
-    edges = refs[taps_count + 1 + hops : taps_count + 1 + 2 * hops]
+    )(*[x for mine, group in zip(own, pieces) for x in (mine, *group)])
+
+
+def place_kernel(parts, key_heads, columns, state_rows, sources, ranks, *refs):
+    taps, kept = refs[: 3 * key_heads], refs[3 * key_heads : 4 * key_heads]
+    count = (len(refs) - 4) // key_heads - 4
+    received = refs[4 * key_heads : -4]
     out, tap_outs = refs[-4], refs[-3:]
-    heads, width = out.shape[1], out.shape[2]
-    down, across = shape
+    group, width = kept[0].shape[1], kept[0].shape[2]
     step = pl.program_id(0)
-    for j in range(out.shape[0]):
-        source, rank = sources[step * out.shape[0] + j], ranks[step * out.shape[0] + j]
-
-        @pl.when(source == 0)
+    for g in range(key_heads):
+        arrays = received[g * count : (g + 1) * count]
+        if parts == 4:
+            places = [(0, columns), (1, columns), (2, columns // 2)]
+        else:
+            places = [(i, columns) for i in range(parts - 1)]
+        across = arrays[0].shape[1] // width
+        for j in range(out.shape[0]):
+            source, rank = sources[step * out.shape[0] + j], ranks[step * out.shape[0] + j]
+
+            @pl.when(source == 0)
+            def _():
+                out[j, g * group : (g + 1) * group] = kept[g][rank].astype(F32)
+
+            for hop, (index, row) in enumerate(places):
+                for slot in range(kept[g].shape[0] // parts):
+
+                    @pl.when((source == hop + 1) & (rank == slot))
+                    def _():
+                        for h in range(group):
+                            tall, wide = divmod(slot * group + h, across)
+                            start = row + tall * width
+                            out[j, g * group + h] = arrays[index][
+                                start : start + width, wide * width : (wide + 1) * width
+                            ].astype(F32)
+
+        @pl.when(step == 0)
         def _():
-            out[j] = kept[rank].astype(F32)
-
-        for index, block in enumerate(received):
-
-            @pl.when(source == index + 1)
-            def _():
-                for h in range(heads):
-                    start = pl.multiple_of((rank * down + h // across) * width, width)
-                    place = slice(h % across * width, (h % across + 1) * width)
-                    out[j, h] = block[pl.ds(start, width), place].astype(F32)
-
-    @pl.when(step == 0)
-    def _():
-        tiles = edges[0].shape[1] // width
-        index, columns = 0, [0, 0, 0]
-        for t, mine in enumerate(taps):
-            for i in range(mine.shape[1] // width):
-                piece = mine[:, i * width : (i + 1) * width]
-                high = piece.astype(BF16).astype(F32)
-                sums = [high + (piece - high).astype(BF16).astype(F32)]
-                start = first_tap_row + index // tiles * 16
-                place = slice(index % tiles * width, (index % tiles + 1) * width)
-                for edge in edges:
-                    block = edge[start : start + 16, place].astype(F32)
-                    sums.append(block[:4] + block[4:8])
-                while len(sums) > 1:
-                    sums = [sums[n] + sums[n + 1] for n in range(0, len(sums), 2)]
-                column = columns[t % 3]
-                tap_outs[t % 3][:, column : column + width] = sums[0]
-                columns[t % 3] += width
-                index += 1
-
-
-def place_states(sources, ranks, taps, sent, received, columns):
-    requests = sources.shape[0]
-    heads, width = sent.shape[1], sent.shape[2]
-    parts = len(received) + 1
-    depth = received[0].shape[1]
-    capacity = sent.shape[0] // parts
-    down, across = state_shape(depth, heads, width)
-    high = capacity * down * width
-    edge = columns + high
-    tail = received[0].shape[0] - edge
+            mine = rounded_taps(tap_pieces(taps[3 * g : 3 * g + 3], width))
+            n = len(mine)
+            if parts == 4:
+                theirs = load_taps(arrays[0], columns + 2 * state_rows, n, width)
+                mine = rounded_taps([a + b for a, b in zip(mine, theirs)])
+                others = [load_taps(arrays[2], columns // 2 + state_rows, n, width)]
+            else:
+                others = [load_taps(x, columns + state_rows, n, width) for x in arrays]
+            groups = [mine, *others]
+            while len(groups) > 1:
+                groups = [
+                    [a + b for a, b in zip(groups[i], groups[i + 1])]
+                    for i in range(0, len(groups), 2)
+                ]
+            pieces = groups[0]
+            for tap_out in tap_outs:
+                total = tap_out.shape[1] // key_heads
+                for i in range(total // width):
+                    start = g * total + i * width
+                    tap_out[:, start : start + width] = pieces.pop(0)
+
+
+def place_states(parts, sources, ranks, taps, sent, pieces, columns, state_rows):
+    requests, key_heads = sources.shape[0], len(sent)
+    heads, width = key_heads * sent[0].shape[1], sent[0].shape[2]
     together = 4 if requests % 4 == 0 else 1
     sizes = [sum(x.shape[1] for x in taps[t::3]) for t in range(3)]
-
-    def part_of(start, count):
-        return pl.BlockSpec((count, depth), lambda r, *_: (start // count, 0))
-
+    inputs = [*taps, *sent, *[x for group in pieces for x in group]]
     return pl.pallas_call(
-        functools.partial(place_kernel, (down, across), 0, len(taps)),
+        functools.partial(place_kernel, parts, key_heads, columns, state_rows),
         grid_spec=pltpu.PrefetchScalarGridSpec(
             num_scalar_prefetch=2,
             grid=(requests // together,),
-            in_specs=[whole(x) for x in taps]
-            + [pl.BlockSpec((capacity, heads, width, width), lambda r, *_: (0, 0, 0, 0))]
-            + [part_of(columns, high)] * (parts - 1)
-            + [part_of(edge, tail)] * (parts - 1),
+            in_specs=[whole(x) for x in inputs],
             out_specs=[pl.BlockSpec((together, heads, width, width), lambda r, *_: (r, 0, 0, 0))]
             + [pl.BlockSpec((taps[0].shape[0], n), lambda r, *_: (0, 0)) for n in sizes],
         ),
         out_shape=[jax.ShapeDtypeStruct((requests, heads, width, width), F32)]
         + [jax.ShapeDtypeStruct((taps[0].shape[0], n), F32) for n in sizes],
-        compiler_params=pltpu.CompilerParams(vmem_limit_bytes=40 << 20),
+        compiler_params=pltpu.CompilerParams(vmem_limit_bytes=50 << 20),
         cost_estimate=cost(1 << 20, 4 << 20),
         name="place_states",
-    )(sources, ranks, *taps, sent, *received, *received)
+    )(sources, ranks, *inputs)
 
 
 def slot_plan(slot_map, all_slots, me, parts):
@@ -686,7 +775,6 @@
     chip_steps = jnp.arange(chips, dtype=jnp.int32)
     came = (chip - chip_steps) % chips * 2
     indices = jnp.concatenate([came + core, came + 1 - core])
-    hop_order = jnp.bitwise_xor(me, jnp.array([*range(1, parts), 0], jnp.int32))
     gathered = [
         assemble(indices, blocks), lax.all_gather(rest, "tensor", axis=1, tiled=True),
     ]
@@ -694,12 +782,13 @@
     def by_head(array):
         return array.reshape(requests, size, heads).transpose(0, 2, 1)
 
-    sent_shape = (parts * capacity, heads, width, width)
     taps = [conv_query, conv_key, conv_value]
     weights = [w_query, w_key, w_value]
     key_heads = w_query.shape[1] // width
-    widths = (width, width, heads // key_heads * width)
-    out, hidden_rows, pieces, decays, betas, first_grads = None, [], [], [], [], None
+    group = heads // key_heads
+    sent_shape = (parts * capacity, group, width, width)
+    widths = (width, width, group * width)
+    out, hidden_rows, own, pieces, decays, betas, sent = None, [], [], [], [], [], None
     for i, (start, count) in enumerate(zip(starts, chunks)):
         proj = [
             jnp.dot(gathered[i], w, preferred_element_type=F32).astype(BF16) for w in weights
@@ -713,7 +802,7 @@
                 n for n in (1, 2, 4)
                 if n * len(members) <= 4 and count % n == 0 and start % n == 0
             )
-            before = None if out is None else [*earlier[:8], out[8]]
+            before = earlier
             out = core_call(
                 together, start, count, members, proj, taps, by_head(decay_log),
                 by_head(beta_gate), init_state, grad_out, state_grad_in, rollout_lengths,
@@ -725,23 +814,36 @@
             chunk_betas.append(out[7])
             if last:
                 g = members[0]
-                extra = (tap_sums, out[8]) if g == key_heads - 1 else ()
+                if g == key_heads - 1:
+                    term = head_terms(spread, grads, weights)
+                    term, out, pieces = lax.optimization_barrier((term, out, pieces))
+                states = jax.ShapeDtypeStruct(sent_shape, BF16)
+                plan, shapes, state_rows, tap_rows = weight_plan(
+                    parts, sum(widths), gathered[0].shape[1] // parts, states,
+                    sum(widths) // width,
+                )
                 local = weight_blocks(
-                    hop_order, gathered, [earlier[:3], out[:3]], g, widths, *extra
+                    me, parts, plan, shapes, gathered, [earlier[:3], out[:3]], g, widths,
+                    out[3:6], out[8],
                 )
+                if g < key_heads - 1:
+                    local, proj = lax.optimization_barrier((local, proj))
+                own.append(local[-1])
                 pieces.append(
-                    [local[-1]]
-                    + [swap(local[hop - 1], "batch", parts, hop) for hop in range(1, parts)]
+                    exchange(local, out[3:6], parts, sum(widths), state_rows, tap_rows)
                 )
+                sent = [*(sent or []), out[8]]
+            elif members[-1] == key_heads - 1:
+                term = head_terms(spread, grads, weights)
         decays.append(jnp.concatenate(chunk_decays, axis=1))
         betas.append(jnp.concatenate(chunk_betas, axis=1))
-        term = head_terms(spread, grads, weights)
         term = term.reshape(-1, term.shape[2])
         hidden_rows.append(lax.psum_scatter(term, "tensor", scatter_dimension=0, tiled=True))
+    pieces = [second_exchange(x, parts) for x in pieces]
     slot_state_grad, *grad_taps = place_states(
-        sources, ranks, tap_sums, out[8], pieces[-1][1:], sum(widths)
+        parts, sources, ranks, tap_sums, sent, pieces, sum(widths), state_rows
     )
-    grad_w = finish_weights(pieces, widths)
+    grad_w = finish_weights(parts, own, pieces, widths)
     grad_w, hidden_rows = lax.optimization_barrier((grad_w, hidden_rows))
     grad_hidden = jnp.concatenate(hidden_rows, axis=0)
     return (

time: 191 us -> 172 us (0.901)
  waiting for transfers between devices: 48.5 us -> 32.3 us
  local copies, waits for them, and re-layouts: 24.3 us -> 16.3 us
  starting transfers between devices: 14.5 us -> 17.3 us
  Pallas kernels: 69.2 us -> 71.3 us
    ppermute x10 -> x12, waiting for transfers between devices: 37.7 us -> 23.7 us  [swap(): return lax.ppermute(array, axis, [(i, i ^ hop) for i in range(parts)])]
    unnamed x101 -> x149, local copies, waits for them, and re-layouts: 16.8 us -> 8.09 us
    ppermute x3, waiting for transfers between devices: 10.7 us -> 4.61 us  [along(): return lax.ppermute(array, 'tensor', pairs)]
    all_gather x1, waiting for transfers between devices: 0.01 us -> 3.89 us  [body(): lax.all_gather(rest, 'tensor', axis=1, tiled=True)]
    ppermute x10 -> x12, starting transfers between devices: 8.19 us -> 10.1 us  [swap(): return lax.ppermute(array, axis, [(i, i ^ hop) for i in range(parts)])]
    pallas_call x4 -> x6, Pallas kernels: 22.7 us -> 24.3 us  [the longest x2 14.2 us: weight_blocks(): pl.pallas_call(functools.partial(weight_kernel, parts, len(features), pla...]
  transfers between devices with their start and end apart: 16 -> 18, of which waited for: 6 -> 12; matrix products, arithmetic and copies ran while one was open for 9% -> 11% of each run, Pallas kernels for 36% -> 42%
where the time goes in v3:
time: 172 us; the launch traced here: 171 us
  Pallas kernels  71.3 us (41%)
  waiting for transfers between devices  32.3 us (19%)
  starting transfers between devices  17.3 us (10%)
  local copies, waits for them, and re-layouts  16.3 us (9%)
  between operations  15.3 us (9%)
  blocking collectives  7.37 us (4%)
  matrix products  7.33 us (4%)
  other arithmetic  4.13 us (2%)
    pallas_call x3, Pallas kernels, core_call(): pl.pallas_call(functools.partial(core_kernel, first, first_head, together...  34.4 us
    ppermute x12, waiting for transfers between devices, swap(): return lax.ppermute(array, axis, [(i, i ^ hop) for i in range(parts)])  23.7 us
    pallas_call x2, Pallas kernels, weight_blocks(): pl.pallas_call(functools.partial(weight_kernel, parts, len(features), pla...  14.2 us
    pallas_call x2, Pallas kernels, head_terms(): pl.pallas_call(functools.partial(term_kernel, len(sets)), grid=(parts //...  11.7 us
    ppermute x12, starting transfers between devices, swap(): return lax.ppermute(array, axis, [(i, i ^ hop) for i in range(parts)])  10.1 us
    unnamed x149, local copies, waits for them, and re-layouts  8.09 us
    unnamed x1, blocking collectives  7.37 us
    dot_general x6, matrix products, body(): jnp.dot(gathered[i], w, preferred_element_type=F32).astype(BF16)  7.33 us
  transfers between devices with their start and end apart: 18, of which 12 were waited for; matrix products, arithmetic and copies ran while one was open for 11% of the time, Pallas kernels for 42%

profile of v3, /device:TPU:0, one launch (start us, length us, event | category | flops | bytes accessed | tf_op | source)
XLA Modules:
  0.0 171.4 jit_solution(2168939651727061591)
XLA Ops:
  7.2 1.8 %fusion.7 = (bf16[512,256]{1,0:T(8,128)(2,1)S(1)}, bf16[512,256]{1,0:T(8,128)(2,1)}) fusion(bf16[1024,256]{1,0:T(8,128)(2,1)} %param.16), kind=kLoop, calls=%fused_computation.37 | loop fusion | bytes 1048576 | tf_op jit(solution)/shard_map/slice | solution.py:766
  9.0 3.0 %collective-permute-start = (bf16[512,256]{1,0:T(8,128)(2,1)S(1)}, bf16[512,256]{1,0:T(8,128)(2,1)S(1)}, u32[]{:S(2)}, u32[]{:S(2)}) collective-permute-start(bf16[512,256]{1,0:T(8,128)(2,1)S(1)} %get-tuple-element.92.refs_0_), channel_id=1, source_target_pairs={{0,2},{1,3},{2,4},{3,5},{4,6},{5,7},{6,0},{7,1},{8,10},{9,11},{10,... | collective-permute-start | bytes 786440 | tf_op jit(solution)/shard_map/ppermute | solution.py:749
  12.0 2.6 %collective-permute-start.1 = (bf16[512,256]{1,0:T(8,128)(2,1)S(1)}, bf16[512,256]{1,0:T(8,128)(2,1)S(1)}, u32[]{:S(2)}, u32[]{:S(2)}) collective-permute-start(bf16[512,256]{1,0:T(8,128)(2,1)S(1)} %get-tuple-element.92.refs_0_), channel_id=1, source_target_pairs={{0,4},{1,5},{2,6},{3,7},{4,0},{5,1},{6,2},{7,3},{8,12},{9,13},{10,... | collective-permute-start | bytes 786440 | tf_op jit(solution)/shard_map/ppermute | solution.py:749
  14.6 1.3 collective-permute-start.2
  16.0 1.2 dynamic-slice
  18.7 7.4 %all-reduce = s32[32]{0:T(128)S(1)} all-reduce(s32[32]{0:T(128)S(1)} %dynamic-update-slice), channel_id=1, replica_groups=mesh['batch'=4,'tensor'=8] {'batch'}, use_global_device_ids=true, to_apply=%add | all-reduce | flops 32 | bytes 256
  27.1 4.6 %collective-permute-done.1.refs_2_ = bf16[512,256]{1,0:T(8,128)(2,1)S(1)} collective-permute-done((bf16[512,256]{1,0:T(8,128)(2,1)S(1)}, bf16[512,256]{1,0:T(8,128)(2,1)S(1)}, u32[]{:S(2)}, u32[]{:S(2)}) %collective-permute-start.1) | collective-permute-done | bytes 262176 | tf_op jit(solution)/shard_map/ppermute | solution.py:749
  36.1 1.3 copy-done.2
  39.0 1.2 convolution_convert_fusion.1.refs_4_
  40.3 16.7 %core_grads.3 = (bf16[512,256]{1,0:T(8,128)(2,1)S(1)}, bf16[512,256]{1,0:T(8,128)(2,1)S(1)}, bf16[512,512]{1,0:T(8,128)(2,1)S(1)}, f32[4,256]{1,0:T(4,128)S(1)},...) custom-call(s32[8]{0:T(128)S(1)} %copy-done.59, ...), custom_call_target="tpu_custom_call" | custom-call | flops 20 | tf_op jit(solution)/shard_map/core_grads/pallas_call | solution.py:310
  57.1 5.8 %head_terms.3 = bf16[8,512,256]{2,1,0:T(8,128)(2,1)} custom-call(bf16[512,256]{1,0:T(8,128)(2,1)S(1)} %get-tuple-element.98.refs_2_.refs_0_, bf16[512,256]{1,0:T(8,128)(2,1)S(1)} %get-tuple-element.99.refs_3_.refs_1_, bf16[512,512]{1,0:T(8,128)(2,1)S(1)} %get-tuple-element.100.refs_4_.refs_2_, bf16[2048,256]{1,0:T(8,128)(2,1)S(1)} %copy-done.2, ...), custom_call_target="tpu_custom_call" | custom-call | flops 2 | tf_op jit(solution)/shard_map/head_terms/pallas_call | solution.py:410
  63.6 3.9 %all-gather.2.cloned.1.call-done.refs_1_ = bf16[512,2048]{1,0:T(8,128)(2,1)} async-done(((bf16[512,256]{1,0:T(8,128)(2,1)}), bf16[512,2048]{1,0:T(8,128)(2,1)}) %all-gather.2.cloned.1.call-update) | async-done | bytes 2097168 | tf_op jit(solution)/shard_map/all_gather | solution.py:779
  67.5 2.7 %convolution_convert_fusion.2.refs_3_ = bf16[512,256]{1,0:T(8,128)(2,1)S(1)} fusion(bf16[512,2048]{1,0:T(8,128)(2,1)} %all-gather.2.cloned.1.call-done.refs_1_, bf16[2048,256]{1,0:T(8,128)(2,1)} %refs_4_.1), kind=kOutput, calls=%fused_computation.2 | convolution fusion | flops 537001984 | bytes 3407872 | tf_op jit(solution)/shard_map/dot_general | solution.py:794
  71.8 1.2 convolution_convert_fusion.refs_4_
  73.1 9.0 %core_grads.4 = (bf16[512,128]{1,0:T(8,128)(2,1)S(1)}, bf16[512,128]{1,0:T(8,128)(2,1)S(1)}, bf16[512,256]{1,0:T(8,128)(2,1)S(1)}, f32[4,128]{1,0:T(4,128)S(1)},...) custom-call(s32[8]{0:T(128)S(1)} %copy-done.59, ...), custom_call_target="tpu_custom_call", output_to_operand_aliasing={{8}: (16, {})} | custom-call | flops 10 | tf_op jit(solution)/shard_map/core_grads/pallas_call | solution.py:310
  83.7 7.1 %weight_blocks.2 = (bf16[784,512]{1,0:T(8,128)(2,1)}, bf16[640,512]{1,0:T(8,128)(2,1)S(1)}, f32[256,512]{1,0:T(8,128)S(1)}, f32[256,512]{1,0:T(8,128)S(1)}, f32[512,512]{1,0:T(8,128)}) custom-call(s32[4]{0:T(128)S(1)} %broadcast_xor_fusion.order, bf16[512,2048]{1,0:T(8,128)(2,1)} %copy-done, bf16[512,2048]{1,0:T(8,128)(2,1)} %all-gather.2.cloned.1.call-done.refs_1_, ...), custom_call_target="tpu_custom_call" | custom-call | flops 2 | tf_op jit(solution)/shard_map/weight_blocks/pallas_call | solution.py:542
  90.8 1.1 collective-permute-start.7
  91.9 1.5 collective-permute-start.8
  93.4 8.7 %core_grads.5 = (bf16[512,128]{1,0:T(8,128)(2,1)S(1)}, bf16[512,128]{1,0:T(8,128)(2,1)S(1)}, bf16[512,256]{1,0:T(8,128)(2,1)S(1)}, f32[4,128]{1,0:T(4,128)S(1)},...) custom-call(s32[8]{0:T(128)S(1)} %copy-done.60, ...), custom_call_target="tpu_custom_call", output_to_operand_aliasing={{8}: (16, {})} | custom-call | flops 10 | tf_op jit(solution)/shard_map/core_grads/pallas_call | solution.py:310
  102.2 5.9 %head_terms.2 = bf16[8,512,256]{2,1,0:T(8,128)(2,1)} custom-call(bf16[512,128]{1,0:T(8,128)(2,1)S(1)} %get-tuple-element.105.refs_5_.refs_0_, bf16[512,128]{1,0:T(8,128)(2,1)S(1)} %get-tuple-element.106.refs_6_.refs_1_, bf16[512,256]{1,0:T(8,128)(2,1)S(1)} %get-tuple-element.107.refs_7_.refs_2_, bf16[512,128]{1,0:T(8,128)(2,1)S(1)} %get-tuple-element.141.refs_3_.refs_5_, ...), custom_call_target="tpu_custom_call" | custom-call | flops 2 | tf_op jit(solution)/shard_map/head_terms/pallas_call | solution.py:410
  108.5 2.5 %collective-permute-done.7.refs_0_.refs_1_.refs_8_ = bf16[784,512]{1,0:T(8,128)(2,1)S(1)} collective-permute-done((bf16[784,512]{1,0:T(8,128)(2,1)}, bf16[784,512]{1,0:T(8,128)(2,1)S(1)}, u32[]{:S(2)}, u32[]{:S(2)}) %collective-permute-start.7) | collective-permute-done | bytes 802848 | tf_op jit(solution)/shard_map/ppermute | solution.py:743
  113.1 7.2 %weight_blocks.3 = (bf16[784,512]{1,0:T(8,128)(2,1)}, bf16[640,512]{1,0:T(8,128)(2,1)S(1)}, f32[256,512]{1,0:T(8,128)S(1)}, f32[256,512]{1,0:T(8,128)S(1)}, f32[512,512]{1,0:T(8,128)}) custom-call(s32[4]{0:T(128)S(1)} %copy-done.64, bf16[512,2048]{1,0:T(8,128)(2,1)} %copy-done, bf16[512,2048]{1,0:T(8,128)(2,1)} %all-gather.2.cloned.1.call-done.refs_1_, ...), custom_call_target="tpu_custom_call" | custom-call | flops 2 | tf_op jit(solution)/shard_map/weight_blocks/pallas_call | solution.py:542
  120.2 1.2 collective-permute-start.11
  121.4 1.5 collective-permute-start.12
  123.4 15.6 %collective-permute-done.12.refs_1_.refs_7_.refs_13_ = bf16[640,512]{1,0:T(8,128)(2,1)S(1)} collective-permute-done((bf16[640,512]{1,0:T(8,128)(2,1)S(1)}, bf16[640,512]{1,0:T(8,128)(2,1)S(1)}, u32[]{:S(2)}, u32[]{:S(2)}) %collective-permute-start.12) | collective-permute-done | bytes 655392 | tf_op jit(solution)/shard_map/ppermute | solution.py:743
  140.6 1.2 collective-permute-start.13
  141.9 1.5 collective-permute-start.10
  147.1 1.1 copy.37
  151.6 2.7 %collective-permute-done.14.refs_9_.refs_15_ = bf16[256,512]{1,0:T(8,128)(2,1)} collective-permute-done((bf16[256,512]{1,0:T(8,128)(2,1)}, bf16[256,512]{1,0:T(8,128)(2,1)}, u32[]{:S(2)}, u32[]{:S(2)}) %collective-permute-start.14) | collective-permute-done | bytes 262176 | tf_op jit(solution)/shard_map/ppermute | solution.py:743
  154.9 4.0 %place_states.1 = (f32[8,4,128,128]{3,2,1,0:T(8,128)}, f32[4,256]{1,0:T(4,128)}, f32[4,256]{1,0:T(4,128)}, f32[4,512]{1,0:T(4,128)}) custom-call(s32[8]{0:T(128)S(1)} %copy-done.66, s32[8]{0:T(128)S(1)} %copy-done.65, f32[4,128]{1,0:T(4,128)S(1)} %copy-done.44, f32[4,128]{1,0:T(4,128)S(1)} %copy-done.46, f32[4,256]{1,0:T(4,128)S(1)} %copy-done.32, ...), custom_call_target="tpu_custom_call" | custom-call | tf_op jit(solution)/shard_map/place_states/pallas_call | solution.py:705
  159.0 4.0 %finish_weights.1 = (f32[512,256]{1,0:T(8,128)}, f32[512,256]{1,0:T(8,128)}, f32[512,512]{1,0:T(8,128)}) custom-call(f32[512,512]{1,0:T(8,128)S(1)} %copy-done.67, bf16[784,512]{1,0:T(8,128)(2,1)S(1)} %copy-done.6, bf16[640,512]{1,0:T(8,128)(2,1)S(1)} %copy-done.10, bf16[400,512]{1,0:T(8,128)(2,1)} %collective-permute-done.9.refs_3_.refs_10_, ...), custom_call_target="tpu_custom_call" | custom-call | flops 15000000512 | bytes 1 | tf_op jit(solution)/shard_map/finish_weights/pallas_call | solution.py:630
  163.0 1.9 %pad_maximum_fusion = bf16[1024,256]{1,0:T(8,128)(2,1)} fusion(bf16[512,256]{1,0:T(8,128)(2,1)} %reduce-scatter.5.cloned.1.call-done, bf16[512,256]{1,0:T(8,128)(2,1)} %reduce-scatter.3.cloned.1.call-done), kind=kLoop, calls=%fused_computation.6 | loop fusion | flops 1048576 | bytes 1048576 | tf_op jit(solution)/shard_map/concatenate | solution.py:848
  (195 shorter events, 23.7 us)
Async XLA Ops:
  7.2 60.3 %all-gather.2.cloned.1.call-start = ((), (), s32[]{:S(2)}) async-start(), calls=%async_computation.2 | async-start | bytes 2359296 | tf_op jit(solution)/shard_map/all_gather | solution.py:779
  9.0 18.1 %collective-permute-start = (bf16[512,256]{1,0:T(8,128)(2,1)S(1)}, bf16[512,256]{1,0:T(8,128)(2,1)S(1)}, u32[]{:S(2)}, u32[]{:S(2)}) collective-permute-start(bf16[512,256]{1,0:T(8,128)(2,1)S(1)} %get-tuple-element.92.refs_0_), channel_id=1, source_target_pairs={{0,2},{1,3},{2,4},{3,5},{4,6},{5,7},{6,0},{7,1},{8,10},{9,11},{10,... | collective-permute-start | bytes 786440 | tf_op jit(solution)/shard_map/ppermute | solution.py:749
  12.0 19.7 %collective-permute-start.1 = (bf16[512,256]{1,0:T(8,128)(2,1)S(1)}, bf16[512,256]{1,0:T(8,128)(2,1)S(1)}, u32[]{:S(2)}, u32[]{:S(2)}) collective-permute-start(bf16[512,256]{1,0:T(8,128)(2,1)S(1)} %get-tuple-element.92.refs_0_), channel_id=1, source_target_pairs={{0,4},{1,5},{2,6},{3,7},{4,0},{5,1},{6,2},{7,3},{8,12},{9,13},{10,... | collective-permute-start | bytes 786440 | tf_op jit(solution)/shard_map/ppermute | solution.py:749
  14.6 17.1 %collective-permute-start.2 = (bf16[512,256]{1,0:T(8,128)(2,1)S(1)}, bf16[512,256]{1,0:T(8,128)(2,1)S(1)}, u32[]{:S(2)}, u32[]{:S(2)}) collective-permute-start(bf16[512,256]{1,0:T(8,128)(2,1)S(1)} %get-tuple-element.92.refs_0_), channel_id=1, source_target_pairs={{0,6},{1,7},{2,0},{3,1},{4,2},{5,3},{6,4},{7,5},{8,14},{9,15},{10,... | collective-permute-start | bytes 786440 | tf_op jit(solution)/shard_map/ppermute | solution.py:749
  26.4 46.7 %copy-start.61 = (s32[8]{0:T(128)}, s32[8]{0:T(128)S(1)}, u32[]{:S(2)}) copy-start(s32[8]{0:T(128)S(1)} %dynamic_slice.3.refs_1_) | copy-start | bytes 100
  31.7 131.3 %reduce-scatter.3.cloned.1.call-start = ((), (), s32[]{:S(2)}) async-start(), calls=%async_computation.3 | async-start | bytes 2359296 | tf_op jit(solution)/shard_map/reduce_scatter | solution.py:841
  31.8 1.6 collective-permute-start.3
  31.9 1.9 %collective-permute-start.4 = (bf16[512,256]{1,0:T(8,128)(2,1)S(1)}, bf16[512,256]{1,0:T(8,128)(2,1)S(1)}, u32[]{:S(2)}, u32[]{:S(2)}) collective-permute-start(bf16[512,256]{1,0:T(8,128)(2,1)S(1)} %collective-permute-done.refs_1_), channel_id=1, source_target_pairs={{0,1},{1,0},{2,3},{3,2},{4,5},{5,4},{6,7},{7,6},{8,9},{9,8},{10,11... | collective-permute-start | bytes 786440 | tf_op jit(solution)/shard_map/ppermute | solution.py:743
  32.4 1.8 %collective-permute-start.5 = (bf16[512,256]{1,0:T(8,128)(2,1)S(1)}, bf16[512,256]{1,0:T(8,128)(2,1)S(1)}, u32[]{:S(2)}, u32[]{:S(2)}) collective-permute-start(bf16[512,256]{1,0:T(8,128)(2,1)S(1)} %collective-permute-done.1.refs_2_), channel_id=1, source_target_pairs={{0,1},{1,0},{2,3},{3,2},{4,5},{5,4},{6,7},{7,6},{8,9},{9,8},{10,11... | collective-permute-start | bytes 786440 | tf_op jit(solution)/shard_map/ppermute | solution.py:743
  32.4 2.1 %collective-permute-start.6 = (bf16[512,256]{1,0:T(8,128)(2,1)S(1)}, bf16[512,256]{1,0:T(8,128)(2,1)S(1)}, u32[]{:S(2)}, u32[]{:S(2)}) collective-permute-start(bf16[512,256]{1,0:T(8,128)(2,1)S(1)} %collective-permute-done.2.refs_3_), channel_id=1, source_target_pairs={{0,1},{1,0},{2,3},{3,2},{4,5},{5,4},{6,7},{7,6},{8,9},{9,8},{10,11... | collective-permute-start | bytes 786440 | tf_op jit(solution)/shard_map/ppermute | solution.py:743
  57.1 16.0 %copy-start.41 = (f32[4,512]{1,0:T(4,128)}, f32[4,512]{1,0:T(4,128)S(1)}, u32[]{:S(2)}) copy-start(f32[4,512]{1,0:T(4,128)S(1)} %get-tuple-element.103.refs_15_) | copy-start | bytes 24580
  57.1 16.0 %copy-start.55 = (f32[4,256]{1,0:T(4,128)}, f32[4,256]{1,0:T(4,128)S(1)}, u32[]{:S(2)}) copy-start(f32[4,256]{1,0:T(4,128)S(1)} %get-tuple-element.101.refs_13_) | copy-start | bytes 12292
  57.1 16.0 %copy-start.57 = (f32[4,256]{1,0:T(4,128)}, f32[4,256]{1,0:T(4,128)S(1)}, u32[]{:S(2)}) copy-start(f32[4,256]{1,0:T(4,128)S(1)} %get-tuple-element.102.refs_14_) | copy-start | bytes 12292
  57.1 26.5 %copy-start.11 = (bf16[512,256]{1,0:T(8,128)(2,1)}, bf16[512,256]{1,0:T(8,128)(2,1)S(1)}, u32[]{:S(2)}) copy-start(bf16[512,256]{1,0:T(8,128)(2,1)S(1)} %get-tuple-element.98.refs_2_.refs_0_) | copy-start | bytes 786436
  57.1 26.5 %copy-start.13 = (bf16[512,256]{1,0:T(8,128)(2,1)}, bf16[512,256]{1,0:T(8,128)(2,1)S(1)}, u32[]{:S(2)}) copy-start(bf16[512,256]{1,0:T(8,128)(2,1)S(1)} %get-tuple-element.99.refs_3_.refs_1_) | copy-start | bytes 786436
  63.0 100.0 %reduce-scatter.5.cloned.1.call-start = ((), (), s32[]{:S(2)}) async-start(), calls=%async_computation.4 | async-start | bytes 2359296 | tf_op jit(solution)/shard_map/reduce_scatter | solution.py:841
  63.6 20.0 %copy-start.63 = (s32[4]{0:T(128)}, s32[4]{0:T(128)S(1)}, u32[]{:S(2)}) copy-start(s32[4]{0:T(128)S(1)} %broadcast_xor_fusion.order) | copy-start | bytes 52
  83.6 27.4 %copy-start.31 = (f32[4,256]{1,0:T(4,128)}, f32[4,256]{1,0:T(4,128)S(1)}, u32[]{:S(2)}) copy-start(f32[4,256]{1,0:T(4,128)S(1)} %get-tuple-element.110.refs_10_.refs_6_.refs_2_) | copy-start | bytes 12292
  83.6 27.4 %copy-start.43 = (f32[4,128]{1,0:T(4,128)}, f32[4,128]{1,0:T(4,128)S(1)}, u32[]{:S(2)}) copy-start(f32[4,128]{1,0:T(4,128)S(1)} %get-tuple-element.108.refs_8_.refs_4_.refs_0_) | copy-start | bytes 6148
  83.6 27.4 %copy-start.45 = (f32[4,128]{1,0:T(4,128)}, f32[4,128]{1,0:T(4,128)S(1)}, u32[]{:S(2)}) copy-start(f32[4,128]{1,0:T(4,128)S(1)} %get-tuple-element.109.refs_9_.refs_5_.refs_1_) | copy-start | bytes 6148
  90.8 20.2 %collective-permute-start.7 = (bf16[784,512]{1,0:T(8,128)(2,1)}, bf16[784,512]{1,0:T(8,128)(2,1)S(1)}, u32[]{:S(2)}, u32[]{:S(2)}) collective-permute-start(bf16[784,512]{1,0:T(8,128)(2,1)} %get-tuple-element.131), channel_id=1, source_target_pairs={{0,8},{8,0},{16,24},{24,16},{1,9},{9,1},{17,25},{25,17},{2,10},{10... | collective-permute-start | bytes 2408456 | tf_op jit(solution)/shard_map/ppermute | solution.py:743
  91.9 16.6 %collective-permute-start.8 = (bf16[640,512]{1,0:T(8,128)(2,1)S(1)}, bf16[640,512]{1,0:T(8,128)(2,1)S(1)}, u32[]{:S(2)}, u32[]{:S(2)}) collective-permute-start(bf16[640,512]{1,0:T(8,128)(2,1)S(1)} %get-tuple-element.132), channel_id=1, source_target_pairs={{0,16},{8,24},{16,0},{24,8},{1,17},{9,25},{17,1},{25,9},{2,18},{10... | collective-permute-start | bytes 1966088 | tf_op jit(solution)/shard_map/ppermute | solution.py:743
  113.0 26.6 %copy-start.35 = (f32[4,256]{1,0:T(4,128)S(1)}, f32[4,256]{1,0:T(4,128)}, u32[]{:S(2)}) copy-start(f32[4,256]{1,0:T(4,128)} %copy-done.33) | copy-start | bytes 12292
  113.0 26.6 %copy-start.49 = (f32[4,128]{1,0:T(4,128)S(1)}, f32[4,128]{1,0:T(4,128)}, u32[]{:S(2)}) copy-start(f32[4,128]{1,0:T(4,128)} %copy-done.47) | copy-start | bytes 6148
  113.1 26.5 %copy-start.53 = (f32[4,128]{1,0:T(4,128)S(1)}, f32[4,128]{1,0:T(4,128)}, u32[]{:S(2)}) copy-start(f32[4,128]{1,0:T(4,128)} %copy-done.51) | copy-start | bytes 6148
  120.2 19.4 %collective-permute-start.11 = (bf16[784,512]{1,0:T(8,128)(2,1)}, bf16[784,512]{1,0:T(8,128)(2,1)S(1)}, u32[]{:S(2)}, u32[]{:S(2)}) collective-permute-start(bf16[784,512]{1,0:T(8,128)(2,1)} %get-tuple-element.149), channel_id=1, source_target_pairs={{0,8},{8,0},{16,24},{24,16},{1,9},{9,1},{17,25},{25,17},{2,10},{10... | collective-permute-start | bytes 2408456 | tf_op jit(solution)/shard_map/ppermute | solution.py:743
  121.4 17.7 %collective-permute-start.12 = (bf16[640,512]{1,0:T(8,128)(2,1)S(1)}, bf16[640,512]{1,0:T(8,128)(2,1)S(1)}, u32[]{:S(2)}, u32[]{:S(2)}) collective-permute-start(bf16[640,512]{1,0:T(8,128)(2,1)S(1)} %get-tuple-element.150), channel_id=1, source_target_pairs={{0,16},{8,24},{16,0},{24,8},{1,17},{9,25},{17,1},{25,9},{2,18},{10... | collective-permute-start | bytes 1966088 | tf_op jit(solution)/shard_map/ppermute | solution.py:743
  122.9 28.7 %collective-permute-start.9 = (bf16[400,512]{1,0:T(8,128)(2,1)}, bf16[400,512]{1,0:T(8,128)(2,1)}, u32[]{:S(2)}, u32[]{:S(2)}) collective-permute-start(bf16[400,512]{1,0:T(8,128)(2,1)} %get-tuple-element.139), channel_id=1, source_target_pairs={{0,16},{8,24},{16,0},{24,8},{1,17},{9,25},{17,1},{25,9},{2,18},{10... | collective-permute-start | bytes 1228808 | tf_op jit(solution)/shard_map/ppermute | solution.py:743
  139.6 15.2 %copy-start.10 = (bf16[640,512]{1,0:T(8,128)(2,1)S(1)}, bf16[640,512]{1,0:T(8,128)(2,1)}, u32[]{:S(2)}) copy-start(bf16[640,512]{1,0:T(8,128)(2,1)} %copy-done.9) | copy-start | bytes 1966084
  140.6 14.2 %collective-permute-start.13 = (bf16[400,512]{1,0:T(8,128)(2,1)}, bf16[400,512]{1,0:T(8,128)(2,1)}, u32[]{:S(2)}, u32[]{:S(2)}) collective-permute-start(bf16[400,512]{1,0:T(8,128)(2,1)} %get-tuple-element.153), channel_id=1, source_target_pairs={{0,16},{8,24},{16,0},{24,8},{1,17},{9,25},{17,1},{25,9},{2,18},{10... | collective-permute-start | bytes 1228808 | tf_op jit(solution)/shard_map/ppermute | solution.py:743
  141.9 9.7 %collective-permute-start.10 = (bf16[256,512]{1,0:T(8,128)(2,1)}, bf16[256,512]{1,0:T(8,128)(2,1)S(1)}, u32[]{:S(2)}, u32[]{:S(2)}) collective-permute-start(bf16[256,512]{1,0:T(8,128)(2,1)} %get-tuple-element.140), channel_id=1, source_target_pairs={{0,8},{8,0},{16,24},{24,16},{1,9},{9,1},{17,25},{25,17},{2,10},{10... | collective-permute-start | bytes 786440 | tf_op jit(solution)/shard_map/ppermute | solution.py:743
  143.3 11.0 %collective-permute-start.14 = (bf16[256,512]{1,0:T(8,128)(2,1)}, bf16[256,512]{1,0:T(8,128)(2,1)}, u32[]{:S(2)}, u32[]{:S(2)}) collective-permute-start(bf16[256,512]{1,0:T(8,128)(2,1)} %get-tuple-element.154), channel_id=1, source_target_pairs={{0,8},{8,0},{16,24},{24,16},{1,9},{9,1},{17,25},{25,17},{2,10},{10... | collective-permute-start | bytes 786440 | tf_op jit(solution)/shard_map/ppermute | solution.py:743
  (59 other events, 386.6 us)
Sparse Core Ops, SparseCore 0:
  31.9 35.5 all-gather.1
  69.8 34.8 reduce-scatter.2
  113.1 36.3 reduce-scatter.4

commit v4 on v3

--- a/solution.py
+++ b/solution.py
@@ -350,29 +350,26 @@
     return pl.CostEstimate(flops=flops // COST, bytes_accessed=size // COST, transcendentals=0)
 
 
-def assemble_kernel(indices, *refs):
-    blocks, features = refs[:-1], refs[-1]
-    width = blocks[0].shape[1]
-    for i, block in enumerate(blocks):
-        features[:, pl.ds(pl.multiple_of(indices[i] * width, width), width)] = block[...]
+def assemble_kernel(indices, own, other, features):
+    chips, _, width = own.shape
+    for i in range(chips):
+        for j, block in enumerate((own, other)):
+            start = pl.multiple_of(indices[j * chips + i] * width, width)
+            features[:, pl.ds(start, width)] = block[i]
 
 
 def assemble(indices, blocks):
-    rows, width = blocks[0].shape
+    chips, rows, width = blocks[0].shape
     tile = 128
-
-    def tiles(count):
-        return pl.BlockSpec((tile, count), lambda i, *_: (i, 0))
-
     return pl.pallas_call(
         assemble_kernel,
         grid_spec=pltpu.PrefetchScalarGridSpec(
             num_scalar_prefetch=1,
             grid=(rows // tile,),
-            in_specs=[tiles(width)] * len(blocks),
-            out_specs=tiles(width * len(blocks)),
+            in_specs=[pl.BlockSpec((chips, tile, width), lambda i, *_: (0, i, 0))] * 2,
+            out_specs=pl.BlockSpec((tile, width * 2 * chips), lambda i, *_: (i, 0)),
         ),
-        out_shape=jax.ShapeDtypeStruct((rows, width * len(blocks)), BF16),
+        out_shape=jax.ShapeDtypeStruct((rows, width * 2 * chips), BF16),
         compiler_params=pltpu.CompilerParams(vmem_limit_bytes=32 << 20),
         cost_estimate=cost(1, 4 << 20),
         name="assemble",
@@ -602,12 +599,20 @@
     return [*arrays[:2], swap(arrays[2], "batch", parts, 2), swap(arrays[3], "batch", parts, 1)]
 
 
-def finish_kernel(parts, sources, widths, *refs):
-    outs = refs[-3:]
-    columns = sum(widths)
-    half = columns // 2
-    for g in range((len(refs) - 3) // (sources + 1)):
-        own, *pieces = refs[g * (sources + 1) : (g + 1) * (sources + 1)]
+def finish_kernel(parts, key_heads, widths, sources, ranks, *refs):
+    hidden_parts, joined, refs = refs[:2], refs[-1], refs[2:-1]
+    columns, half = sum(widths), sum(widths) // 2
+    taps, kept, refs = refs[: 3 * key_heads], refs[3 * key_heads : 4 * key_heads], refs[4 * key_heads :]
+    outs, out, tap_outs = refs[-7:-4], refs[-4], refs[-3:]
+    refs = refs[:-7]
+    per = len(refs) // key_heads
+    count = 4 if parts == 4 else parts - 1
+    hops = parts - 1
+    group, width = kept[0].shape[1], kept[0].shape[2]
+    step = pl.program_id(0)
+    for g in range(key_heads):
+        own, *rest = refs[g * per : (g + 1) * per]
+        pieces, states, edges = rest[:count], rest[count : count + hops], rest[count + hops :]
         if parts == 4:
             upper = own[:half] + (pieces[0][...].astype(F32) + pieces[2][...].astype(F32))
             lower = own[half:] + (pieces[1][...].astype(F32) + pieces[3][...].astype(F32))
@@ -615,44 +620,10 @@
         else:
             total = sum((piece[...].astype(F32) for piece in pieces), own[...]).T
         start = 0
-        for out, width in zip(outs, widths):
-            out[:, g * width : (g + 1) * width] = total[:, start : start + width]
-            start += width
-
-
-def finish_weights(parts, own, pieces, widths):
-    key_heads, rows, columns = len(pieces), own[0].shape[1], sum(widths)
-    tile = min(rows, 128)
-    sizes = [key_heads * n for n in widths]
-    count = columns // 2 if parts == 4 else columns
-    specs = [pl.BlockSpec((columns, tile), lambda i: (0, i))]
-    specs += [pl.BlockSpec((count, tile), lambda i: (0, i))] * len(pieces[0])
-    return pl.pallas_call(
-        functools.partial(finish_kernel, parts, len(pieces[0]), widths),
-        grid=(rows // tile,),
-        in_specs=specs * key_heads,
-        out_specs=[pl.BlockSpec((tile, n), lambda i: (i, 0)) for n in sizes],
-        out_shape=[jax.ShapeDtypeStruct((rows, n), F32) for n in sizes],
-        compiler_params=pltpu.CompilerParams(vmem_limit_bytes=32 << 20),
-        cost_estimate=pl.CostEstimate(flops=FINISH, bytes_accessed=1, transcendentals=0),
-        name="finish_weights",
-    )(*[x for mine, group in zip(own, pieces) for x in (mine, *group)])
-
-
-def place_kernel(parts, key_heads, columns, state_rows, sources, ranks, *refs):
-    taps, kept = refs[: 3 * key_heads], refs[3 * key_heads : 4 * key_heads]
-    count = (len(refs) - 4) // key_heads - 4
-    received = refs[4 * key_heads : -4]
-    out, tap_outs = refs[-4], refs[-3:]
-    group, width = kept[0].shape[1], kept[0].shape[2]
-    step = pl.program_id(0)
-    for g in range(key_heads):
-        arrays = received[g * count : (g + 1) * count]
-        if parts == 4:
-            places = [(0, columns), (1, columns), (2, columns // 2)]
-        else:
-            places = [(i, columns) for i in range(parts - 1)]
-        across = arrays[0].shape[1] // width
+        for weight, size in zip(outs, widths):
+            weight[:, g * size : (g + 1) * size] = total[:, start : start + size]
+            start += size
+        across = states[0].shape[1] // width
         for j in range(out.shape[0]):
             source, rank = sources[step * out.shape[0] + j], ranks[step * out.shape[0] + j]
 
@@ -660,63 +631,95 @@
             def _():
                 out[j, g * group : (g + 1) * group] = kept[g][rank].astype(F32)
 
-            for hop, (index, row) in enumerate(places):
-                for slot in range(kept[g].shape[0] // parts):
+            for hop, block in enumerate(states):
+                for slot in range(kept[g].shape[0]):
 
                     @pl.when((source == hop + 1) & (rank == slot))
                     def _():
                         for h in range(group):
                             tall, wide = divmod(slot * group + h, across)
-                            start = row + tall * width
-                            out[j, g * group + h] = arrays[index][
-                                start : start + width, wide * width : (wide + 1) * width
+                            out[j, g * group + h] = block[
+                                tall * width : (tall + 1) * width, wide * width : (wide + 1) * width
                             ].astype(F32)
 
         @pl.when(step == 0)
         def _():
+            count = hidden_parts[0].shape[0]
+            joined[:count, :] = hidden_parts[0][...]
+            joined[count:, :] = hidden_parts[1][...]
             mine = rounded_taps(tap_pieces(taps[3 * g : 3 * g + 3], width))
-            n = len(mine)
+            others = [load_taps(x, 0, len(mine), width) for x in edges]
             if parts == 4:
-                theirs = load_taps(arrays[0], columns + 2 * state_rows, n, width)
-                mine = rounded_taps([a + b for a, b in zip(mine, theirs)])
-                others = [load_taps(arrays[2], columns // 2 + state_rows, n, width)]
-            else:
-                others = [load_taps(x, columns + state_rows, n, width) for x in arrays]
+                mine = rounded_taps([a + b for a, b in zip(mine, others.pop(0))])
             groups = [mine, *others]
             while len(groups) > 1:
                 groups = [
                     [a + b for a, b in zip(groups[i], groups[i + 1])]
                     for i in range(0, len(groups), 2)
                 ]
-            pieces = groups[0]
+            sums = groups[0]
             for tap_out in tap_outs:
-                total = tap_out.shape[1] // key_heads
-                for i in range(total // width):
-                    start = g * total + i * width
-                    tap_out[:, start : start + width] = pieces.pop(0)
-
-
-def place_states(parts, sources, ranks, taps, sent, pieces, columns, state_rows):
+                size = tap_out.shape[1] // key_heads
+                for i in range(size // width):
+                    start = g * size + i * width
+                    tap_out[:, start : start + width] = sums.pop(0)
+
+
+def finish(parts, sources, ranks, hidden_rows, taps, sent, own, pieces, widths, state_rows, tap_rows):
     requests, key_heads = sources.shape[0], len(sent)
-    heads, width = key_heads * sent[0].shape[1], sent[0].shape[2]
-    together = 4 if requests % 4 == 0 else 1
-    sizes = [sum(x.shape[1] for x in taps[t::3]) for t in range(3)]
-    inputs = [*taps, *sent, *[x for group in pieces for x in group]]
+    columns, rows = sum(widths), own[0].shape[1]
+    group, width = sent[0].shape[1:3]
+    capacity = sent[0].shape[0] // parts
+    tile = min(rows, 128)
+    tiles = rows // tile
+    together = requests // tiles
+    if parts == 4:
+        state_places = [(0, columns), (1, columns), (2, columns // 2)]
+        tap_places = [(0, columns + 2 * state_rows), (2, columns // 2 + state_rows)]
+    else:
+        state_places = [(i, columns) for i in range(parts - 1)]
+        tap_places = [(i, columns + state_rows) for i in range(parts - 1)]
+
+    def rows_at(start, count):
+        return pl.BlockSpec((count, rows), lambda i, *_: (start // count, 0))
+
+    def column(count):
+        return pl.BlockSpec((count, tile), lambda i, *_: (0, i))
+
+    inputs, specs = [], []
+    for mine, group_pieces in zip(own, pieces):
+        inputs += [mine, *group_pieces]
+        specs += [column(columns)]
+        specs += [column(columns // 2 if parts == 4 else columns)] * len(group_pieces)
+        inputs += [group_pieces[i] for i, _ in (*state_places, *tap_places)]
+        specs += [rows_at(start, state_rows) for _, start in state_places]
+        specs += [rows_at(start, tap_rows) for _, start in tap_places]
+    sizes = [key_heads * n for n in widths]
+    heads = key_heads * group
+    joined = jax.ShapeDtypeStruct(
+        (sum(x.shape[0] for x in hidden_rows), hidden_rows[0].shape[1]), BF16
+    )
     return pl.pallas_call(
-        functools.partial(place_kernel, parts, key_heads, columns, state_rows),
+        functools.partial(finish_kernel, parts, key_heads, widths),
         grid_spec=pltpu.PrefetchScalarGridSpec(
             num_scalar_prefetch=2,
-            grid=(requests // together,),
-            in_specs=[whole(x) for x in inputs],
-            out_specs=[pl.BlockSpec((together, heads, width, width), lambda r, *_: (r, 0, 0, 0))]
-            + [pl.BlockSpec((taps[0].shape[0], n), lambda r, *_: (0, 0)) for n in sizes],
+            grid=(tiles,),
+            in_specs=[whole(x) for x in (*hidden_rows, *taps)]
+            + [pl.BlockSpec((capacity, group, width, width), lambda i, *_: (0, 0, 0, 0))] * key_heads
+            + specs,
+            out_specs=[pl.BlockSpec((tile, n), lambda i, *_: (i, 0)) for n in sizes]
+            + [pl.BlockSpec((together, heads, width, width), lambda i, *_: (i, 0, 0, 0))]
+            + [pl.BlockSpec((taps[0].shape[0], n), lambda i, *_: (0, 0)) for n in sizes]
+            + [whole(joined)],
         ),
-        out_shape=[jax.ShapeDtypeStruct((requests, heads, width, width), F32)]
-        + [jax.ShapeDtypeStruct((taps[0].shape[0], n), F32) for n in sizes],
+        out_shape=[jax.ShapeDtypeStruct((rows, n), F32) for n in sizes]
+        + [jax.ShapeDtypeStruct((requests, heads, width, width), F32)]
+        + [jax.ShapeDtypeStruct((taps[0].shape[0], n), F32) for n in sizes]
+        + [joined],
         compiler_params=pltpu.CompilerParams(vmem_limit_bytes=50 << 20),
-        cost_estimate=cost(1 << 20, 4 << 20),
-        name="place_states",
-    )(sources, ranks, *inputs)
+        cost_estimate=pl.CostEstimate(flops=FINISH, bytes_accessed=1, transcendentals=0),
+        name="finish",
+    )(sources, ranks, *hidden_rows, *taps, *sent, *inputs)
 
 
 def slot_plan(slot_map, all_slots, me, parts):
@@ -771,7 +774,8 @@
     rest, blocks, places, sources, ranks = lax.optimization_barrier(
         (rest, blocks, places, sources, ranks)
     )
-    blocks = blocks + [swap(x, "tensor", spread, 1) for x in blocks]
+    blocks = jnp.stack(blocks)
+    blocks = [blocks, swap(blocks, "tensor", spread, 1)]
     chip_steps = jnp.arange(chips, dtype=jnp.int32)
     came = (chip - chip_steps) % chips * 2
     indices = jnp.concatenate([came + core, came + 1 - core])
@@ -840,14 +844,11 @@
         term = term.reshape(-1, term.shape[2])
         hidden_rows.append(lax.psum_scatter(term, "tensor", scatter_dimension=0, tiled=True))
     pieces = [second_exchange(x, parts) for x in pieces]
-    slot_state_grad, *grad_taps = place_states(
-        parts, sources, ranks, tap_sums, sent, pieces, sum(widths), state_rows
-    )
-    grad_w = finish_weights(parts, own, pieces, widths)
-    grad_w, hidden_rows = lax.optimization_barrier((grad_w, hidden_rows))
-    grad_hidden = jnp.concatenate(hidden_rows, axis=0)
+    *grad_w, slot_state_grad, tap_q, tap_k, tap_v, grad_hidden = finish(
+        parts, sources, ranks, hidden_rows, tap_sums, sent, own, pieces, widths, state_rows, tap_rows
+    )
     return (
-        grad_hidden, *grad_w, *grad_taps, jnp.concatenate(decays), jnp.concatenate(betas),
+        grad_hidden, *grad_w, tap_q, tap_k, tap_v, jnp.concatenate(decays), jnp.concatenate(betas),
         slot_state_grad,
     )
 

time: 172 us -> 172 us (level)
  the two profiles are of different devices: /device:TPU:0 before, /device:TPU:12 now
where the time goes in v4:
time: 172 us; the launch traced here: 171 us
  Pallas kernels  69.8 us (41%)
  waiting for transfers between devices  36.9 us (21%)
  local copies, waits for them, and re-layouts  20.3 us (12%)
  between operations  15.3 us (9%)
  starting transfers between devices  13 us (8%)
  matrix products  7.07 us (4%)
  blocking collectives  6.36 us (4%)
  other arithmetic  2.44 us (1%)
    pallas_call x3, Pallas kernels, core_call(): pl.pallas_call(functools.partial(core_kernel, first, first_head, together...  34.1 us
    ppermute x9, waiting for transfers between devices, swap(): return lax.ppermute(array, axis, [(i, i ^ hop) for i in range(parts)])  25.9 us
    pallas_call x2, Pallas kernels, weight_blocks(): pl.pallas_call(functools.partial(weight_kernel, parts, len(features), pla...  14.3 us
    unnamed x147, local copies, waits for them, and re-layouts  13 us
    pallas_call x2, Pallas kernels, head_terms(): pl.pallas_call(functools.partial(term_kernel, len(sets)), grid=(parts //...  11.8 us
    ppermute x3, waiting for transfers between devices, along(): return lax.ppermute(array, 'tensor', pairs)  11 us
    ppermute x9, starting transfers between devices, swap(): return lax.ppermute(array, axis, [(i, i ^ hop) for i in range(parts)])  8.1 us
    dot_general x6, matrix products, body(): jnp.dot(gathered[i], w, preferred_element_type=F32).astype(BF16)  7.07 us
  transfers between devices with their start and end apart: 15, of which 11 were waited for; matrix products, arithmetic and copies ran while one was open for 10% of the time, Pallas kernels for 37%

profile of v4, /device:TPU:12, one launch (start us, length us, event | category | flops | bytes accessed | tf_op | source)
XLA Modules:
  0.0 171.2 jit_solution(692039328255560036)
XLA Ops:
  7.2 1.8 %fusion.7 = (bf16[512,256]{1,0:T(8,128)(2,1)S(1)}, bf16[512,256]{1,0:T(8,128)(2,1)}) fusion(bf16[1024,256]{1,0:T(8,128)(2,1)} %param.16), kind=kLoop, calls=%fused_computation.37 | loop fusion | bytes 1048576 | tf_op jit(solution)/shard_map/slice | solution.py:769
  9.0 1.6 collective-permute-start
  10.6 1.2 collective-permute-start.1
  11.8 1.8 %collective-permute-start.2 = (bf16[512,256]{1,0:T(8,128)(2,1)S(1)}, bf16[512,256]{1,0:T(8,128)(2,1)S(1)}, u32[]{:S(2)}, u32[]{:S(2)}) collective-permute-start(bf16[512,256]{1,0:T(8,128)(2,1)S(1)} %get-tuple-element.91), channel_id=1, source_target_pairs={{0,6},{1,7},{2,0},{3,1},{4,2},{5,3},{6,4},{7,5},{8,14},{9,15},{10,... | collective-permute-start | bytes 786440 | tf_op jit(solution)/shard_map/ppermute | solution.py:752
  13.6 1.2 dynamic-slice
  16.4 6.4 %all-reduce = s32[32]{0:T(128)S(1)} all-reduce(s32[32]{0:T(128)S(1)} %dynamic-update-slice), channel_id=1, replica_groups=mesh['batch'=4,'tensor'=8] {'batch'}, use_global_device_ids=true, to_apply=%add | all-reduce | flops 32 | bytes 256
  23.8 4.7 %collective-permute-done = bf16[512,256]{1,0:T(8,128)(2,1)S(1)} collective-permute-done((bf16[512,256]{1,0:T(8,128)(2,1)S(1)}, bf16[512,256]{1,0:T(8,128)(2,1)S(1)}, u32[]{:S(2)}, u32[]{:S(2)}) %collective-permute-start) | collective-permute-done | bytes 262176 | tf_op jit(solution)/shard_map/ppermute | solution.py:752
  28.5 4.5 %collective-permute-done.1 = bf16[512,256]{1,0:T(8,128)(2,1)S(1)} collective-permute-done((bf16[512,256]{1,0:T(8,128)(2,1)S(1)}, bf16[512,256]{1,0:T(8,128)(2,1)S(1)}, u32[]{:S(2)}, u32[]{:S(2)}) %collective-permute-start.1) | collective-permute-done | bytes 262176 | tf_op jit(solution)/shard_map/ppermute | solution.py:752
  33.0 1.8 %collective-permute-done.2 = bf16[512,256]{1,0:T(8,128)(2,1)S(1)} collective-permute-done((bf16[512,256]{1,0:T(8,128)(2,1)S(1)}, bf16[512,256]{1,0:T(8,128)(2,1)S(1)}, u32[]{:S(2)}, u32[]{:S(2)}) %collective-permute-start.2) | collective-permute-done | bytes 262176 | tf_op jit(solution)/shard_map/ppermute | solution.py:752
  36.1 1.6 collective-permute-done.3.other
  38.7 1.2 copy-done.6
  39.9 1.2 copy-done.16
  42.9 1.3 copy-done.3
  45.8 1.2 convolution_convert_fusion.1.refs_4_
  47.1 16.7 %core_grads.3 = (bf16[512,256]{1,0:T(8,128)(2,1)S(1)}, bf16[512,256]{1,0:T(8,128)(2,1)S(1)}, bf16[512,512]{1,0:T(8,128)(2,1)S(1)}, f32[4,256]{1,0:T(4,128)S(1)},...) custom-call(s32[8]{0:T(128)S(1)} %copy-done.58, ...), custom_call_target="tpu_custom_call" | custom-call | flops 20 | tf_op jit(solution)/shard_map/core_grads/pallas_call | solution.py:310
  63.9 5.9 %head_terms.2 = bf16[8,512,256]{2,1,0:T(8,128)(2,1)} custom-call(bf16[512,256]{1,0:T(8,128)(2,1)S(1)} %get-tuple-element.95.refs_0_.refs_2_, bf16[512,256]{1,0:T(8,128)(2,1)S(1)} %get-tuple-element.96.refs_1_.refs_3_, bf16[512,512]{1,0:T(8,128)(2,1)S(1)} %get-tuple-element.97.refs_2_.refs_4_, bf16[2048,256]{1,0:T(8,128)(2,1)S(1)} %copy-done.2, ...), custom_call_target="tpu_custom_call" | custom-call | flops 2 | tf_op jit(solution)/shard_map/head_terms/pallas_call | solution.py:407
  70.5 2.4 %convolution_convert_fusion.3.refs_2_ = bf16[512,256]{1,0:T(8,128)(2,1)S(1)} fusion(bf16[512,2048]{1,0:T(8,128)(2,1)} %all-gather.2.cloned.1.call-done.refs_1_, bf16[2048,256]{1,0:T(8,128)(2,1)S(1)} %copy-done.2), kind=kOutput, calls=%fused_computation.3 | convolution fusion | flops 537001984 | bytes 3407872 | tf_op jit(solution)/shard_map/dot_general | solution.py:798
  74.6 1.2 convolution_convert_fusion.refs_4_
  75.9 8.7 %core_grads.4 = (bf16[512,128]{1,0:T(8,128)(2,1)S(1)}, bf16[512,128]{1,0:T(8,128)(2,1)S(1)}, bf16[512,256]{1,0:T(8,128)(2,1)S(1)}, f32[4,128]{1,0:T(4,128)S(1)},...) custom-call(s32[8]{0:T(128)S(1)} %copy-done.58, ...), custom_call_target="tpu_custom_call", output_to_operand_aliasing={{8}: (16, {})} | custom-call | flops 10 | tf_op jit(solution)/shard_map/core_grads/pallas_call | solution.py:310
  84.8 7.2 %weight_blocks.2 = (bf16[784,512]{1,0:T(8,128)(2,1)}, bf16[640,512]{1,0:T(8,128)(2,1)S(1)}, f32[256,512]{1,0:T(8,128)S(1)}, f32[256,512]{1,0:T(8,128)S(1)}, f32[512,512]{1,0:T(8,128)}) custom-call(s32[4]{0:T(128)S(1)} %broadcast_xor_fusion.order, bf16[512,2048]{1,0:T(8,128)(2,1)} %copy-done, bf16[512,2048]{1,0:T(8,128)(2,1)} %all-gather.2.cloned.1.call-done.refs_1_, ...), custom_call_target="tpu_custom_call" | custom-call | flops 2 | tf_op jit(solution)/shard_map/weight_blocks/pallas_call | solution.py:539
  92.0 1.5 collective-permute-start.4
  94.1 8.7 %core_grads.5 = (bf16[512,128]{1,0:T(8,128)(2,1)S(1)}, bf16[512,128]{1,0:T(8,128)(2,1)S(1)}, bf16[512,256]{1,0:T(8,128)(2,1)S(1)}, f32[4,128]{1,0:T(4,128)S(1)},...) custom-call(s32[8]{0:T(128)S(1)} %copy-done.59, ...), custom_call_target="tpu_custom_call", output_to_operand_aliasing={{8}: (16, {})} | custom-call | flops 10 | tf_op jit(solution)/shard_map/core_grads/pallas_call | solution.py:310
  102.9 5.9 %head_terms.3 = bf16[8,512,256]{2,1,0:T(8,128)(2,1)} custom-call(bf16[512,128]{1,0:T(8,128)(2,1)S(1)} %get-tuple-element.103.refs_5_.refs_0_, bf16[512,128]{1,0:T(8,128)(2,1)S(1)} %get-tuple-element.104.refs_6_.refs_1_, bf16[512,256]{1,0:T(8,128)(2,1)S(1)} %get-tuple-element.105.refs_7_.refs_2_, bf16[512,128]{1,0:T(8,128)(2,1)S(1)} %get-tuple-element.141.refs_3_.refs_5_, ...), custom_call_target="tpu_custom_call" | custom-call | flops 2 | tf_op jit(solution)/shard_map/head_terms/pallas_call | solution.py:407
  110.0 2.1 %collective-permute-done.4.refs_0_.refs_11_.refs_15_.refs_18_ = bf16[784,512]{1,0:T(8,128)(2,1)S(1)} collective-permute-done((bf16[784,512]{1,0:T(8,128)(2,1)}, bf16[784,512]{1,0:T(8,128)(2,1)S(1)}, u32[]{:S(2)}, u32[]{:S(2)}) %collective-permute-start.4) | collective-permute-done | bytes 802848 | tf_op jit(solution)/shard_map/ppermute | solution.py:746
  114.1 7.1 %weight_blocks.3 = (bf16[784,512]{1,0:T(8,128)(2,1)}, bf16[640,512]{1,0:T(8,128)(2,1)S(1)}, f32[256,512]{1,0:T(8,128)S(1)}, f32[256,512]{1,0:T(8,128)S(1)}, f32[512,512]{1,0:T(8,128)}) custom-call(s32[4]{0:T(128)S(1)} %copy-done.63, bf16[512,2048]{1,0:T(8,128)(2,1)} %copy-done, bf16[512,2048]{1,0:T(8,128)(2,1)} %all-gather.2.cloned.1.call-done.refs_1_, ...), custom_call_target="tpu_custom_call" | custom-call | flops 2 | tf_op jit(solution)/shard_map/weight_blocks/pallas_call | solution.py:539
  121.2 1.5 collective-permute-start.8
  123.2 1.5 collective-permute-start.6
  124.7 15.6 %collective-permute-done.9.refs_1_.refs_22_.refs_26_ = bf16[640,512]{1,0:T(8,128)(2,1)S(1)} collective-permute-done((bf16[640,512]{1,0:T(8,128)(2,1)S(1)}, bf16[640,512]{1,0:T(8,128)(2,1)S(1)}, u32[]{:S(2)}, u32[]{:S(2)}) %collective-permute-start.9) | collective-permute-done | bytes 655392 | tf_op jit(solution)/shard_map/ppermute | solution.py:746
  142.0 1.5 collective-permute-start.7
  151.5 2.8 %collective-permute-done.11.refs_24_ = bf16[256,512]{1,0:T(8,128)(2,1)} collective-permute-done((bf16[256,512]{1,0:T(8,128)(2,1)}, bf16[256,512]{1,0:T(8,128)(2,1)}, u32[]{:S(2)}, u32[]{:S(2)}) %collective-permute-start.11) | collective-permute-done | bytes 262176 | tf_op jit(solution)/shard_map/ppermute | solution.py:746
  154.3 1.7 collective-permute-done.10.refs_23_.refs_27_.refs_29_
  158.0 6.7 %finish.1 = (f32[512,256]{1,0:T(8,128)}, f32[512,256]{1,0:T(8,128)}, f32[512,512]{1,0:T(8,128)}, f32[8,4,128,128]{3,2,1,0:T(8,128)}, f32[4,256]{1,0:T(4,128)}, /...) custom-call(s32[8]{0:T(128)S(1)} %copy-done.65, s32[8]{0:T(128)S(1)} %copy-done.64, ...), custom_call_target="tpu_custom_call" | custom-call | flops 15000000512 | bytes 1 | tf_op jit(solution)/shard_map/finish/pallas_call | solution.py:702
  (186 shorter events, 25.6 us)
Async XLA Ops:
  7.2 63.3 %all-gather.2.cloned.1.call-start = ((), (), s32[]{:S(2)}) async-start(), calls=%async_computation.3 | async-start | bytes 2359296 | tf_op jit(solution)/shard_map/all_gather | solution.py:783
  9.0 19.5 %collective-permute-start = (bf16[512,256]{1,0:T(8,128)(2,1)S(1)}, bf16[512,256]{1,0:T(8,128)(2,1)S(1)}, u32[]{:S(2)}, u32[]{:S(2)}) collective-permute-start(bf16[512,256]{1,0:T(8,128)(2,1)S(1)} %get-tuple-element.91), channel_id=1, source_target_pairs={{0,2},{1,3},{2,4},{3,5},{4,6},{5,7},{6,0},{7,1},{8,10},{9,11},{10,... | collective-permute-start | bytes 786440 | tf_op jit(solution)/shard_map/ppermute | solution.py:752
  10.6 22.4 %collective-permute-start.1 = (bf16[512,256]{1,0:T(8,128)(2,1)S(1)}, bf16[512,256]{1,0:T(8,128)(2,1)S(1)}, u32[]{:S(2)}, u32[]{:S(2)}) collective-permute-start(bf16[512,256]{1,0:T(8,128)(2,1)S(1)} %get-tuple-element.91), channel_id=1, source_target_pairs={{0,4},{1,5},{2,6},{3,7},{4,0},{5,1},{6,2},{7,3},{8,12},{9,13},{10,... | collective-permute-start | bytes 786440 | tf_op jit(solution)/shard_map/ppermute | solution.py:752
  11.8 23.0 %collective-permute-start.2 = (bf16[512,256]{1,0:T(8,128)(2,1)S(1)}, bf16[512,256]{1,0:T(8,128)(2,1)S(1)}, u32[]{:S(2)}, u32[]{:S(2)}) collective-permute-start(bf16[512,256]{1,0:T(8,128)(2,1)S(1)} %get-tuple-element.91), channel_id=1, source_target_pairs={{0,6},{1,7},{2,0},{3,1},{4,2},{5,3},{6,4},{7,5},{8,14},{9,15},{10,... | collective-permute-start | bytes 786440 | tf_op jit(solution)/shard_map/ppermute | solution.py:752
  23.0 52.8 %copy-start.60 = (s32[8]{0:T(128)}, s32[8]{0:T(128)S(1)}, u32[]{:S(2)}) copy-start(s32[8]{0:T(128)S(1)} %dynamic_slice.3.refs_1_) | copy-start | bytes 100
  34.8 116.7 %reduce-scatter.3.cloned.1.call-start = ((), (), s32[]{:S(2)}) async-start(), calls=%async_computation.2 | async-start | bytes 2359296 | tf_op jit(solution)/shard_map/reduce_scatter | solution.py:845
  35.0 2.7 %collective-permute-start.3 = (bf16[4,512,256]{2,1,0:T(8,128)(2,1)S(1)}, bf16[4,512,256]{2,1,0:T(8,128)(2,1)S(1)}, u32[]{:S(2)}, u32[]{:S(2)}) collective-permute-start(bf16[4,512,256]{2,1,0:T(8,128)(2,1)S(1)} %pad_maximum_fusion.own), channel_id=1, source_target_pairs={{0,1},{1,0},{2,3},{3,2},{4,5},{5,4},{6,7},{7,6},{8,9},{9,8},{10,11... | collective-permute-start | bytes 3145736 | tf_op jit(solution)/shard_map/ppermute | solution.py:746
  63.9 11.9 %copy-start.40 = (f32[4,512]{1,0:T(4,128)}, f32[4,512]{1,0:T(4,128)S(1)}, u32[]{:S(2)}) copy-start(f32[4,512]{1,0:T(4,128)S(1)} %get-tuple-element.101.refs_15_) | copy-start | bytes 24580
  63.9 11.9 %copy-start.46 = (f32[4,256]{1,0:T(4,128)}, f32[4,256]{1,0:T(4,128)S(1)}, u32[]{:S(2)}) copy-start(f32[4,256]{1,0:T(4,128)S(1)} %get-tuple-element.99.refs_13_) | copy-start | bytes 12292
  63.9 11.9 %copy-start.48 = (f32[4,256]{1,0:T(4,128)}, f32[4,256]{1,0:T(4,128)S(1)}, u32[]{:S(2)}) copy-start(f32[4,256]{1,0:T(4,128)S(1)} %get-tuple-element.100.refs_14_) | copy-start | bytes 12292
  69.9 86.1 %reduce-scatter.5.cloned.1.call-start = ((), (), s32[]{:S(2)}) async-start(), calls=%async_computation.4 | async-start | bytes 2359296 | tf_op jit(solution)/shard_map/reduce_scatter | solution.py:845
  70.5 14.2 %copy-start.62 = (s32[4]{0:T(128)}, s32[4]{0:T(128)S(1)}, u32[]{:S(2)}) copy-start(s32[4]{0:T(128)S(1)} %broadcast_xor_fusion.order) | copy-start | bytes 52
  84.6 27.5 %copy-start.42 = (f32[4,256]{1,0:T(4,128)}, f32[4,256]{1,0:T(4,128)S(1)}, u32[]{:S(2)}) copy-start(f32[4,256]{1,0:T(4,128)S(1)} %get-tuple-element.108.refs_10_.refs_6_.refs_4_) | copy-start | bytes 12292
  84.7 27.5 %copy-start.50 = (f32[4,128]{1,0:T(4,128)}, f32[4,128]{1,0:T(4,128)S(1)}, u32[]{:S(2)}) copy-start(f32[4,128]{1,0:T(4,128)S(1)} %get-tuple-element.106.refs_8_.refs_4_.refs_2_) | copy-start | bytes 6148
  84.7 27.5 %copy-start.52 = (f32[4,128]{1,0:T(4,128)}, f32[4,128]{1,0:T(4,128)S(1)}, u32[]{:S(2)}) copy-start(f32[4,128]{1,0:T(4,128)S(1)} %get-tuple-element.107.refs_9_.refs_5_.refs_3_) | copy-start | bytes 6148
  92.0 20.2 %collective-permute-start.4 = (bf16[784,512]{1,0:T(8,128)(2,1)}, bf16[784,512]{1,0:T(8,128)(2,1)S(1)}, u32[]{:S(2)}, u32[]{:S(2)}) collective-permute-start(bf16[784,512]{1,0:T(8,128)(2,1)} %get-tuple-element.128), channel_id=1, source_target_pairs={{0,8},{8,0},{16,24},{24,16},{1,9},{9,1},{17,25},{25,17},{2,10},{10... | collective-permute-start | bytes 2408456 | tf_op jit(solution)/shard_map/ppermute | solution.py:746
  93.5 16.5 %collective-permute-start.5 = (bf16[640,512]{1,0:T(8,128)(2,1)S(1)}, bf16[640,512]{1,0:T(8,128)(2,1)S(1)}, u32[]{:S(2)}, u32[]{:S(2)}) collective-permute-start(bf16[640,512]{1,0:T(8,128)(2,1)S(1)} %get-tuple-element.129), channel_id=1, source_target_pairs={{0,16},{8,24},{16,0},{24,8},{1,17},{9,25},{17,1},{25,9},{2,18},{10... | collective-permute-start | bytes 1966088 | tf_op jit(solution)/shard_map/ppermute | solution.py:746
  102.9 11.1 %copy-start.29 = (f32[512,2]{1,0:T(8,128)}, f32[512,2]{1,0:T(8,128)S(1)}, u32[]{:S(2)}) copy-start(f32[512,2]{1,0:T(8,128)S(1)} %get-tuple-element.126) | copy-start | bytes 12292
  121.2 23.9 %copy-start.25 = (f32[512,4]{1,0:T(8,128)S(1)}, f32[512,4]{1,0:T(8,128)}, u32[]{:S(2)}) copy-start(f32[512,4]{1,0:T(8,128)} %copy-done.24) | copy-start | bytes 24580
  121.2 19.3 %collective-permute-start.8 = (bf16[784,512]{1,0:T(8,128)(2,1)}, bf16[784,512]{1,0:T(8,128)(2,1)S(1)}, u32[]{:S(2)}, u32[]{:S(2)}) collective-permute-start(bf16[784,512]{1,0:T(8,128)(2,1)} %get-tuple-element.148), channel_id=1, source_target_pairs={{0,8},{8,0},{16,24},{24,16},{1,9},{9,1},{17,25},{25,17},{2,10},{10... | collective-permute-start | bytes 2408456 | tf_op jit(solution)/shard_map/ppermute | solution.py:746
  122.7 17.7 %collective-permute-start.9 = (bf16[640,512]{1,0:T(8,128)(2,1)S(1)}, bf16[640,512]{1,0:T(8,128)(2,1)S(1)}, u32[]{:S(2)}, u32[]{:S(2)}) collective-permute-start(bf16[640,512]{1,0:T(8,128)(2,1)S(1)} %get-tuple-element.149), channel_id=1, source_target_pairs={{0,16},{8,24},{16,0},{24,8},{1,17},{9,25},{17,1},{25,9},{2,18},{10... | collective-permute-start | bytes 1966088 | tf_op jit(solution)/shard_map/ppermute | solution.py:746
  123.2 28.4 %collective-permute-start.6 = (bf16[400,512]{1,0:T(8,128)(2,1)}, bf16[400,512]{1,0:T(8,128)(2,1)}, u32[]{:S(2)}, u32[]{:S(2)}) collective-permute-start(bf16[400,512]{1,0:T(8,128)(2,1)} %get-tuple-element.139), channel_id=1, source_target_pairs={{0,16},{8,24},{16,0},{24,8},{1,17},{9,25},{17,1},{25,9},{2,18},{10... | collective-permute-start | bytes 1228808 | tf_op jit(solution)/shard_map/ppermute | solution.py:746
  140.5 15.5 %copy-start.14 = (bf16[8,2,128,128]{3,2,1,0:T(8,128)(2,1)S(1)}, bf16[8,2,128,128]{3,2,1,0:T(8,128)(2,1)}, u32[]{:S(2)}) copy-start(bf16[8,2,128,128]{3,2,1,0:T(8,128)(2,1)} %copy-done.13) | copy-start | bytes 1572868
  140.5 15.5 %copy-start.20 = (bf16[640,512]{1,0:T(8,128)(2,1)S(1)}, bf16[640,512]{1,0:T(8,128)(2,1)}, u32[]{:S(2)}) copy-start(bf16[640,512]{1,0:T(8,128)(2,1)} %copy-done.19) | copy-start | bytes 1966084
  140.5 15.5 %copy-start.43 = (f32[4,256]{1,0:T(4,128)S(1)}, f32[4,256]{1,0:T(4,128)}, u32[]{:S(2)}) copy-start(f32[4,256]{1,0:T(4,128)} %copy-done.42) | copy-start | bytes 12292
  140.5 15.5 %copy-start.51 = (f32[4,128]{1,0:T(4,128)S(1)}, f32[4,128]{1,0:T(4,128)}, u32[]{:S(2)}) copy-start(f32[4,128]{1,0:T(4,128)} %copy-done.50) | copy-start | bytes 6148
  140.5 15.5 %copy-start.53 = (f32[4,128]{1,0:T(4,128)S(1)}, f32[4,128]{1,0:T(4,128)}, u32[]{:S(2)}) copy-start(f32[4,128]{1,0:T(4,128)} %copy-done.52) | copy-start | bytes 6148
  140.5 15.5 %copy-start.64 = (s32[8]{0:T(128)S(1)}, s32[8]{0:T(128)}, u32[]{:S(2)}) copy-start(s32[8]{0:T(128)} %get-tuple-element.89.ranks) | copy-start | bytes 100
  140.6 15.5 %copy-start.65 = (s32[8]{0:T(128)S(1)}, s32[8]{0:T(128)}, u32[]{:S(2)}) copy-start(s32[8]{0:T(128)} %get-tuple-element.88.sources) | copy-start | bytes 100
  141.5 14.5 %collective-permute-start.10 = (bf16[400,512]{1,0:T(8,128)(2,1)}, bf16[400,512]{1,0:T(8,128)(2,1)}, u32[]{:S(2)}, u32[]{:S(2)}) collective-permute-start(bf16[400,512]{1,0:T(8,128)(2,1)} %get-tuple-element.152), channel_id=1, source_target_pairs={{0,16},{8,24},{16,0},{24,8},{1,17},{9,25},{17,1},{25,9},{2,18},{10... | collective-permute-start | bytes 1228808 | tf_op jit(solution)/shard_map/ppermute | solution.py:746
  142.0 9.5 %collective-permute-start.7 = (bf16[256,512]{1,0:T(8,128)(2,1)}, bf16[256,512]{1,0:T(8,128)(2,1)}, u32[]{:S(2)}, u32[]{:S(2)}) collective-permute-start(bf16[256,512]{1,0:T(8,128)(2,1)} %get-tuple-element.140), channel_id=1, source_target_pairs={{0,8},{8,0},{16,24},{24,16},{1,9},{9,1},{17,25},{25,17},{2,10},{10... | collective-permute-start | bytes 786440 | tf_op jit(solution)/shard_map/ppermute | solution.py:746
  143.5 10.9 %collective-permute-start.11 = (bf16[256,512]{1,0:T(8,128)(2,1)}, bf16[256,512]{1,0:T(8,128)(2,1)}, u32[]{:S(2)}, u32[]{:S(2)}) collective-permute-start(bf16[256,512]{1,0:T(8,128)(2,1)} %get-tuple-element.153), channel_id=1, source_target_pairs={{0,8},{8,0},{16,24},{24,16},{1,9},{9,1},{17,25},{25,17},{2,10},{10... | collective-permute-start | bytes 786440 | tf_op jit(solution)/shard_map/ppermute | solution.py:746
  (55 other events, 265.6 us)
Sparse Core Ops, SparseCore 0:
  34.9 29.9 all-gather.1
  70.0 32.2 reduce-scatter.2
  114.1 32.3 reduce-scatter.4
